TPU v7x, 32 devices: a whole 2x2x4 slice. The times are simulated.
32 devices in a mesh: rep: 16 (over z, y, x), shard: 2 (over core).
Axes of the slice: x: 2, y: 2, z: 4, core: 2. Of those that a mesh axis runs over, the one named last changes fastest.
Arguments:
- tokens: bfloat16 [32768, 768], P(('rep', 'shard')), may hold values from -6 to 6
- encoder_states: bfloat16 [65536, 768], P(('rep', 'shard')), may hold values from -6 to 6
- cotangent: bfloat16 [32768, 768], P(('rep', 'shard')), may hold values from -6 to 6
- block_mask: int32 [32, 4, 4], P(('rep', 'shard')), may hold values from 0 to 1, as said below
- wide_master: float32 [768, 9216], P('shard')
- narrow_master: float32 [3072, 768], P('shard'), may hold values from -0.15625 to 0.15625
- vec_master: float32 [768, 17], P('shard')
- wide_first: float32 [768, 9216], P('shard'), may hold values from -1.75 to 1.75
- narrow_first: float32 [3072, 768], P('shard'), may hold values from -1.75 to 1.75
- vec_first: float32 [768, 17], P('shard'), may hold values from -1.75 to 1.75
- wide_second: float32 [768, 9216], P('shard'), may hold values from 0.01 to 1
- narrow_second: float32 [3072, 768], P('shard'), may hold values from 0.01 to 1
- vec_second: float32 [768, 17], P('shard'), may hold values from 0.01 to 1
Outputs:
- out: bfloat16 [32768, 768], P(('rep', 'shard'))
- in_grad: bfloat16 [32768, 768], P(('rep', 'shard'))
- enc_grad: bfloat16 [65536, 768], P(('rep', 'shard'))
- wide_grad: float32 [768, 9216], P('shard')
- narrow_grad: float32 [3072, 768], P('shard')
- vec_grad: float32 [768, 17], P('shard')
- wide_new: float32 [768, 9216], P('shard')
- narrow_new: float32 [3072, 768], P('shard')
- vec_new: float32 [768, 17], P('shard')
- wide_first_new: float32 [768, 9216], P('shard')
- narrow_first_new: float32 [3072, 768], P('shard')
- vec_first_new: float32 [768, 17], P('shard')
- wide_second_new: float32 [768, 9216], P('shard')
- narrow_second_new: float32 [3072, 768], P('shard')
- vec_second_new: float32 [768, 17], P('shard')
- wide_copy: bfloat16 [768, 9216], P('shard')
- narrow_copy: bfloat16 [3072, 768], P('shard')
- vec_copy: bfloat16 [768, 17], P('shard')
Inputs may be any that keep to these rules, and one draw needn't show every extreme that they name: block_mask[s, a, b] is 1 where a == b and 0 where b > a; below the diagonal each entry is 0 or 1.
All inputs are finite; a program needn't handle non-finite values.
Results may differ from a plain program's by a relative error of at most 0.03.
The roundings to bfloat16 on the way count: a program that leaves them out, or rounds other values in their place, can miss the bound.
Values may be sent and summed in bfloat16 or wider, within the bound.
A program may use at most 512 MiB of HBM per device.

v0:
```python
from functools import partial

import jax
import jax.numpy as jnp
from jax import lax
from jax.sharding import PartitionSpec as P

D = 768
H = 12
HD = 64
FF = 3072
LEN = 1024
BLK = 256
STEP = 4


eps_norm = 1e-05
eps_adam = 1e-08
beta_one = 0.5
beta_two = 0.5
learn_rate = 0.03
vec_rate = 0.25
weight_decay = 0.1
masked_score = -1e30


def matmul(left, right):
    return jnp.dot(left, right, preferred_element_type=jnp.float32)


def matmul_left(left, right):
    return lax.dot_general(
        left, right, (((0,), (0,)), ((), ())), preferred_element_type=jnp.float32
    )


def matmul_right(left, right):
    return lax.dot_general(
        left, right, (((1,), (1,)), ((), ())), preferred_element_type=jnp.float32
    )


def norm_forward(resid, gain, shift):
    average = jnp.mean(resid, axis=-1, keepdims=True)
    centred = resid - average
    inverse = lax.rsqrt(jnp.mean(centred * centred, axis=-1, keepdims=True) + eps_norm)
    normed = centred * inverse
    return (normed * gain + shift, normed, inverse)


def norm_backward(upstream, normed, inverse, gain):
    scaled = upstream * gain
    centred = scaled - jnp.mean(scaled, axis=-1, keepdims=True)
    resid_grad = inverse * (centred - normed * jnp.mean(scaled * normed, axis=-1, keepdims=True))
    return (resid_grad, jnp.sum(upstream * normed, axis=0), jnp.sum(upstream, axis=0))


def allowed_pairs(block_table):
    expanded = jnp.repeat(jnp.repeat(block_table, BLK, axis=0), BLK, axis=1) > 0
    places = jnp.arange(LEN, dtype=jnp.int32)
    blocks = places // BLK
    causal = (blocks[:, None] > blocks[None, :]) | (places[:, None] >= places[None, :])
    return expanded & causal


def attend_forward(queries, keys_in, values_in, allowed):
    length = queries.shape[0]
    width_rows = min(512, length)
    blocks_count = length // width_rows
    head_k = keys_in.reshape(-1, H, HD)
    head_v = values_in.reshape(-1, H, HD)
    factor = HD ** (-0.5)

    def one_block(block_index):
        offset = block_index * width_rows
        head_q = lax.dynamic_slice_in_dim(queries, offset, width_rows, 0).reshape(width_rows, H, HD)
        scores = (
            jnp.einsum("qhd,khd->hqk", head_q, head_k, preferred_element_type=jnp.float32) * factor
        )
        if allowed is not None:
            permitted = lax.dynamic_slice_in_dim(allowed, offset, width_rows, 0)
            scores = jnp.where(permitted[None], scores, masked_score)
        row_max = jnp.max(scores, axis=-1, keepdims=True)
        weights = jnp.exp(scores - row_max)
        row_total = jnp.sum(weights, axis=-1, keepdims=True)
        probs_low = (weights / row_total).astype(jnp.bfloat16)
        mixed = jnp.einsum("hqk,khd->qhd", probs_low, head_v, preferred_element_type=jnp.float32)
        return (
            mixed.reshape(width_rows, H * HD).astype(jnp.bfloat16),
            (row_max + jnp.log(row_total))[:, :, 0],
        )

    mixed_blocks, log_totals = lax.map(one_block, jnp.arange(blocks_count, dtype=jnp.int32))
    return (mixed_blocks.reshape(length, H * HD), log_totals)


def attend_backward(queries, keys_in, values_in, allowed, log_totals, mixed_grad):
    length = queries.shape[0]
    width_rows = min(512, length)
    blocks_count = length // width_rows
    head_k = keys_in.reshape(-1, H, HD)
    head_v = values_in.reshape(-1, H, HD)
    factor = HD ** (-0.5)

    def one_block(running, block_index):
        keys_grad, values_grad = running
        offset = block_index * width_rows
        head_q = lax.dynamic_slice_in_dim(queries, offset, width_rows, 0).reshape(width_rows, H, HD)
        head_g = lax.dynamic_slice_in_dim(mixed_grad, offset, width_rows, 0).reshape(
            width_rows, H, HD
        )
        scores = (
            jnp.einsum("qhd,khd->hqk", head_q, head_k, preferred_element_type=jnp.float32) * factor
        )
        if allowed is not None:
            permitted = lax.dynamic_slice_in_dim(allowed, offset, width_rows, 0)
            scores = jnp.where(permitted[None], scores, masked_score)
        probs = jnp.exp(scores - log_totals[block_index][:, :, None])
        prob_grad = jnp.einsum("qhd,khd->hqk", head_g, head_v, preferred_element_type=jnp.float32)
        centre = jnp.sum(probs * prob_grad, axis=-1, keepdims=True)
        scores_grad = (probs * (prob_grad - centre)).astype(jnp.bfloat16)
        query_grad = (
            jnp.einsum("hqk,khd->qhd", scores_grad, head_k, preferred_element_type=jnp.float32)
            * factor
        )
        keys_grad = (
            keys_grad
            + jnp.einsum("hqk,qhd->khd", scores_grad, head_q, preferred_element_type=jnp.float32)
            * factor
        )
        values_grad = values_grad + jnp.einsum(
            "hqk,qhd->khd", probs.astype(jnp.bfloat16), head_g, preferred_element_type=jnp.float32
        )
        return (
            (keys_grad, values_grad),
            query_grad.reshape(width_rows, H * HD).astype(jnp.bfloat16),
        )

    initial = (jnp.zeros(head_k.shape, jnp.float32), jnp.zeros(head_v.shape, jnp.float32))
    (keys_grad, values_grad), query_blocks = lax.scan(
        one_block, initial, jnp.arange(blocks_count, dtype=jnp.int32)
    )
    return (
        query_blocks.reshape(length, H * HD),
        keys_grad.reshape(-1, H * HD).astype(jnp.bfloat16),
        values_grad.reshape(-1, H * HD).astype(jnp.bfloat16),
    )


def adam_update(master, first, second, gradient, decay_on, rate):
    first_new = beta_one * first + (1.0 - beta_one) * gradient
    second_new = beta_two * second + (1.0 - beta_two) * gradient * gradient
    first_hat = first_new / (1.0 - beta_one**STEP)
    second_hat = second_new / (1.0 - beta_two**STEP)
    master_new = master - rate * (first_hat / (jnp.sqrt(second_hat) + eps_adam) + decay_on * master)
    return (master_new, first_new, second_new)


def column_sum(matrix):
    return jnp.sum(matrix.astype(jnp.float32), axis=0)


def on_device(
    tokens,
    encoder_states,
    cotangent,
    block_mask,
    wide_master,
    narrow_master,
    vec_master,
    wide_first,
    narrow_first,
    vec_first,
    wide_second,
    narrow_second,
    vec_second,
):
    replicas = lax.axis_size("rep")
    shards = lax.axis_size("shard")
    seqs_dev = tokens.shape[0] // LEN
    tokens_all = tokens.shape[0] * replicas * shards

    def per_sequence(matrix):
        return matrix.reshape(seqs_dev, -1, D)

    copies = (
        wide_master.astype(jnp.bfloat16),
        narrow_master.astype(jnp.bfloat16),
        vec_master.astype(jnp.bfloat16),
    )
    wide_full, narrow_full, vec_full = (
        lax.all_gather(copies[0], "shard", axis=0, tiled=True),
        lax.all_gather(copies[1], "shard", axis=0, tiled=True),
        lax.all_gather(copies[2], "shard", axis=0, tiled=True),
    )
    vector = vec_full.astype(jnp.float32)
    ffn_bias = vector[:, 6:10].T.reshape(FF)
    joint_proj = matmul(tokens, wide_full[:, : 3 * D])
    queries = (joint_proj[:, :D] + vector[:, 0]).astype(jnp.bfloat16)
    keys_self = joint_proj[:, D : 2 * D].astype(jnp.bfloat16)
    values_self = (joint_proj[:, 2 * D :] + vector[:, 1]).astype(jnp.bfloat16)
    permitted_all = jax.vmap(allowed_pairs)(block_mask)

    def self_forward(pieces):
        return attend_forward(pieces[0], pieces[1], pieces[2], pieces[3])

    mixed_self, totals_self = lax.map(
        self_forward,
        (per_sequence(queries), per_sequence(keys_self), per_sequence(values_self), permitted_all),
    )
    mixed_self = mixed_self.reshape(-1, D)
    branch_one = matmul(mixed_self, wide_full[:, 3 * D : 4 * D]) + vector[:, 2]
    normed_one, unit_one, scale_one = norm_forward(
        tokens.astype(jnp.float32) + branch_one, vector[:, 11], vector[:, 14]
    )
    normed_low = normed_one.astype(jnp.bfloat16)
    cross_queries = (matmul(normed_low, wide_full[:, 4 * D : 5 * D]) + vector[:, 3]).astype(
        jnp.bfloat16
    )
    enc_proj = matmul(encoder_states, wide_full[:, 5 * D : 7 * D])
    cross_keys = enc_proj[:, :D].astype(jnp.bfloat16)
    cross_values = (enc_proj[:, D:] + vector[:, 4]).astype(jnp.bfloat16)

    def cross_forward(pieces):
        return attend_forward(pieces[0], pieces[1], pieces[2], None)

    mixed_cross, totals_cross = lax.map(
        cross_forward,
        (per_sequence(cross_queries), per_sequence(cross_keys), per_sequence(cross_values)),
    )
    mixed_cross = mixed_cross.reshape(-1, D)
    branch_two = matmul(mixed_cross, wide_full[:, 7 * D : 8 * D]) + vector[:, 5]
    normed_two, unit_two, scale_two = norm_forward(
        normed_one + branch_two, vector[:, 12], vector[:, 15]
    )
    second_low = normed_two.astype(jnp.bfloat16)
    hidden = matmul(second_low, wide_full[:, 8 * D :]) + ffn_bias
    active_full, gelu_pull = jax.vjp(partial(jax.nn.gelu, approximate=False), hidden)
    active = active_full.astype(jnp.bfloat16)
    branch_three = matmul(active, narrow_full) + vector[:, 10]
    final_out, unit_three, scale_three = norm_forward(
        normed_two + branch_three, vector[:, 13], vector[:, 16]
    )
    output = final_out.astype(jnp.bfloat16)
    wide_full, narrow_full, vec_full = (
        lax.all_gather(copies[0], "shard", axis=0, tiled=True),
        lax.all_gather(copies[1], "shard", axis=0, tiled=True),
        lax.all_gather(copies[2], "shard", axis=0, tiled=True),
    )
    vector = vec_full.astype(jnp.float32)
    grad_three, gain_three, shift_three = norm_backward(
        cotangent.astype(jnp.float32), unit_three, scale_three, vector[:, 13]
    )
    grad_ffn = grad_three.astype(jnp.bfloat16)
    grad_narrow = matmul_left(active, grad_ffn)
    grad_hidden = gelu_pull(matmul_right(grad_ffn, narrow_full))[0].astype(jnp.bfloat16)
    grad_ffn_in = matmul_left(second_low, grad_hidden)
    grad_two, gain_two, shift_two = norm_backward(
        grad_three + matmul_right(grad_hidden, wide_full[:, 8 * D :]),
        unit_two,
        scale_two,
        vector[:, 12],
    )
    grad_cross = grad_two.astype(jnp.bfloat16)
    grad_cross_out = matmul_left(mixed_cross, grad_cross)
    grad_cross_mix = matmul_right(grad_cross, wide_full[:, 7 * D : 8 * D]).astype(jnp.bfloat16)

    def cross_backward(pieces):
        return attend_backward(pieces[0], pieces[1], pieces[2], None, pieces[3], pieces[4])

    grad_cross_queries, grad_cross_keys, grad_cross_values = lax.map(
        cross_backward,
        (
            per_sequence(cross_queries),
            per_sequence(cross_keys),
            per_sequence(cross_values),
            totals_cross,
            per_sequence(grad_cross_mix),
        ),
    )
    grad_cross_queries = grad_cross_queries.reshape(-1, D)
    grad_enc_proj = jnp.concatenate(
        [grad_cross_keys.reshape(-1, D), grad_cross_values.reshape(-1, D)], 1
    )
    grad_cross_query = matmul_left(normed_low, grad_cross_queries)
    grad_cross_pair = matmul_left(encoder_states, grad_enc_proj)
    enc_grad = matmul_right(grad_enc_proj, wide_full[:, 5 * D : 7 * D]).astype(jnp.bfloat16)
    grad_one, gain_one, shift_one = norm_backward(
        grad_two + matmul_right(grad_cross_queries, wide_full[:, 4 * D : 5 * D]),
        unit_one,
        scale_one,
        vector[:, 11],
    )
    grad_self = grad_one.astype(jnp.bfloat16)
    grad_self_out = matmul_left(mixed_self, grad_self)
    grad_self_mix = matmul_right(grad_self, wide_full[:, 3 * D : 4 * D]).astype(jnp.bfloat16)

    def self_backward(pieces):
        return attend_backward(pieces[0], pieces[1], pieces[2], pieces[3], pieces[4], pieces[5])

    grad_queries, grad_keys, grad_values = lax.map(
        self_backward,
        (
            per_sequence(queries),
            per_sequence(keys_self),
            per_sequence(values_self),
            permitted_all,
            totals_self,
            per_sequence(grad_self_mix),
        ),
    )
    grad_joint_proj = jnp.concatenate(
        [grad_queries.reshape(-1, D), grad_keys.reshape(-1, D), grad_values.reshape(-1, D)], 1
    )
    grad_joint = matmul_left(tokens, grad_joint_proj)
    in_grad = (grad_one + matmul_right(grad_joint_proj, wide_full[:, : 3 * D])).astype(jnp.bfloat16)
    factor = float(tokens_all) ** (-0.5)
    term_wide = (
        jnp.concatenate(
            [
                grad_joint,
                grad_self_out,
                grad_cross_query,
                grad_cross_pair,
                grad_cross_out,
                grad_ffn_in,
            ],
            1,
        )
        * factor
    )
    term_narrow = grad_narrow * factor
    bias_front = jnp.stack(
        [
            column_sum(grad_joint_proj[:, :D]),
            column_sum(grad_joint_proj[:, 2 * D :]),
            column_sum(grad_self),
            column_sum(grad_cross_queries),
            column_sum(grad_enc_proj[:, D:]),
            column_sum(grad_cross),
        ],
        1,
    )
    bias_back = jnp.stack(
        [column_sum(grad_ffn), gain_one, gain_two, gain_three, shift_one, shift_two, shift_three], 1
    )
    term_vec = (
        jnp.concatenate([bias_front, column_sum(grad_hidden).reshape(4, D).T, bias_back], 1)
        * factor
    )
    wide_owned, narrow_owned, vec_owned = (
        lax.psum_scatter(
            term_wide.astype(jnp.bfloat16), "shard", scatter_dimension=0, tiled=True
        ).astype(jnp.float32),
        lax.psum_scatter(
            term_narrow.astype(jnp.bfloat16), "shard", scatter_dimension=0, tiled=True
        ).astype(jnp.float32),
        lax.psum_scatter(
            term_vec.astype(jnp.bfloat16), "shard", scatter_dimension=0, tiled=True
        ).astype(jnp.float32),
    )
    wide_grad, narrow_grad, vec_grad = (
        lax.psum(wide_owned.astype(jnp.bfloat16), "rep").astype(jnp.float32),
        lax.psum(narrow_owned.astype(jnp.bfloat16), "rep").astype(jnp.float32),
        lax.psum(vec_owned.astype(jnp.bfloat16), "rep").astype(jnp.float32),
    )
    wide_new, wide_first_new, wide_second_new = adam_update(
        wide_master, wide_first, wide_second, wide_grad, weight_decay, learn_rate
    )
    narrow_new, narrow_first_new, narrow_second_new = adam_update(
        narrow_master, narrow_first, narrow_second, narrow_grad, weight_decay, learn_rate
    )
    vec_new, vec_first_new, vec_second_new = adam_update(
        vec_master, vec_first, vec_second, vec_grad, 0.0, vec_rate
    )
    return (
        output,
        in_grad,
        enc_grad,
        wide_grad,
        narrow_grad,
        vec_grad,
        wide_new,
        narrow_new,
        vec_new,
        wide_first_new,
        narrow_first_new,
        vec_first_new,
        wide_second_new,
        narrow_second_new,
        vec_second_new,
        wide_new.astype(jnp.bfloat16),
        narrow_new.astype(jnp.bfloat16),
        vec_new.astype(jnp.bfloat16),
    )


def solution(mesh):
    in_specs = (
        P(("rep", "shard"), None),
        P(("rep", "shard"), None),
        P(("rep", "shard"), None),
        P(("rep", "shard"), None, None),
        P("shard", None),
        P("shard", None),
        P("shard", None),
        P("shard", None),
        P("shard", None),
        P("shard", None),
        P("shard", None),
        P("shard", None),
        P("shard", None),
    )
    out_specs = (
        P(("rep", "shard"), None),
        P(("rep", "shard"), None),
        P(("rep", "shard"), None),
        P("shard", None),
        P("shard", None),
        P("shard", None),
        P("shard", None),
        P("shard", None),
        P("shard", None),
        P("shard", None),
        P("shard", None),
        P("shard", None),
        P("shard", None),
        P("shard", None),
        P("shard", None),
        P("shard", None),
        P("shard", None),
        P("shard", None),
    )
    return jax.shard_map(
        on_device, mesh=mesh, in_specs=in_specs, out_specs=out_specs, check_vma=False
    )
```

profile of v0, /device:TPU:0, one launch (start us, length us, event | category | flops | bytes accessed | tf_op | source)
XLA Modules:
  0.0 1441.9 jit_solution(5287523161790611952)
XLA Ops:
  65.0 87.8 %while.94 = (s32[]{:T(128)}, bf16[2,512,768]{2,1,0:T(8,128)(2,1)}, f32[2,12,512]{2,1,0:T(8,128)S(1)}, s32[2]{0:T(128)S(1)}, pred[1024,1024]{1,0:T(8,128)(4,1)}, ...) while((s32[]{:T(128)}, bf16[2,512,768]{2,1,0:T(8,128)(2,1)}, ...), condition=%wide.region_3.4_spmd, body=%wide.region_0.3_spmd.sunk | while | flops 1686497280 | bytes 194732784 | solution.py:93
  68.8 12.0 fusion.182
  80.8 12.3 fusion.183
  112.6 12.0 fusion.182
  124.6 12.3 fusion.183
  178.2 140.2 %while.95 = (s32[]{:T(128)}, bf16[2,512,768]{2,1,0:T(8,128)(2,1)}, f32[2,12,512]{2,1,0:T(8,128)S(1)}, s32[2]{0:T(128)S(1)}, bf16[1024,768]{0,1:T(8,128)(2,1)}, /...) while((s32[]{:T(128)}, bf16[2,512,768]{2,1,0:T(8,128)(2,1)}, ...), condition=%wide.region_9.10_spmd, body=%wide.region_6.9_spmd.sunk | while | flops 3334858752 | bytes 176382672 | solution.py:93
  182.0 21.5 %multiply_reduce_fusion.15 = (f32[12,512]{1,0:T(8,128)S(1)}, f32[12,512,2048]{2,1,0:T(8,128)}) fusion(bf16[512,12,64]{0,2,1:T(8,128)(2,1)} %bitcast.210, bf16[2048,12,64]{0,2,1:T(8,128)(2,1)} %get-tuple-element.1052), kind=kOutput, calls=%fused_computation.15.clone.1 | convolution fusion | flops 1635772416 | bytes 54288384 | tf_op jit(solution)/shard_map/while/body/eval_jaxpr/while/body/eval_jaxpr/qhd,khd->hqk/dot_general | solution.py:78
  203.4 20.7 %fusion.188 = f32[12,512]{1,0:T(8,128)S(1)} fusion(f32[12,512,2048]{2,1,0:T(8,128)} %get-tuple-element.962, f32[12,512]{1,0:T(8,128)S(1)} %get-tuple-element.963), kind=kLoop, calls=%fused_computation.16.clone.1 | loop fusion | flops 37742592 | bytes 50380800 | tf_op jit(solution)/shard_map/while/body/eval_jaxpr/while/body/eval_jaxpr/reduce_sum | solution.py:85
  224.1 20.1 %fusion.189 = bf16[12,512,64]{1,2,0:T(8,128)(2,1)} fusion(bf16[2048,12,64]{0,2,1:T(8,128)(2,1)S(1)} %copy-done.4, f32[12,512,2048]{2,1,0:T(8,128)} %get-tuple-element.962, f32[12,512]{1,0:T(8,128)S(1)} %fusion.188, f32[12,512]{1,0:T(8,128)S(1)} %get-tuple-element.963), kind=kOutput, calls=%fused_computation.18.clone.1 | convolution fusion | flops 1661337600 | bytes 54312960 | tf_op jit(solution)/shard_map/while/body/eval_jaxpr/while/body/eval_jaxpr/hqk,khd->qhd/dot_general | solution.py:87
  251.9 21.5 %multiply_reduce_fusion.15 = (f32[12,512]{1,0:T(8,128)S(1)}, f32[12,512,2048]{2,1,0:T(8,128)}) fusion(bf16[512,12,64]{0,2,1:T(8,128)(2,1)} %bitcast.210, bf16[2048,12,64]{0,2,1:T(8,128)(2,1)} %get-tuple-element.1052), kind=kOutput, calls=%fused_computation.15.clone.1 | convolution fusion | flops 1635772416 | bytes 54288384 | tf_op jit(solution)/shard_map/while/body/eval_jaxpr/while/body/eval_jaxpr/qhd,khd->hqk/dot_general | solution.py:78
  273.3 20.7 %fusion.188 = f32[12,512]{1,0:T(8,128)S(1)} fusion(f32[12,512,2048]{2,1,0:T(8,128)} %get-tuple-element.962, f32[12,512]{1,0:T(8,128)S(1)} %get-tuple-element.963), kind=kLoop, calls=%fused_computation.16.clone.1 | loop fusion | flops 37742592 | bytes 50380800 | tf_op jit(solution)/shard_map/while/body/eval_jaxpr/while/body/eval_jaxpr/reduce_sum | solution.py:85
  294.1 20.1 %fusion.189 = bf16[12,512,64]{1,2,0:T(8,128)(2,1)} fusion(bf16[2048,12,64]{0,2,1:T(8,128)(2,1)S(1)} %copy-done.4, f32[12,512,2048]{2,1,0:T(8,128)} %get-tuple-element.962, f32[12,512]{1,0:T(8,128)S(1)} %fusion.188, f32[12,512]{1,0:T(8,128)S(1)} %get-tuple-element.963), kind=kOutput, calls=%fused_computation.18.clone.1 | convolution fusion | flops 1661337600 | bytes 54312960 | tf_op jit(solution)/shard_map/while/body/eval_jaxpr/while/body/eval_jaxpr/hqk,khd->qhd/dot_general | solution.py:87
  324.9 37.7 %multiply_convert_fusion.5 = (bf16[1024,3072]{1,0:T(8,128)(2,1)}, f32[1024,3072]{1,0:T(8,128)}, f32[1024,3072]{1,0:T(8,128)}) fusion(f32[3072]{0:T(1024)S(1)} %copy-done.62, bf16[768,9216]{1,0:T(8,128)(2,1)} %all-gather.3.cloned.1.call-done, f32[1024,768]{0,1:T(8,128)S(1)} %get-tuple-element.743, f32[768]{0:T(1024)S(1)} %copy-done.63, ...), kind=kOutput, calls=%fused_computation.63 | convolution fusion | flops 5043388416 | bytes 39348224 | tf_op jit(solution)/shard_map/dot_general | solution.py:28
  362.7 9.8 fusion.101
  386.1 19.5 %convert_reduce_fusion = (f32[3072]{0:T(1024)}, bf16[1024,3072]{1,0:T(8,128)(2,1)}) fusion(f32[1024,3072]{1,0:T(8,128)} %get-tuple-element.728, bf16[1024,768]{0,1:T(8,128)(2,1)} %copy-done.26, bf16[3072,768]{1,0:T(8,128)(2,1)} %all-gather.5.cloned.1.call-done, f32[1024,3072]{1,0:T(8,128)} %get-tuple-element.744, f32[3072]{0:T(1024)S(1)} %copy-done.62), kind=kOutput, calls=%fused_computation.61 | convolution fusion | flops 4885312512 | bytes 37773312 | tf_op jit(solution)/shard_map/dot_general | solution.py:38
  405.7 12.5 multiply_reduce_fusion.3
  426.7 321.9 %while.96 = (s32[]{:T(128)}, f32[2048,12,64]{0,2,1:T(8,128)}, f32[2048,12,64]{0,2,1:T(8,128)}, bf16[2,512,768]{1,2,0:T(8,128)(2,1)}, s32[2]{0:T(128)S(1)}, /*ind...) while((s32[]{:T(128)}, f32[2048,12,64]{0,2,1:T(8,128)}, ...), condition=%wide.region_20.21_spmd.clone, body=%wide.region_18.20_spmd.clone.sunk | while | flops 8212703232 | bytes 422486784 | solution.py:140
  430.2 21.3 %fusion.200 = f32[12,512,2048]{2,1,0:T(8,128)} fusion(bf16[512,12,64]{0,2,1:T(8,128)(2,1)} %bitcast.205, bf16[2048,12,64]{0,2,1:T(8,128)(2,1)} %get-tuple-element.1094), kind=kOutput, calls=%fused_computation.222.clone.1 | convolution fusion | flops 1610612736 | bytes 54263808 | tf_op jit(solution)/shard_map/while/body/eval_jaxpr/while/body/eval_jaxpr/qhd,khd->hqk/dot_general | solution.py:113
  457.7 34.1 %multiply_reduce_fusion.16 = (f32[12,512]{1,0:T(8,128)S(1)}, f32[12,512,2048]{2,1,0:T(8,128)}) fusion(f32[12,512,2048]{2,1,0:T(8,128)} %fusion.200, f32[12,512]{1,0:T(8,128)S(1)} %dynamic-slice_bitcast_fusion.4, bf16[512,12,64]{0,2,1:T(8,128)(2,1)} %bitcast.207, bf16[2048,12,64]{0,2,1:T(8,128)(2,1)} %get-tuple-element.1097), kind=kOutput, calls=%fused_computation.24.clone.1 | convolution fusion | flops 1660938240 | bytes 104644608 | tf_op jit(solution)/shard_map/while/body/eval_jaxpr/while/body/eval_jaxpr/qhd,khd->hqk/dot_general | solution.py:119
  491.8 40.4 %multiply_convert_fusion.12 = bf16[12,512,2048]{2,1,0:T(8,128)(2,1)} fusion(f32[12,512,2048]{2,1,0:T(8,128)} %get-tuple-element.974, f32[12,512,2048]{2,1,0:T(8,128)} %fusion.200, f32[12,512]{1,0:T(8,128)S(1)} %get-tuple-element.975, f32[12,512]{1,0:T(8,128)S(1)} %dynamic-slice_bitcast_fusion.4), kind=kLoop, calls=%fused_computation.23.clone.1 | loop fusion | flops 62914560 | bytes 125878272 | tf_op jit(solution)/shard_map/while/body/eval_jaxpr/while/body/eval_jaxpr/convert_element_type | solution.py:121
  532.2 15.6 %bitcast_add_fusion.8 = f32[2048,12,64]{0,2,1:T(8,128)} fusion(f32[2048,12,64]{0,2,1:T(8,128)} %get-tuple-element.1074, bf16[512,12,64]{0,2,1:T(8,128)(2,1)} %bitcast.206, bf16[12,512,2048]{2,1,0:T(8,128)(2,1)} %multiply_convert_fusion.12, pred[]{:T(512)S(6)} %compare.12), kind=kOutput, calls=%fused_computation.31.clone.1 | convolution fusion | flops 1615331328 | bytes 38535168 | tf_op jit(solution)/shard_map/while/body/eval_jaxpr/while/body/eval_jaxpr/hqk,qhd->khd/dot_general | solution.py:128
  547.9 14.1 multiply_convert_fusion.13
  564.0 21.8 %bitcast_add_fusion.9 = f32[2048,12,64]{0,2,1:T(8,128)} fusion(f32[2048,12,64]{0,2,1:T(8,128)} %get-tuple-element.1075, bf16[512,12,64]{0,2,1:T(8,128)(2,1)} %bitcast.208, f32[12,512,2048]{2,1,0:T(8,128)} %fusion.200, f32[12,512]{1,0:T(8,128)S(1)} %dynamic-slice_bitcast_fusion.4, pred[]{:T(512)S(6)} %compare.12), kind=kOutput, calls=%fused_computation.30.clone.1 | convolution fusion | flops 1651507200 | bytes 63725568 | tf_op jit(solution)/shard_map/while/body/eval_jaxpr/while/body/eval_jaxpr/hqk,qhd->khd/dot_general | solution.py:131
  589.1 21.3 %fusion.200 = f32[12,512,2048]{2,1,0:T(8,128)} fusion(bf16[512,12,64]{0,2,1:T(8,128)(2,1)} %bitcast.205, bf16[2048,12,64]{0,2,1:T(8,128)(2,1)} %get-tuple-element.1094), kind=kOutput, calls=%fused_computation.222.clone.1 | convolution fusion | flops 1610612736 | bytes 54263808 | tf_op jit(solution)/shard_map/while/body/eval_jaxpr/while/body/eval_jaxpr/qhd,khd->hqk/dot_general | solution.py:113
  616.6 34.1 %multiply_reduce_fusion.16 = (f32[12,512]{1,0:T(8,128)S(1)}, f32[12,512,2048]{2,1,0:T(8,128)}) fusion(f32[12,512,2048]{2,1,0:T(8,128)} %fusion.200, f32[12,512]{1,0:T(8,128)S(1)} %dynamic-slice_bitcast_fusion.4, bf16[512,12,64]{0,2,1:T(8,128)(2,1)} %bitcast.207, bf16[2048,12,64]{0,2,1:T(8,128)(2,1)} %get-tuple-element.1097), kind=kOutput, calls=%fused_computation.24.clone.1 | convolution fusion | flops 1660938240 | bytes 104644608 | tf_op jit(solution)/shard_map/while/body/eval_jaxpr/while/body/eval_jaxpr/qhd,khd->hqk/dot_general | solution.py:119
  650.7 40.4 %multiply_convert_fusion.12 = bf16[12,512,2048]{2,1,0:T(8,128)(2,1)} fusion(f32[12,512,2048]{2,1,0:T(8,128)} %get-tuple-element.974, f32[12,512,2048]{2,1,0:T(8,128)} %fusion.200, f32[12,512]{1,0:T(8,128)S(1)} %get-tuple-element.975, f32[12,512]{1,0:T(8,128)S(1)} %dynamic-slice_bitcast_fusion.4), kind=kLoop, calls=%fused_computation.23.clone.1 | loop fusion | flops 62914560 | bytes 125878272 | tf_op jit(solution)/shard_map/while/body/eval_jaxpr/while/body/eval_jaxpr/convert_element_type | solution.py:121
  691.1 17.4 %bitcast_add_fusion.8 = f32[2048,12,64]{0,2,1:T(8,128)} fusion(f32[2048,12,64]{0,2,1:T(8,128)} %get-tuple-element.1074, bf16[512,12,64]{0,2,1:T(8,128)(2,1)} %bitcast.206, bf16[12,512,2048]{2,1,0:T(8,128)(2,1)} %multiply_convert_fusion.12, pred[]{:T(512)S(6)} %compare.12), kind=kOutput, calls=%fused_computation.31.clone.1 | convolution fusion | flops 1615331328 | bytes 38535168 | tf_op jit(solution)/shard_map/while/body/eval_jaxpr/while/body/eval_jaxpr/hqk,qhd->khd/dot_general | solution.py:128
  708.5 14.1 multiply_convert_fusion.13
  724.7 23.5 %bitcast_add_fusion.9 = f32[2048,12,64]{0,2,1:T(8,128)} fusion(f32[2048,12,64]{0,2,1:T(8,128)} %get-tuple-element.1075, bf16[512,12,64]{0,2,1:T(8,128)(2,1)} %bitcast.208, f32[12,512,2048]{2,1,0:T(8,128)} %fusion.200, f32[12,512]{1,0:T(8,128)S(1)} %dynamic-slice_bitcast_fusion.4, pred[]{:T(512)S(6)} %compare.12), kind=kOutput, calls=%fused_computation.30.clone.1 | convolution fusion | flops 1651507200 | bytes 63725568 | tf_op jit(solution)/shard_map/while/body/eval_jaxpr/while/body/eval_jaxpr/hqk,qhd->khd/dot_general | solution.py:131
  766.3 192.1 %while.97 = (s32[]{:T(128)}, f32[1024,12,64]{0,2,1:T(8,128)}, f32[1024,12,64]{0,2,1:T(8,128)}, bf16[2,512,768]{1,2,0:T(8,128)(2,1)}, s32[2]{0:T(128)S(1)}, /*ind...) while((s32[]{:T(128)}, f32[1024,12,64]{0,2,1:T(8,128)}, ...), condition=%wide.region_25.26_spmd.clone, body=%wide.region_23.25_spmd.clone.sunk | while | flops 4125616128 | bytes 232694640 | solution.py:140
  768.9 11.8 fusion.211
  786.7 18.2 %multiply_reduce_fusion.17 = (f32[12,512]{1,0:T(8,128)S(1)}, f32[12,512,1024]{2,1,0:T(8,128)}) fusion(f32[12,512,1024]{2,1,0:T(8,128)} %fusion.211, f32[12,512]{1,0:T(8,128)S(1)} %dynamic-slice_bitcast_fusion.5, pred[512,1024]{1,0:T(8,128)(4,1)} %constant_dynamic-slice_fusion.22, bf16[512,12,64]{0,2,1:T(8,128)(2,1)} %bitcast.212, ...), kind=kOutput, calls=%fused_computation.39.clone.1 | convolution fusion | flops 836757504 | bytes 53264384 | tf_op jit(solution)/shard_map/while/body/eval_jaxpr/while/body/eval_jaxpr/qhd,khd->hqk/dot_general | solution.py:119
  804.9 22.1 %multiply_convert_fusion.14 = bf16[12,512,1024]{2,1,0:T(8,128)(2,1)} fusion(f32[12,512,1024]{2,1,0:T(8,128)} %get-tuple-element.987, f32[12,512,1024]{2,1,0:T(8,128)} %fusion.211, f32[12,512]{1,0:T(8,128)S(1)} %get-tuple-element.988, f32[12,512]{1,0:T(8,128)S(1)} %dynamic-slice_bitcast_fusion.5, pred[512,1024]{1,0:T(8,128)(4,1)} %constant_dynamic-slice_fusion.22), kind=kLoop, calls=%fused_computation.38.clone.1 | loop fusion | flops 37748736 | bytes 63488000 | tf_op jit(solution)/shard_map/while/body/eval_jaxpr/while/body/eval_jaxpr/convert_element_type | solution.py:121
  835.8 9.8 multiply_convert_fusion.15
  847.7 13.7 bitcast_add_fusion.11
  863.8 11.8 fusion.211
  881.6 18.2 %multiply_reduce_fusion.17 = (f32[12,512]{1,0:T(8,128)S(1)}, f32[12,512,1024]{2,1,0:T(8,128)}) fusion(f32[12,512,1024]{2,1,0:T(8,128)} %fusion.211, f32[12,512]{1,0:T(8,128)S(1)} %dynamic-slice_bitcast_fusion.5, pred[512,1024]{1,0:T(8,128)(4,1)} %constant_dynamic-slice_fusion.22, bf16[512,12,64]{0,2,1:T(8,128)(2,1)} %bitcast.212, ...), kind=kOutput, calls=%fused_computation.39.clone.1 | convolution fusion | flops 836757504 | bytes 53264384 | tf_op jit(solution)/shard_map/while/body/eval_jaxpr/while/body/eval_jaxpr/qhd,khd->hqk/dot_general | solution.py:119
  899.8 22.1 %multiply_convert_fusion.14 = bf16[12,512,1024]{2,1,0:T(8,128)(2,1)} fusion(f32[12,512,1024]{2,1,0:T(8,128)} %get-tuple-element.987, f32[12,512,1024]{2,1,0:T(8,128)} %fusion.211, f32[12,512]{1,0:T(8,128)S(1)} %get-tuple-element.988, f32[12,512]{1,0:T(8,128)S(1)} %dynamic-slice_bitcast_fusion.5, pred[512,1024]{1,0:T(8,128)(4,1)} %constant_dynamic-slice_fusion.22), kind=kLoop, calls=%fused_computation.38.clone.1 | loop fusion | flops 37748736 | bytes 63488000 | tf_op jit(solution)/shard_map/while/body/eval_jaxpr/while/body/eval_jaxpr/convert_element_type | solution.py:121
  921.9 9.7 bitcast_add_fusion.10
  931.6 9.8 multiply_convert_fusion.15
  943.5 14.5 %bitcast_add_fusion.11 = f32[1024,12,64]{0,2,1:T(8,128)} fusion(f32[1024,12,64]{0,2,1:T(8,128)} %get-tuple-element.1121, bf16[512,12,64]{0,2,1:T(8,128)(2,1)} %bitcast.213, f32[12,512,1024]{2,1,0:T(8,128)} %fusion.211, f32[12,512]{1,0:T(8,128)S(1)} %dynamic-slice_bitcast_fusion.5, pred[512,1024]{1,0:T(8,128)(4,1)} %constant_dynamic-slice_fusion.22, ...), kind=kOutput, calls=%fused_computation.44.clone.1 | convolution fusion | flops 832045056 | bytes 32792576 | tf_op jit(solution)/shard_map/while/body/eval_jaxpr/while/body/eval_jaxpr/hqk,qhd->khd/dot_general | solution.py:131
  995.2 9.7 convolution_bitcast_fusion
  1040.4 16.2 %multiply_convert_fusion.4 = bf16[768,9216]{1,0:T(8,128)(2,1)} fusion(f32[768,9216]{1,0:T(8,128)} %convolution_dynamic-update-slice_fusion), kind=kLoop, calls=%fused_computation.54 | loop fusion | flops 14155776 | bytes 42467328 | tf_op jit(solution)/shard_map/convert_element_type | solution.py:353
  1061.7 19.7 %reduce-scatter.6.cloned.1.call-done = bf16[384,9216]{1,0:T(8,128)(2,1)} async-done(((bf16[768,9216]{1,0:T(8,128)(2,1)}), bf16[384,9216]{1,0:T(8,128)(2,1)}) %reduce-scatter.6.cloned.1.call-update) | async-done | bytes 7077904 | tf_op jit(solution)/shard_map/reduce_scatter | solution.py:352
  1106.2 82.0 %psum.23 = bf16[384,17]{0,1:T(8,128)(2,1)S(1)} all-reduce(bf16[384,17]{0,1:T(8,128)(2,1)S(1)} %copy.143), channel_id=1, replica_groups=mesh['rep'=16,'shard'=2] {'rep'}, use_global_device_ids=true, to_apply=%region_45.46 | all-reduce | flops 6528 | bytes 26112 | tf_op jit(solution)/shard_map/psum | solution.py:365
  1188.8 195.2 %all-reduce.3.cloned.1.call-done = (bf16[384,9216]{1,0:T(8,128)(2,1)}, bf16[1536,768]{1,0:T(8,128)(2,1)}) async-done(((bf16[384,9216]{1,0:T(8,128)(2,1)}, bf16[1536,768]{1,0:T(8,128)(2,1)}), (bf16[384,9216]{1,0:T(8,128)(2,1)}, bf16[1536,768]{1,0:T(8,128)(2,1)})) %all-reduce.3.cloned.1.call-update) | async-done | bytes 9437200 | tf_op jit(solution)/shard_map/psum | solution.py:363
  1384.0 37.9 %fusion.95 = (bf16[384,9216]{1,0:T(8,128)(2,1)}, f32[384,9216]{1,0:T(8,128)}, f32[384,9216]{1,0:T(8,128)}, f32[384,9216]{1,0:T(8,128)}, f32[384,9216]{1,0:T(8,128)}) fusion(f32[384,9216]{1,0:T(8,128)} %param.25, f32[384,9216]{1,0:T(8,128)} %param.28, f32[384,9216]{1,0:T(8,128)} %param.31, bf16[384,9216]{1,0:T(8,128)(2,1)} %get-tuple-element.700), kind=kLoop, calls=%fused_computation.218 | loop fusion | flops 56623104 | bytes 113246208 | tf_op jit(solution)/shard_map/convert_element_type | solution.py:392
  1422.0 12.9 fusion.93
  (355 shorter events, 326.0 us)
Async XLA Ops:
  7.2 158.4 %copy-start = (bf16[2048,768]{1,0:T(8,128)(2,1)S(1)}, bf16[2048,768]{1,0:T(8,128)(2,1)}, u32[]{:S(2)}) copy-start(bf16[2048,768]{1,0:T(8,128)(2,1)} %param.22) | copy-start | bytes 9437188
  7.2 38.5 %all-gather.3.cloned.1.call-start = ((), (), s32[]{:S(2)}) async-start(), calls=%async_computation.3 | async-start | bytes 21233664 | tf_op jit(solution)/shard_map/all_gather | solution.py:192
  16.4 6.8 copy-start.76
  16.4 346.2 %all-gather.5.cloned.1.call-start = ((), (), s32[]{:S(2)}) async-start(), calls=%async_computation.4 | async-start | bytes 7077888 | tf_op jit(solution)/shard_map/all_gather | solution.py:193
  20.5 1041.2 %reduce-scatter.8.cloned.1.call-start = ((), (), s32[]{:S(2)}) async-start(), calls=%async_computation.6 | async-start | bytes 7077888 | tf_op jit(solution)/shard_map/reduce_scatter | solution.py:355
  65.0 87.8 %copy-start.71 = (f32[768]{0:T(1024)S(1)}, f32[768]{0:T(1024)}, u32[]{:S(2)}) copy-start(f32[768]{0:T(1024)} %get-tuple-element.625) | copy-start | bytes 9220
  68.8 24.4 %copy-start.5 = (bf16[1024,12,64]{0,2,1:T(8,128)(2,1)S(1)}, bf16[1024,12,64]{0,2,1:T(8,128)(2,1)}, u32[]{:S(2)}) copy-start(bf16[1024,12,64]{0,2,1:T(8,128)(2,1)} %get-tuple-element.1020) | copy-start | bytes 4718596 | tf_op jit(solution)/shard_map/while/body/eval_jaxpr/while
  80.8 15.4 %copy-start.1 = (f32[12,512,1024]{2,1,0:T(8,128)S(1)}, f32[12,512,1024]{2,1,0:T(8,128)}, u32[]{:S(2)}) copy-start(f32[12,512,1024]{2,1,0:T(8,128)} %get-tuple-element.953) | copy-start | bytes 75497472 | tf_op jit(solution)/shard_map/while/body/eval_jaxpr/while
  112.6 24.4 %copy-start.5 = (bf16[1024,12,64]{0,2,1:T(8,128)(2,1)S(1)}, bf16[1024,12,64]{0,2,1:T(8,128)(2,1)}, u32[]{:S(2)}) copy-start(bf16[1024,12,64]{0,2,1:T(8,128)(2,1)} %get-tuple-element.1020) | copy-start | bytes 4718596 | tf_op jit(solution)/shard_map/while/body/eval_jaxpr/while
  124.6 15.4 %copy-start.1 = (f32[12,512,1024]{2,1,0:T(8,128)S(1)}, f32[12,512,1024]{2,1,0:T(8,128)}, u32[]{:S(2)}) copy-start(f32[12,512,1024]{2,1,0:T(8,128)} %get-tuple-element.953) | copy-start | bytes 75497472 | tf_op jit(solution)/shard_map/while/body/eval_jaxpr/while
  178.2 140.3 %copy-start.34 = (f32[1024]{0:T(1024)S(1)}, f32[1024]{0:T(1024)}, u32[]{:S(2)}) copy-start(f32[1024]{0:T(1024)} %copy-done.33) | copy-start | bytes 12292
  178.2 140.3 %copy-start.45 = (f32[768]{0:T(1024)S(1)}, f32[768]{0:T(1024)}, u32[]{:S(2)}) copy-start(f32[768]{0:T(1024)} %get-tuple-element.624) | copy-start | bytes 9220
  178.2 140.3 %copy-start.54 = (f32[1024]{0:T(1024)S(1)}, f32[1024]{0:T(1024)}, u32[]{:S(2)}) copy-start(f32[1024]{0:T(1024)} %copy-done.53) | copy-start | bytes 12292
  178.2 140.3 %copy-start.66 = (f32[768]{0:T(1024)S(1)}, f32[768]{0:T(1024)}, u32[]{:S(2)}) copy-start(f32[768]{0:T(1024)} %get-tuple-element.623) | copy-start | bytes 9220
  178.2 140.3 %copy-start.69 = (f32[768]{0:T(1024)S(1)}, f32[768]{0:T(1024)}, u32[]{:S(2)}) copy-start(f32[768]{0:T(1024)} %get-tuple-element.620) | copy-start | bytes 9220
  203.4 20.7 %copy-start.4 = (bf16[2048,12,64]{0,2,1:T(8,128)(2,1)S(1)}, bf16[2048,12,64]{0,2,1:T(8,128)(2,1)}, u32[]{:S(2)}) copy-start(bf16[2048,12,64]{0,2,1:T(8,128)(2,1)} %get-tuple-element.1053) | copy-start | bytes 9437188 | tf_op jit(solution)/shard_map/while/body/eval_jaxpr/while
  273.3 20.7 %copy-start.4 = (bf16[2048,12,64]{0,2,1:T(8,128)(2,1)S(1)}, bf16[2048,12,64]{0,2,1:T(8,128)(2,1)}, u32[]{:S(2)}) copy-start(bf16[2048,12,64]{0,2,1:T(8,128)(2,1)} %get-tuple-element.1053) | copy-start | bytes 9437188 | tf_op jit(solution)/shard_map/while/body/eval_jaxpr/while
  318.5 6.4 copy-start.42
  318.5 6.4 copy-start.62
  323.2 95.0 %copy-start.37 = (f32[1024]{0:T(1024)}, f32[1024]{0:T(1024)S(1)}, u32[]{:S(2)}) copy-start(f32[1024]{0:T(1024)S(1)} %broadcast_multiply_fusion.7) | copy-start | bytes 12292
  323.6 94.6 %copy-start.57 = (f32[1024]{0:T(1024)}, f32[1024]{0:T(1024)S(1)}, u32[]{:S(2)}) copy-start(f32[1024]{0:T(1024)S(1)} %add_rsqrt_fusion.1) | copy-start | bytes 12292
  324.9 37.8 %copy-start.68 = (f32[768]{0:T(1024)S(1)}, f32[768]{0:T(1024)}, u32[]{:S(2)}) copy-start(f32[768]{0:T(1024)} %get-tuple-element.617) | copy-start | bytes 9220
  362.6 10.2 copy-start.9
  362.7 10.2 copy-start.41
  386.1 19.5 %copy-start.8 = (f32[1024,768]{0,1:T(8,128)S(1)}, f32[1024,768]{0,1:T(8,128)}, u32[]{:S(2)}) copy-start(f32[1024,768]{0,1:T(8,128)} %copy-done.7) | copy-start | bytes 9437188
  405.7 12.5 copy-start.14
  419.9 6.8 copy-start.28
  426.7 324.5 %copy-start.35 = (f32[1024]{0:T(1024)S(1)}, f32[1024]{0:T(1024)}, u32[]{:S(2)}) copy-start(f32[1024]{0:T(1024)} %copy-done.33) | copy-start | bytes 12292
  426.7 324.5 %copy-start.46 = (f32[768]{0:T(1024)S(1)}, f32[768]{0:T(1024)}, u32[]{:S(2)}) copy-start(f32[768]{0:T(1024)} %get-tuple-element.624) | copy-start | bytes 9220
  426.7 324.5 %copy-start.55 = (f32[1024]{0:T(1024)S(1)}, f32[1024]{0:T(1024)}, u32[]{:S(2)}) copy-start(f32[1024]{0:T(1024)} %copy-done.53) | copy-start | bytes 12292
  751.2 6.6 copy-start.11
  759.5 6.8 copy-start.30
  768.9 11.8 copy-start.2
  768.9 11.8 copy-start.6
  768.9 12.6 copy-start.16
  863.8 11.8 copy-start.2
  863.8 11.8 copy-start.6
  863.8 12.6 copy-start.16
  958.4 122.9 %reduce-scatter.6.cloned.1.call-start = ((), (), s32[]{:S(2)}) async-start(), calls=%async_computation.5 | async-start | bytes 21233664 | tf_op jit(solution)/shard_map/reduce_scatter | solution.py:352
  1013.0 6.6 copy-start.20
  1013.0 6.5 copy-start.25
  1022.5 10.0 slice-start.2
  1025.6 7.0 slice-start.3
  1056.7 48.5 %reduce-scatter.10.cloned.1.call-start = ((), (), s32[]{:S(2)}) async-start(), calls=%async_computation.7 | async-start | bytes 294912
  1061.6 322.4 %all-reduce.3.cloned.1.call-start = ((), (), s32[]{:S(2)}) async-start(), calls=%async_computation.8 | async-start | bytes 18874368 | tf_op jit(solution)/shard_map/psum | solution.py:363
  1096.0 92.1 %copy-start.32 = (f32[384,17]{0,1:T(8,128)S(1)}, f32[384,17]{0,1:T(8,128)}, u32[]{:S(2)}) copy-start(f32[384,17]{0,1:T(8,128)} %param.27) | copy-start | bytes 78340
  1096.0 92.1 %copy-start.39 = (f32[384,17]{0,1:T(8,128)S(1)}, f32[384,17]{0,1:T(8,128)}, u32[]{:S(2)}) copy-start(f32[384,17]{0,1:T(8,128)} %param.30) | copy-start | bytes 78340
  1096.0 92.1 %copy-start.40 = (f32[384,17]{0,1:T(8,128)S(1)}, f32[384,17]{0,1:T(8,128)}, u32[]{:S(2)}) copy-start(f32[384,17]{0,1:T(8,128)} %param.33) | copy-start | bytes 78340
  (47 other events, 157.9 us)
Sparse Core Ops, SparseCore 0:
  16.5 29.1 all-gather.2
  47.8 15.5 all-gather.4
  958.6 13.7 reduce-scatter.7
  1056.8 24.4 reduce-scatter.5
  1084.1 8.8 reduce-scatter.9
  1100.3 283.7 all-reduce.2
where the time goes:
time: 1450 us; the launch traced here: 1440 us
  matrix products  648 us (45%)
  other arithmetic  303 us (21%)
  waiting for transfers between devices  223 us (15%)
  local copies, waits for them, and re-layouts  154 us (11%)
  blocking collectives  83.9 us (6%)
  between operations  15.3 us (1%)
  loops' own time  14.6 us (1%)
    psum x1, waiting for transfers between devices, on_device(): lax.psum(wide_owned.astype(jnp.bfloat16), 'rep').astype(jnp.float32)  195 us
    dot_general x8, matrix products, one_block(): jnp.einsum('qhd,khd->hqk', head_q, head_k, preferred_element_type=jnp.flo...  133 us
    convert_element_type x4, other arithmetic, one_block(): scores_grad = (probs * (prob_grad - centre)).astype(jnp.bfloat16)  125 us
    dot_general x4, matrix products, one_block(): jnp.einsum('qhd,khd->hqk', head_g, head_v, preferred_element_type=jnp.flo...  105 us
    psum x1, blocking collectives, on_device(): lax.psum(vec_owned.astype(jnp.bfloat16), 'rep').astype(jnp.float32)  82 us
    dot_general x7, matrix products, matmul(): return jnp.dot(left, right, preferred_element_type=jnp.float32)  73.7 us
    dot_general x4, matrix products, one_block(): jnp.einsum('hqk,qhd->khd', probs.astype(jnp.bfloat16), head_g, preferred_...  73.5 us
    reduce_sum x4, other arithmetic, one_block(): row_total = jnp.sum(weights, axis=-1, keepdims=True)  66 us
  transfers between devices with their start and end apart: 6, of which 3 were waited for; matrix products, arithmetic and copies ran while one was open for 31% of the time, Pallas kernels for 0%

commit v1 on v0

v1 whole, which is shorter than its diff:
```python
from functools import partial
import math

import jax
import jax.numpy as jnp
from jax import lax
from jax.experimental import pallas as pl
from jax.experimental.pallas import tpu as pltpu
from jax.sharding import PartitionSpec as P

D = 768
H = 12
HD = 64
FF = 3072
LEN = 1024
BLK = 256
STEP = 4


eps_norm = 1e-05
eps_adam = 1e-08
beta_one = 0.5
beta_two = 0.5
learn_rate = 0.03
vec_rate = 0.25
weight_decay = 0.1
masked_score = -1e30
FACTOR = HD ** (-0.5)
SCALE2 = FACTOR / math.log(2.0)


def matmul(left, right):
    return jnp.dot(left, right, preferred_element_type=jnp.float32)


def matmul_left(left, right):
    return lax.dot_general(
        left, right, (((0,), (0,)), ((), ())), preferred_element_type=jnp.float32
    )


def matmul_right(left, right):
    return lax.dot_general(
        left, right, (((1,), (1,)), ((), ())), preferred_element_type=jnp.float32
    )


def norm_forward(resid, gain, shift):
    average = jnp.mean(resid, axis=-1, keepdims=True)
    centred = resid - average
    inverse = lax.rsqrt(jnp.mean(centred * centred, axis=-1, keepdims=True) + eps_norm)
    normed = centred * inverse
    return (normed * gain + shift, normed, inverse)


def norm_backward(upstream, normed, inverse, gain):
    scaled = upstream * gain
    centred = scaled - jnp.mean(scaled, axis=-1, keepdims=True)
    resid_grad = inverse * (centred - normed * jnp.mean(scaled * normed, axis=-1, keepdims=True))
    return (resid_grad, jnp.sum(upstream * normed, axis=0), jnp.sum(upstream, axis=0))


def head_masks(rows):
    first = lax.broadcasted_iota(jnp.int32, (rows, 128), 1) < HD
    return (first, jnp.logical_not(first))


def keep(mask, value):
    return jnp.where(mask, value, jnp.zeros((), value.dtype))


def rows_dot(left, right):
    return jnp.dot(left, right, preferred_element_type=jnp.float32)


def rows_dot_t(left, right):
    return lax.dot_general(
        left, right, (((1,), (1,)), ((), ())), preferred_element_type=jnp.float32
    )


def forward_kernel(causal, mask_ref, q_ref, k_ref, v_ref, o_ref, lse_ref, qm_ref, vt_ref, acc_ref, sum_ref, top_ref):
    rows, keys = q_ref.shape[0], k_ref.shape[0]
    tile = BLK
    seq = pl.program_id(0)
    queries = q_ref[...]
    for head, mask in enumerate(head_masks(rows)):
        qm_ref[head] = keep(mask, queries)
    vt_ref[...] = v_ref[...].T
    if causal:
        below = lax.broadcasted_iota(jnp.int32, (BLK, BLK), 0) <= lax.broadcasted_iota(
            jnp.int32, (BLK, BLK), 1
        )

    def start_of(j):
        return j * tile if causal else 0

    def scores_of(j, head):
        begin = start_of(j)
        scores = rows_dot_t(k_ref[j * tile : (j + 1) * tile, :], qm_ref[head, begin:, :]) * SCALE2
        if causal:
            pieces = [jnp.where(below, scores[:, :BLK], masked_score)]
            for i in range(j + 1, rows // BLK):
                off = jnp.where(mask_ref[seq, i, j] > 0, 0.0, masked_score)
                pieces.append(scores[:, (i - j) * BLK : (i - j + 1) * BLK] + off)
            scores = jnp.concatenate(pieces, axis=1)
        return scores

    def add_tile(j, head, scores, shift):
        begin = start_of(j)
        if shift is not None:
            scores = scores - shift[:, begin:]
        probs = jnp.exp2(scores)
        total = jnp.sum(probs, axis=0, keepdims=True)
        mixed = rows_dot(
            vt_ref[head * HD : (head + 1) * HD, j * tile : (j + 1) * tile], probs.astype(jnp.bfloat16)
        )
        if j == 0:
            sum_ref[head : head + 1, :] = total
            acc_ref[head] = mixed
        else:
            sum_ref[head : head + 1, begin:] += total
            acc_ref[head, :, begin:] += mixed

    def finish(shifts):
        both = []
        for head in range(2):
            total = sum_ref[head : head + 1, :]
            lse = jnp.log2(total)
            if shifts is not None:
                lse = lse + shifts[head]
            lse_ref[0, 0, head : head + 1, :] = lse
            both.append(acc_ref[head] * (1.0 / total))
        o_ref[...] = jnp.concatenate(both, axis=0).T.astype(jnp.bfloat16)

    lse_ref[...] = jnp.zeros_like(lse_ref)
    waiting = []
    for j in range(keys // tile):
        for head in range(2):
            waiting.append((j, head, scores_of(j, head)))
            if len(waiting) > 1:
                add_tile(*waiting.pop(0), None)
    while waiting:
        add_tile(*waiting.pop(0), None)
    finish(None)
    sums = sum_ref[...]
    usable = jnp.min(jnp.where((sums > 1e-25) & (sums < 1e30), 1, 0))

    @pl.when(usable == 0)
    def _():
        for head in range(2):
            for j in range(keys // tile):
                peak = jnp.max(scores_of(j, head), axis=0, keepdims=True)
                begin = start_of(j)
                if j == 0:
                    top_ref[head : head + 1, :] = peak
                else:
                    top_ref[head : head + 1, begin:] = jnp.maximum(
                        top_ref[head : head + 1, begin:], peak
                    )
        shifts = [top_ref[0:1, :], top_ref[1:2, :]]
        for head in range(2):
            for j in range(keys // tile):
                add_tile(j, head, scores_of(j, head), shifts[head])
        finish(shifts)


def attend_forward(queries, keys_in, values_in, block_table, causal):
    seqs = block_table.shape[0]
    rows, keys = queries.shape[0] // seqs, keys_in.shape[0] // seqs
    spec_q = pl.BlockSpec((rows, 128), lambda s, i, m: (s, i))
    spec_k = pl.BlockSpec((keys, 128), lambda s, i, m: (s, i))
    spec_l = pl.BlockSpec((1, 1, 8, rows), lambda s, i, m: (s, i, 0, 0))
    area = rows * keys * H * HD * seqs
    return pl.pallas_call(
        partial(forward_kernel, causal),
        grid_spec=pltpu.PrefetchScalarGridSpec(
            num_scalar_prefetch=1,
            grid=(seqs, D // 128),
            in_specs=[spec_q, spec_k, spec_k],
            out_specs=[spec_q, spec_l],
            scratch_shapes=[
                pltpu.VMEM((2, rows, 128), jnp.bfloat16),
                pltpu.VMEM((128, keys), jnp.bfloat16),
                pltpu.VMEM((2, HD, rows), jnp.float32),
                pltpu.VMEM((2, rows), jnp.float32),
                pltpu.VMEM((2, rows), jnp.float32),
            ],
        ),
        out_shape=[
            jax.ShapeDtypeStruct(queries.shape, jnp.bfloat16),
            jax.ShapeDtypeStruct((seqs, D // 128, 8, rows), jnp.float32),
        ],
        compiler_params=pltpu.CompilerParams(vmem_limit_bytes=48 << 20),
        cost_estimate=pl.CostEstimate(
            flops=(8 if causal else 16) * area, bytes_accessed=4 * queries.size, transcendentals=0
        ),
    )(block_table, queries, keys_in, values_in)


def backward_kernel(
    causal, mask_ref, q_ref, k_ref, v_ref, m_ref, x_ref, lse_ref, dq_ref, dk_ref, dv_ref,
    qm_ref, mm_ref, qt_ref, mt_ref, col_ref, acc_ref, dkt_ref, dvt_ref,
):
    rows, keys = q_ref.shape[0], k_ref.shape[0]
    seq = pl.program_id(0)
    step, tile = (BLK, BLK) if causal else (2 * BLK, 2 * BLK)
    masks = head_masks(rows)
    masks_k = head_masks(tile)
    queries, grads = q_ref[...], m_ref[...]
    qt_ref[...] = queries.T
    mt_ref[...] = grads.T
    product = grads.astype(jnp.float32) * x_ref[...].astype(jnp.float32)
    lse = lse_ref[0, 0].T
    for head in range(2):
        qm_ref[head] = keep(masks[head], queries)
        mm_ref[head] = keep(masks[head], grads)
        centre = jnp.sum(keep(masks[head], product), axis=1, keepdims=True)
        col_ref[head] = jnp.broadcast_to(centre, (rows, 128))
        col_ref[2 + head] = jnp.broadcast_to(lse[:, head : head + 1], (rows, 128))
    if causal:
        below = lax.broadcasted_iota(jnp.int32, (BLK, BLK), 0) >= lax.broadcasted_iota(
            jnp.int32, (BLK, BLK), 1
        )

    def widen(column):
        return jnp.concatenate([column] * (tile // 128), axis=1)

    for j in range(keys // tile):
        key_rows = slice(j * tile, (j + 1) * tile)
        key, value = k_ref[key_rows, :], v_ref[key_rows, :]
        key_masked = [keep(mask, key) for mask in masks_k]
        total_k, total_v = [None, None], [None, None]
        first_step = j if causal else 0
        for i in range(first_step, rows // step):
            here = slice(i * step, (i + 1) * step)
            for head in range(2):
                scores = rows_dot_t(qm_ref[head, here, :], key)
                prob_grad = rows_dot_t(mm_ref[head, here, :], value)
                level = col_ref[2 + head, here]
                if causal and i > j:
                    level = level + jnp.where(mask_ref[seq, i, j] > 0, 0.0, -masked_score)
                probs = jnp.exp2(scores * SCALE2 - widen(level))
                if causal and i == j:
                    probs = jnp.where(below, probs, 0.0)
                score_grad = (probs * (prob_grad - widen(col_ref[head, here]))).astype(jnp.bfloat16)
                probs = probs.astype(jnp.bfloat16)
                part = slice(head * HD, (head + 1) * HD)
                add_v = rows_dot(mt_ref[part, here], probs)
                add_k = rows_dot(qt_ref[part, here], score_grad)
                total_v[head] = add_v if total_v[head] is None else total_v[head] + add_v
                total_k[head] = add_k if total_k[head] is None else total_k[head] + add_k
                add_q = rows_dot(score_grad, key_masked[head])
                if j == 0 and head == 0:
                    acc_ref[here, :] = add_q
                else:
                    acc_ref[here, :] += add_q
        for head in range(2):
            part = slice(head * HD, (head + 1) * HD)
            dkt_ref[part, key_rows] = total_k[head] * FACTOR
            dvt_ref[part, key_rows] = total_v[head]
    dq_ref[...] = (acc_ref[...] * FACTOR).astype(jnp.bfloat16)
    dk_ref[...] = dkt_ref[...].T.astype(jnp.bfloat16)
    dv_ref[...] = dvt_ref[...].T.astype(jnp.bfloat16)


def attend_backward(queries, keys_in, values_in, block_table, causal, mixed, lse, mixed_grad):
    seqs = block_table.shape[0]
    rows, keys = queries.shape[0] // seqs, keys_in.shape[0] // seqs
    spec_q = pl.BlockSpec((rows, 128), lambda s, i, m: (s, i))
    spec_k = pl.BlockSpec((keys, 128), lambda s, i, m: (s, i))
    spec_l = pl.BlockSpec((1, 1, 8, rows), lambda s, i, m: (s, i, 0, 0))
    area = rows * keys * H * HD * seqs
    return pl.pallas_call(
        partial(backward_kernel, causal),
        grid_spec=pltpu.PrefetchScalarGridSpec(
            num_scalar_prefetch=1,
            grid=(seqs, D // 128),
            in_specs=[spec_q, spec_k, spec_k, spec_q, spec_q, spec_l],
            out_specs=[spec_q, spec_k, spec_k],
            scratch_shapes=[
                pltpu.VMEM((2, rows, 128), jnp.bfloat16),
                pltpu.VMEM((2, rows, 128), jnp.bfloat16),
                pltpu.VMEM((128, rows), jnp.bfloat16),
                pltpu.VMEM((128, rows), jnp.bfloat16),
                pltpu.VMEM((4, rows, 128), jnp.float32),
                pltpu.VMEM((rows, 128), jnp.float32),
                pltpu.VMEM((128, keys), jnp.float32),
                pltpu.VMEM((128, keys), jnp.float32),
            ],
        ),
        out_shape=[
            jax.ShapeDtypeStruct(queries.shape, jnp.bfloat16),
            jax.ShapeDtypeStruct(keys_in.shape, jnp.bfloat16),
            jax.ShapeDtypeStruct(keys_in.shape, jnp.bfloat16),
        ],
        compiler_params=pltpu.CompilerParams(vmem_limit_bytes=48 << 20),
        cost_estimate=pl.CostEstimate(
            flops=(20 if causal else 40) * area, bytes_accessed=4 * queries.size, transcendentals=0
        ),
    )(block_table, queries, keys_in, values_in, mixed_grad, mixed, lse)


def adam_update(master, first, second, gradient, decay_on, rate):
    first_new = beta_one * first + (1.0 - beta_one) * gradient
    second_new = beta_two * second + (1.0 - beta_two) * gradient * gradient
    first_hat = first_new / (1.0 - beta_one**STEP)
    second_hat = second_new / (1.0 - beta_two**STEP)
    master_new = master - rate * (first_hat / (jnp.sqrt(second_hat) + eps_adam) + decay_on * master)
    return (master_new, first_new, second_new)


def column_sum(matrix):
    return jnp.sum(matrix.astype(jnp.float32), axis=0)


def on_device(
    tokens,
    encoder_states,
    cotangent,
    block_mask,
    wide_master,
    narrow_master,
    vec_master,
    wide_first,
    narrow_first,
    vec_first,
    wide_second,
    narrow_second,
    vec_second,
):
    replicas = lax.axis_size("rep")
    shards = lax.axis_size("shard")
    tokens_all = tokens.shape[0] * replicas * shards

    copies = (
        wide_master.astype(jnp.bfloat16),
        narrow_master.astype(jnp.bfloat16),
        vec_master.astype(jnp.bfloat16),
    )
    wide_full, narrow_full, vec_full = (
        lax.all_gather(copies[0], "shard", axis=0, tiled=True),
        lax.all_gather(copies[1], "shard", axis=0, tiled=True),
        lax.all_gather(copies[2], "shard", axis=0, tiled=True),
    )
    vector = vec_full.astype(jnp.float32)
    ffn_bias = vector[:, 6:10].T.reshape(FF)
    joint_proj = matmul(tokens, wide_full[:, : 3 * D])
    queries = (joint_proj[:, :D] + vector[:, 0]).astype(jnp.bfloat16)
    keys_self = joint_proj[:, D : 2 * D].astype(jnp.bfloat16)
    values_self = (joint_proj[:, 2 * D :] + vector[:, 1]).astype(jnp.bfloat16)
    mixed_self, totals_self = attend_forward(queries, keys_self, values_self, block_mask, True)
    branch_one = matmul(mixed_self, wide_full[:, 3 * D : 4 * D]) + vector[:, 2]
    normed_one, unit_one, scale_one = norm_forward(
        tokens.astype(jnp.float32) + branch_one, vector[:, 11], vector[:, 14]
    )
    normed_low = normed_one.astype(jnp.bfloat16)
    cross_queries = (matmul(normed_low, wide_full[:, 4 * D : 5 * D]) + vector[:, 3]).astype(
        jnp.bfloat16
    )
    enc_proj = matmul(encoder_states, wide_full[:, 5 * D : 7 * D])
    cross_keys = enc_proj[:, :D].astype(jnp.bfloat16)
    cross_values = (enc_proj[:, D:] + vector[:, 4]).astype(jnp.bfloat16)

    mixed_cross, totals_cross = attend_forward(
        cross_queries, cross_keys, cross_values, block_mask, False
    )
    branch_two = matmul(mixed_cross, wide_full[:, 7 * D : 8 * D]) + vector[:, 5]
    normed_two, unit_two, scale_two = norm_forward(
        normed_one + branch_two, vector[:, 12], vector[:, 15]
    )
    second_low = normed_two.astype(jnp.bfloat16)
    hidden = matmul(second_low, wide_full[:, 8 * D :]) + ffn_bias
    active_full, gelu_pull = jax.vjp(partial(jax.nn.gelu, approximate=False), hidden)
    active = active_full.astype(jnp.bfloat16)
    branch_three = matmul(active, narrow_full) + vector[:, 10]
    final_out, unit_three, scale_three = norm_forward(
        normed_two + branch_three, vector[:, 13], vector[:, 16]
    )
    output = final_out.astype(jnp.bfloat16)
    grad_three, gain_three, shift_three = norm_backward(
        cotangent.astype(jnp.float32), unit_three, scale_three, vector[:, 13]
    )
    grad_ffn = grad_three.astype(jnp.bfloat16)
    grad_narrow = matmul_left(active, grad_ffn)
    grad_hidden = gelu_pull(matmul_right(grad_ffn, narrow_full))[0].astype(jnp.bfloat16)
    grad_ffn_in = matmul_left(second_low, grad_hidden)
    grad_two, gain_two, shift_two = norm_backward(
        grad_three + matmul_right(grad_hidden, wide_full[:, 8 * D :]),
        unit_two,
        scale_two,
        vector[:, 12],
    )
    grad_cross = grad_two.astype(jnp.bfloat16)
    grad_cross_out = matmul_left(mixed_cross, grad_cross)
    grad_cross_mix = matmul_right(grad_cross, wide_full[:, 7 * D : 8 * D]).astype(jnp.bfloat16)

    grad_cross_queries, grad_cross_keys, grad_cross_values = attend_backward(
        cross_queries, cross_keys, cross_values, block_mask, False, mixed_cross, totals_cross, grad_cross_mix
    )
    grad_enc_proj = jnp.concatenate([grad_cross_keys, grad_cross_values], 1)
    grad_cross_query = matmul_left(normed_low, grad_cross_queries)
    grad_cross_pair = matmul_left(encoder_states, grad_enc_proj)
    enc_grad = matmul_right(grad_enc_proj, wide_full[:, 5 * D : 7 * D]).astype(jnp.bfloat16)
    grad_one, gain_one, shift_one = norm_backward(
        grad_two + matmul_right(grad_cross_queries, wide_full[:, 4 * D : 5 * D]),
        unit_one,
        scale_one,
        vector[:, 11],
    )
    grad_self = grad_one.astype(jnp.bfloat16)
    grad_self_out = matmul_left(mixed_self, grad_self)
    grad_self_mix = matmul_right(grad_self, wide_full[:, 3 * D : 4 * D]).astype(jnp.bfloat16)

    grad_queries, grad_keys, grad_values = attend_backward(
        queries, keys_self, values_self, block_mask, True, mixed_self, totals_self, grad_self_mix
    )
    grad_joint_proj = jnp.concatenate([grad_queries, grad_keys, grad_values], 1)
    grad_joint = matmul_left(tokens, grad_joint_proj)
    in_grad = (grad_one + matmul_right(grad_joint_proj, wide_full[:, : 3 * D])).astype(jnp.bfloat16)
    factor = float(tokens_all) ** (-0.5)

    def summed(term):
        owned = lax.psum_scatter(
            (term * factor).astype(jnp.bfloat16), "shard", scatter_dimension=0, tiled=True
        )
        return lax.psum(owned, "rep").astype(jnp.float32)

    ffn_sum = summed(grad_ffn_in)
    narrow_grad = summed(grad_narrow)
    cross_sum = summed(jnp.concatenate([grad_self_out, grad_cross_query, grad_cross_pair, grad_cross_out], 1))
    joint_sum = summed(grad_joint)
    wide_grad = jnp.concatenate([joint_sum, cross_sum, ffn_sum], 1)
    bias_front = jnp.stack(
        [
            column_sum(grad_joint_proj[:, :D]),
            column_sum(grad_joint_proj[:, 2 * D :]),
            column_sum(grad_self),
            column_sum(grad_cross_queries),
            column_sum(grad_enc_proj[:, D:]),
            column_sum(grad_cross),
        ],
        1,
    )
    bias_back = jnp.stack(
        [column_sum(grad_ffn), gain_one, gain_two, gain_three, shift_one, shift_two, shift_three], 1
    )
    vec_grad = summed(jnp.concatenate([bias_front, column_sum(grad_hidden).reshape(4, D).T, bias_back], 1))
    wide_new, wide_first_new, wide_second_new = adam_update(
        wide_master, wide_first, wide_second, wide_grad, weight_decay, learn_rate
    )
    narrow_new, narrow_first_new, narrow_second_new = adam_update(
        narrow_master, narrow_first, narrow_second, narrow_grad, weight_decay, learn_rate
    )
    vec_new, vec_first_new, vec_second_new = adam_update(
        vec_master, vec_first, vec_second, vec_grad, 0.0, vec_rate
    )
    return (
        output,
        in_grad,
        enc_grad,
        wide_grad,
        narrow_grad,
        vec_grad,
        wide_new,
        narrow_new,
        vec_new,
        wide_first_new,
        narrow_first_new,
        vec_first_new,
        wide_second_new,
        narrow_second_new,
        vec_second_new,
        wide_new.astype(jnp.bfloat16),
        narrow_new.astype(jnp.bfloat16),
        vec_new.astype(jnp.bfloat16),
    )


def solution(mesh):
    in_specs = (
        P(("rep", "shard"), None),
        P(("rep", "shard"), None),
        P(("rep", "shard"), None),
        P(("rep", "shard"), None, None),
        P("shard", None),
        P("shard", None),
        P("shard", None),
        P("shard", None),
        P("shard", None),
        P("shard", None),
        P("shard", None),
        P("shard", None),
        P("shard", None),
    )
    out_specs = (
        P(("rep", "shard"), None),
        P(("rep", "shard"), None),
        P(("rep", "shard"), None),
        P("shard", None),
        P("shard", None),
        P("shard", None),
        P("shard", None),
        P("shard", None),
        P("shard", None),
        P("shard", None),
        P("shard", None),
        P("shard", None),
        P("shard", None),
        P("shard", None),
        P("shard", None),
        P("shard", None),
        P("shard", None),
        P("shard", None),
    )
    return jax.shard_map(
        on_device, mesh=mesh, in_specs=in_specs, out_specs=out_specs, check_vma=False
    )
```

time: 1450 us -> 861 us (0.59)
  matrix products: 648 us -> 168 us
  other arithmetic: 303 us -> 95.3 us
  Pallas kernels: 0 us -> 141 us
  waiting for transfers between devices: 223 us -> 172 us
  local copies, waits for them, and re-layouts: 154 us -> 177 us
  loops' own time: 14.6 us -> 0 us
    dot_general x28 -> x0, matrix products: 468 us -> none  [the longest x8 133 us: one_block(): jnp.einsum('qhd,khd->hqk', head_q, head_k, preferred_element_type=jnp.flo...]
    convert_element_type x8 -> x2, other arithmetic: 145 us -> 3.73 us  [summed(): (term * factor).astype(jnp.bfloat16)]
    pallas_call x0 -> x4, Pallas kernels: none -> 141 us  [the longest x2 99.4 us: attend_backward(): pl.pallas_call(partial(backward_kernel, causal), grid_spec=pltpu.Prefetch...]
    unnamed x163 -> x148, local copies, waits for them, and re-layouts: 36 us -> 173 us
    reduce_sum x4 -> x0, other arithmetic: 66 us -> none  [one_block(): row_total = jnp.sum(weights, axis=-1, keepdims=True)]
    psum x1, waiting for transfers between devices: 195 us -> 153 us  [summed(): return lax.psum(owned, 'rep').astype(jnp.float32)]
    dynamic_slice x28 -> x0, local copies, waits for them, and re-layouts: 36.8 us -> none  [the longest x8 15.2 us: one_block(): lax.dynamic_slice_in_dim(mixed_grad, offset, width_rows, 0)]
    dynamic_update_slice x12 -> x0, local copies, waits for them, and re-layouts: 25.7 us -> none  [attend_forward(): lax.map(one_block, jnp.arange(blocks_count, dtype=jnp.int32))]
  transfers between devices with their start and end apart: 6 -> 8, of which waited for: 3 -> 3; matrix products, arithmetic and copies ran while one was open for 31% -> 25% of each run, Pallas kernels for 0% -> 5%
where the time goes in v1:
time: 861 us; the launch traced here: 851 us
  local copies, waits for them, and re-layouts  177 us (21%)
  waiting for transfers between devices  172 us (20%)
  matrix products  168 us (20%)
  Pallas kernels  141 us (16%)
  other arithmetic  95.3 us (11%)
  blocking collectives  82.7 us (10%)
  between operations  15.5 us (2%)
    unnamed x148, local copies, waits for them, and re-layouts  173 us
    psum x1, waiting for transfers between devices, summed(): return lax.psum(owned, 'rep').astype(jnp.float32)  153 us
    pallas_call x2, Pallas kernels, attend_backward(): pl.pallas_call(partial(backward_kernel, causal), grid_spec=pltpu.Prefetch...  99.4 us
    psum x1, blocking collectives, summed(): return lax.psum(owned, 'rep').astype(jnp.float32)  80.8 us
    dot_general x7, matrix products, matmul(): return jnp.dot(left, right, preferred_element_type=jnp.float32)  72.1 us
    dot_general x7, matrix products, matmul_right(): lax.dot_general(left, right, (((1,), (1,)), ((), ())), preferred_element_...  61.4 us
    pallas_call x2, Pallas kernels, attend_forward(): pl.pallas_call(partial(forward_kernel, causal), grid_spec=pltpu.PrefetchS...  41.3 us
    dot_general x7, matrix products, matmul_left(): lax.dot_general(left, right, (((0,), (0,)), ((), ())), preferred_element_...  34.5 us
  transfers between devices with their start and end apart: 8, of which 3 were waited for; matrix products, arithmetic and copies ran while one was open for 25% of the time, Pallas kernels for 5%

profile of v1, /device:TPU:0, one launch (start us, length us, event | category | flops | bytes accessed | tf_op | source)
XLA Modules:
  0.0 851.1 jit_solution(11559440805444694424)
XLA Ops:
  7.2 9.1 %convert_element_type.129 = bf16[384,9216]{1,0:T(8,128)(2,1)} convert(f32[384,9216]{1,0:T(8,128)} %param.17) | non-fusion elementwise | flops 3538944 | bytes 21233664 | tf_op jit(solution)/shard_map/convert_element_type | solution.py:337
  16.5 4.0 convert_element_type.139
  26.4 2.8 copy.49
  29.2 16.5 %all-gather.3.cloned.1.call-done = bf16[768,9216]{1,0:T(8,128)(2,1)} async-done(((bf16[384,9216]{1,0:T(8,128)(2,1)}), bf16[768,9216]{1,0:T(8,128)(2,1)}) %all-gather.3.cloned.1.call-update) | async-done | bytes 14155792 | tf_op jit(solution)/shard_map/all_gather | solution.py:342
  45.7 6.3 fusion.26
  54.0 13.1 %shard_map.268 = (bf16[1024,768]{1,0:T(8,128)(2,1)S(1)}, f32[1,6,8,1024]{3,2,1,0:T(8,128)S(1)}) custom-call(s32[1,4,4]{2,1,0:T(4,128)S(1)} %copy-done.8, bf16[1024,768]{1,0:T(8,128)(2,1)S(1)} %get-tuple-element.126.q_ref, bf16[1024,768]{1,0:T(8,128)(2,1)S(1)} %slice.190.k_ref, bf16[1024,768]{1,0:T(8,128)(2,1)} %get-tuple-element.125.v_ref), custom_call_target="tpu_custom_call" | custom-call | flops 6442450944 | bytes 3145728 | tf_op jit(solution)/shard_map/pallas_call | solution.py:175
  67.2 3.5 fusion.65
  71.1 7.5 fusion.31
  83.3 3.1 add_convert_fusion.3.q_ref
  86.5 28.2 %shard_map.269 = (bf16[1024,768]{1,0:T(8,128)(2,1)S(1)}, f32[1,6,8,1024]{3,2,1,0:T(8,128)S(1)}) custom-call(s32[1,4,4]{2,1,0:T(4,128)S(1)} %copy-done.8, bf16[1024,768]{1,0:T(8,128)(2,1)S(1)} %add_convert_fusion.3.q_ref, bf16[2048,768]{1,0:T(8,128)(2,1)} %slice.189.k_ref, bf16[2048,768]{1,0:T(8,128)(2,1)} %fusion.8.v_ref), custom_call_target="tpu_custom_call" | custom-call | flops 25769803776 | bytes 3145728 | tf_op jit(solution)/shard_map/pallas_call | solution.py:175
  114.7 3.7 fusion.66
  120.1 38.1 %multiply_convert_fusion = (bf16[1024,3072]{1,0:T(8,128)(2,1)}, f32[1024,3072]{1,0:T(8,128)}, f32[1024,3072]{1,0:T(8,128)}) fusion(f32[3072]{0:T(1024)S(1)} %copy-done.53, bf16[768,9216]{1,0:T(8,128)(2,1)} %all-gather.3.cloned.1.call-done, f32[1024,768]{0,1:T(8,128)S(1)} %get-tuple-element.131, f32[768]{0:T(1024)S(1)} %copy-done.57, ...), kind=kOutput, calls=%fused_computation.8 | convolution fusion | flops 5043388416 | bytes 39348224 | tf_op jit(solution)/shard_map/dot_general | solution.py:33
  158.2 9.8 %fusion.67 = (f32[1024]{0:T(1024)S(1)}, f32[1024,768]{0,1:T(8,128)S(1)}) fusion(f32[768]{0:T(1024)} %get-tuple-element.88, bf16[1024,3072]{1,0:T(8,128)(2,1)} %get-tuple-element.123, bf16[3072,768]{1,0:T(8,128)(2,1)} %all-gather.5.cloned.1.call-done, f32[768]{0:T(1024)S(1)} %copy-done.58, f32[768]{0:T(1024)S(1)} %get-tuple-element.90, ...), kind=kOutput, calls=%fused_computation.154 | convolution fusion | flops 4837342208 | bytes 17323008 | tf_op jit(solution)/shard_map/dot_general | solution.py:33
  171.4 3.5 convert_reduce_fusion.3
  174.9 17.2 %convert_reduce_fusion = (f32[3072]{0:T(1024)}, bf16[1024,3072]{1,0:T(8,128)(2,1)}) fusion(f32[1024,3072]{1,0:T(8,128)} %get-tuple-element.124, bf16[1024,768]{0,1:T(8,128)(2,1)} %get-tuple-element.118, bf16[3072,768]{1,0:T(8,128)(2,1)} %all-gather.5.cloned.1.call-done, f32[1024,3072]{1,0:T(8,128)} %get-tuple-element.132, f32[3072]{0:T(1024)} %add.245), kind=kOutput, calls=%fused_computation.6 | convolution fusion | flops 4885312512 | bytes 37773312 | tf_op jit(solution)/shard_map/dot_general | solution.py:43
  192.1 12.6 %multiply_reduce_fusion = (f32[768]{0:T(1024)}, f32[1024]{0:T(1024)S(1)}, f32[1024]{0:T(1024)S(1)}, f32[768]{0:T(1024)}, f32[1024,768]{0,1:T(8,128)S(1)}) fusion(f32[1024,768]{0,1:T(8,128)} %copy-done.22, f32[1024]{0:T(1024)S(1)} %copy-done.48, f32[1024]{0:T(1024)S(1)} %broadcast_multiply_fusion.7, f32[768]{0:T(1024)S(1)} %get-tuple-element.90, ...), kind=kOutput, calls=%fused_computation.58 | convolution fusion | flops 4845989888 | bytes 22065152 | tf_op jit(solution)/shard_map/dot_general | solution.py:43
  206.5 3.8 convolution_convert_fusion.2.m_ref
  210.3 63.8 %shard_map.270 = (bf16[1024,768]{1,0:T(8,128)(2,1)S(1)}, bf16[2048,768]{1,0:T(8,128)(2,1)}, bf16[2048,768]{1,0:T(8,128)(2,1)}) custom-call(s32[1,4,4]{2,1,0:T(4,128)S(1)} %copy-done.9, bf16[1024,768]{1,0:T(8,128)(2,1)S(1)} %copy-done.15, bf16[2048,768]{1,0:T(8,128)(2,1)} %slice.189.k_ref, bf16[2048,768]{1,0:T(8,128)(2,1)} %fusion.8.v_ref, ...), custom_call_target="tpu_custom_call" | custom-call | flops 64424509440 | bytes 3145728 | tf_op jit(solution)/shard_map/pallas_call | solution.py:274
  274.2 4.4 multiply_reduce_fusion.1
  279.8 4.8 convolution_convert_fusion.1.m_ref
  284.6 35.5 %shard_map.271 = (bf16[1024,768]{1,0:T(8,128)(2,1)S(1)}, bf16[1024,768]{1,0:T(8,128)(2,1)S(1)}, bf16[1024,768]{1,0:T(8,128)(2,1)S(1)}) custom-call(s32[1,4,4]{2,1,0:T(4,128)S(1)} %copy-done.9, bf16[1024,768]{1,0:T(8,128)(2,1)} %copy-done.7, bf16[1024,768]{1,0:T(8,128)(2,1)} %copy-done.3, bf16[1024,768]{1,0:T(8,128)(2,1)} %get-tuple-element.125.v_ref, ...), custom_call_target="tpu_custom_call" | custom-call | flops 16106127360 | bytes 3145728 | tf_op jit(solution)/shard_map/pallas_call | solution.py:274
  324.1 5.4 fusion.10
  329.4 5.7 copy.71
  335.8 9.9 %multiply_convert_fusion.2 = bf16[768,3072]{1,0:T(8,128)(2,1)} fusion(bf16[1024,3072]{1,0:T(8,128)(2,1)} %get-tuple-element.138, f32[1024,768]{0,1:T(8,128)} %copy-done.22, f32[768]{0:T(1024)S(1)} %copy-done.59, f32[768]{0:T(1024)S(1)} %get-tuple-element.90, f32[1024]{0:T(1024)S(1)} %copy-done.49, f32[1024]{0:T(1024)S(1)} %broadcast_multiply_fusion.7), kind=kOutput, calls=%fused_computation.25 | convolution fusion | flops 4840488960 | bytes 14170112 | tf_op jit(solution)/shard_map/dot_general | solution.py:37
  360.9 5.4 convolution_bitcast_fusion
  366.3 3.7 fusion.7
  370.0 8.4 copy.73
  378.5 9.1 %multiply_convert_fusion.1 = bf16[3072,768]{1,0:T(8,128)(2,1)} fusion(bf16[1024,3072]{1,0:T(8,128)(2,1)} %get-tuple-element.123, bf16[1024,768]{0,1:T(8,128)(2,1)} %get-tuple-element.118), kind=kOutput, calls=%fused_computation.24 | convolution fusion | flops 4836556800 | bytes 12582912 | tf_op jit(solution)/shard_map/dot_general | solution.py:37
  390.2 2.7 convert_reduce_fusion.7
  395.1 3.9 copy.72
  399.0 4.3 copy.76
  403.3 4.9 copy.74
  410.4 15.1 %copy.59 = f32[384,9216]{0,1:T(8,128)} copy(f32[384,9216]{1,0:T(8,128)} %param.17) | data formatting | bytes 28311552 | tf_op args[4]
  425.5 15.2 %copy.56 = f32[384,9216]{0,1:T(8,128)} copy(f32[384,9216]{1,0:T(8,128)} %param.20) | data formatting | bytes 28311552 | tf_op args[7]
  440.7 15.1 %copy.57 = f32[384,9216]{0,1:T(8,128)} copy(f32[384,9216]{1,0:T(8,128)} %param.23) | data formatting | bytes 28311552 | tf_op args[10]
  458.4 9.5 %add_convert_fusion.1 = bf16[1024,768]{0,1:T(8,128)(2,1)} fusion(f32[1024,768]{0,1:T(8,128)} %copy-done.24, bf16[1024,2304]{1,0:T(8,128)(2,1)} %copy-done.31, bf16[768,9216]{1,0:T(8,128)(2,1)} %all-gather.3.cloned.1.call-done), kind=kOutput, calls=%fused_computation.66 | convolution fusion | flops 3625451520 | bytes 12976128 | tf_op jit(solution)/shard_map/dot_general | solution.py:43
  467.9 2.6 copy.61
  470.5 9.2 %convolution_convert_fusion = bf16[2048,768]{1,0:T(8,128)(2,1)} fusion(bf16[2048,1536]{1,0:T(8,128)(2,1)} %copy-done.28, bf16[768,9216]{1,0:T(8,128)(2,1)} %all-gather.3.cloned.1.call-done), kind=kOutput, calls=%fused_computation.48 | convolution fusion | flops 4833411072 | bytes 11796480 | tf_op jit(solution)/shard_map/dot_general | solution.py:43
  480.7 80.8 %psum.39 = bf16[384,17]{0,1:T(8,128)(2,1)S(1)} all-reduce(bf16[384,17]{0,1:T(8,128)(2,1)S(1)} %copy.78), channel_id=1, replica_groups=mesh['rep'=16,'shard'=2] {'rep'}, use_global_device_ids=true, to_apply=%region_35.0 | all-reduce | flops 6528 | bytes 26112 | tf_op jit(solution)/shard_map/psum | solution.py:427
  562.1 152.9 %all-reduce.3.cloned.1.call-done = (bf16[384,3072]{0,1:T(8,128)(2,1)}, bf16[384,3840]{0,1:T(8,128)(2,1)}, bf16[384,2304]{0,1:T(8,128)(2,1)}, bf16[1536,768]{1,0:T(8,128)(2,1)}) async-done(((bf16[384,3072]{0,1:T(8,128)(2,1)}, bf16[384,3840]{0,1:T(8,128)(2,1)}, bf16[384,2304]{0,1:T(8,128)(2,1)}, bf16[1536,768]{1,0:T(8,128)(2,1)}), (bf16[384,3072]{0,1:T(8,128)(2,1)}, bf16[384,3840]{0,1:T(8,128)(2,1)}, ...) | async-done | bytes 9437200 | tf_op jit(solution)/shard_map/psum | solution.py:427
  715.1 11.3 %maximum_convert_fusion = f32[384,9216]{0,1:T(8,128)} fusion(bf16[384,3072]{0,1:T(8,128)(2,1)} %get-tuple-element.99, bf16[384,3840]{0,1:T(8,128)(2,1)} %get-tuple-element.100, bf16[384,2304]{0,1:T(8,128)(2,1)} %get-tuple-element.101), kind=kLoop, calls=%fused_computation.26 | loop fusion | flops 21233664 | bytes 21233664 | tf_op jit(solution)/shard_map/concatenate | solution.py:433
  726.4 15.1 %copy.62 = f32[384,9216]{1,0:T(8,128)} copy(f32[384,9216]{0,1:T(8,128)} %maximum_convert_fusion) | data formatting | bytes 28311552
  741.5 33.9 %fusion.61 = (bf16[384,9216]{0,1:T(8,128)(2,1)}, f32[384,9216]{0,1:T(8,128)}, f32[384,9216]{0,1:T(8,128)}, f32[384,9216]{0,1:T(8,128)}) fusion(f32[384,9216]{0,1:T(8,128)} %copy.59, bf16[384,3072]{0,1:T(8,128)(2,1)} %get-tuple-element.99, bf16[384,3840]{0,1:T(8,128)(2,1)} %get-tuple-element.100, bf16[384,2304]{0,1:T(8,128)(2,1)} %get-tuple-element.101, ...), kind=kLoop, calls=%fused_computation.151 | loop fusion | flops 74317824 | bytes 99090432 | tf_op jit(solution)/shard_map/convert_element_type | solution.py:474
  775.4 15.1 %copy.63 = f32[384,9216]{1,0:T(8,128)} copy(f32[384,9216]{0,1:T(8,128)} %get-tuple-element.114) | data formatting | bytes 28311552
  790.5 15.1 %copy.64 = f32[384,9216]{1,0:T(8,128)} copy(f32[384,9216]{0,1:T(8,128)} %get-tuple-element.115) | data formatting | bytes 28311552
  805.6 15.1 %copy.65 = f32[384,9216]{1,0:T(8,128)} copy(f32[384,9216]{0,1:T(8,128)} %get-tuple-element.116) | data formatting | bytes 28311552
  820.7 10.3 %copy.66 = bf16[384,9216]{1,0:T(8,128)(2,1)} copy(bf16[384,9216]{0,1:T(8,128)(2,1)} %get-tuple-element.113) | data formatting | bytes 14155776
  831.0 12.9 %fusion.59 = (bf16[1536,768]{1,0:T(8,128)(2,1)}, f32[1536,768]{1,0:T(8,128)}, f32[1536,768]{1,0:T(8,128)}, f32[1536,768]{1,0:T(8,128)}, f32[1536,768]{1,0:T(8,128)}) fusion(f32[1536,768]{1,0:T(8,128)} %param.18, f32[1536,768]{1,0:T(8,128)} %param.21, f32[1536,768]{1,0:T(8,128)} %param.24, bf16[1536,768]{1,0:T(8,128)(2,1)} %get-tuple-element.102), kind=kLoop, calls=%fused_computation.150 | loop fusion | flops 18874368 | bytes 37748736 | tf_op jit(solution)/shard_map/convert_element_type | solution.py:475
  (207 shorter events, 51.6 us)
Async XLA Ops:
  7.2 63.9 %copy-start = (bf16[2048,768]{1,0:T(8,128)(2,1)S(1)}, bf16[2048,768]{1,0:T(8,128)(2,1)}, u32[]{:S(2)}) copy-start(bf16[2048,768]{1,0:T(8,128)(2,1)} %param.14) | copy-start | bytes 9437188
  7.2 38.5 %all-gather.3.cloned.1.call-start = ((), (), s32[]{:S(2)}) async-start(), calls=%async_computation.5 | async-start | bytes 21233664 | tf_op jit(solution)/shard_map/all_gather | solution.py:342
  16.4 4.1 copy-start.32
  16.4 141.8 %all-gather.5.cloned.1.call-start = ((), (), s32[]{:S(2)}) async-start(), calls=%async_computation.6 | async-start | bytes 7077888 | tf_op jit(solution)/shard_map/all_gather | solution.py:343
  20.5 374.6 %reduce-scatter.16.cloned.1.call-start = ((), (), s32[]{:S(2)}) async-start(), calls=%async_computation.8 | async-start | bytes 5308416
  23.2 60.2 %copy-start.54 = (f32[768]{0:T(1024)}, f32[768]{0:T(1024)S(1)}, u32[]{:S(2)}) copy-start(f32[768]{0:T(1024)S(1)} %get-tuple-element.94) | copy-start | bytes 9220
  23.2 91.5 %copy-start.39 = (f32[768]{0:T(1024)}, f32[768]{0:T(1024)S(1)}, u32[]{:S(2)}) copy-start(f32[768]{0:T(1024)S(1)} %get-tuple-element.95) | copy-start | bytes 9220
  54.0 13.1 %copy-start.7 = (bf16[1024,768]{1,0:T(8,128)(2,1)}, bf16[1024,768]{1,0:T(8,128)(2,1)S(1)}, u32[]{:S(2)}) copy-start(bf16[1024,768]{1,0:T(8,128)(2,1)S(1)} %get-tuple-element.126.q_ref) | copy-start | bytes 4718596
  54.0 13.2 %copy-start.30 = (bf16[1024,768]{0,1:T(8,128)(2,1)S(1)}, bf16[1024,768]{0,1:T(8,128)(2,1)}, u32[]{:S(2)}) copy-start(bf16[1024,768]{0,1:T(8,128)(2,1)} %copy.49) | copy-start | bytes 4718596
  70.7 44.0 %copy-start.19 = (f32[1024,768]{0,1:T(8,128)}, f32[1024,768]{0,1:T(8,128)S(1)}, u32[]{:S(2)}) copy-start(f32[1024,768]{0,1:T(8,128)S(1)} %get-tuple-element.129) | copy-start | bytes 9437188
  70.7 44.0 %copy-start.34 = (f32[1024]{0:T(1024)}, f32[1024]{0:T(1024)S(1)}, u32[]{:S(2)}) copy-start(f32[1024]{0:T(1024)S(1)} %broadcast_multiply_fusion.8) | copy-start | bytes 12292
  71.1 43.6 %copy-start.44 = (f32[1024]{0:T(1024)}, f32[1024]{0:T(1024)S(1)}, u32[]{:S(2)}) copy-start(f32[1024]{0:T(1024)S(1)} %add_rsqrt_fusion.2) | copy-start | bytes 12292
  86.4 28.2 %copy-start.14 = (bf16[1024,768]{1,0:T(8,128)(2,1)}, bf16[1024,768]{1,0:T(8,128)(2,1)S(1)}, u32[]{:S(2)}) copy-start(bf16[1024,768]{1,0:T(8,128)(2,1)S(1)} %add_convert_fusion.3.q_ref) | copy-start | bytes 4718596
  86.4 28.3 %copy-start.55 = (f32[768]{0:T(1024)S(1)}, f32[768]{0:T(1024)}, u32[]{:S(2)}) copy-start(f32[768]{0:T(1024)} %copy-done.54) | copy-start | bytes 9220
  86.4 28.3 %copy-start.60 = (f32[768]{0:T(1024)S(1)}, f32[768]{0:T(1024)}, u32[]{:S(2)}) copy-start(f32[768]{0:T(1024)} %get-tuple-element.91) | copy-start | bytes 9220
  114.6 3.8 copy-start.12
  118.9 39.3 %copy-start.47 = (f32[1024]{0:T(1024)}, f32[1024]{0:T(1024)S(1)}, u32[]{:S(2)}) copy-start(f32[1024]{0:T(1024)S(1)} %add_rsqrt_fusion.1) | copy-start | bytes 12292
  120.1 38.1 %copy-start.58 = (f32[768]{0:T(1024)S(1)}, f32[768]{0:T(1024)}, u32[]{:S(2)}) copy-start(f32[768]{0:T(1024)} %get-tuple-element.89) | copy-start | bytes 9220
  174.9 17.2 %copy-start.48 = (f32[1024]{0:T(1024)S(1)}, f32[1024]{0:T(1024)}, u32[]{:S(2)}) copy-start(f32[1024]{0:T(1024)} %copy-done.47) | copy-start | bytes 12292
  192.1 12.6 %copy-start.23 = (f32[1024,768]{0,1:T(8,128)S(1)}, f32[1024,768]{0,1:T(8,128)}, u32[]{:S(2)}) copy-start(f32[1024,768]{0,1:T(8,128)} %copy-done.22) | copy-start | bytes 9437188
  206.4 67.7 %copy-start.26 = (f32[1024,768]{0,1:T(8,128)}, f32[1024,768]{0,1:T(8,128)S(1)}, u32[]{:S(2)}) copy-start(f32[1024,768]{0,1:T(8,128)S(1)} %get-tuple-element.120) | copy-start | bytes 9437188
  206.4 3.8 copy-start.9
  206.4 3.8 copy-start.15
  210.2 63.9 %copy-start.20 = (f32[1024,768]{0,1:T(8,128)S(1)}, f32[1024,768]{0,1:T(8,128)}, u32[]{:S(2)}) copy-start(f32[1024,768]{0,1:T(8,128)} %copy-done.19) | copy-start | bytes 9437188
  210.3 63.9 %copy-start.35 = (f32[1024]{0:T(1024)S(1)}, f32[1024]{0:T(1024)}, u32[]{:S(2)}) copy-start(f32[1024]{0:T(1024)} %copy-done.34) | copy-start | bytes 12292
  210.3 63.9 %copy-start.40 = (f32[768]{0:T(1024)S(1)}, f32[768]{0:T(1024)}, u32[]{:S(2)}) copy-start(f32[768]{0:T(1024)} %copy-done.39) | copy-start | bytes 9220
  210.3 63.9 %copy-start.45 = (f32[1024]{0:T(1024)S(1)}, f32[1024]{0:T(1024)}, u32[]{:S(2)}) copy-start(f32[1024]{0:T(1024)} %copy-done.44) | copy-start | bytes 12292
  274.1 4.5 copy-start.4
  279.8 4.8 copy-start.24
  320.2 3.8 copy-start.29
  335.2 63.8 %reduce-scatter.20.cloned.1.call-start = ((), (), s32[]{:S(2)}) async-start(), calls=%async_computation.10 | async-start | bytes 7077888
  345.8 57.5 %reduce-scatter.18.cloned.1.call-start = ((), (), s32[]{:S(2)}) async-start(), calls=%async_computation.9 | async-start | bytes 8847360
  351.4 9.5 %copy-start.28 = (bf16[2048,1536]{1,0:T(8,128)(2,1)}, bf16[2048,1536]{1,0:T(8,128)(2,1)S(1)}, u32[]{:S(2)}) copy-start(bf16[2048,1536]{1,0:T(8,128)(2,1)S(1)} %constant_dynamic-update-slice_fusion.3) | copy-start | bytes 18874372
  351.4 4.6 copy-start.25
  378.5 31.9 %reduce-scatter.14.cloned.1.call-start = ((), (), s32[]{:S(2)}) async-start(), calls=%async_computation.7 | async-start | bytes 7077888 | tf_op jit(solution)/shard_map/reduce_scatter | solution.py:424
  387.7 92.0 %reduce-scatter.22.cloned.1.call-start = ((), (), s32[]{:S(2)}) async-start(), calls=%async_computation.11 | async-start | bytes 294912
  387.7 5.2 copy-start.6
  387.7 5.5 copy-start.18
  390.2 3.7 copy-start.52
  390.2 3.7 copy-start.42
  390.2 3.7 copy-start.62
  390.2 3.7 copy-start.51
  390.2 3.7 copy-start.61
  390.2 3.7 copy-start.50
  395.1 320.0 %all-reduce.3.cloned.1.call-start = ((), (), s32[]{:S(2)}) async-start(), calls=%async_computation.12 | async-start | bytes 18874368 | tf_op jit(solution)/shard_map/psum | solution.py:427
  470.5 91.0 %copy-start.33 = (f32[384,17]{0,1:T(8,128)S(1)}, f32[384,17]{0,1:T(8,128)}, u32[]{:S(2)}) copy-start(f32[384,17]{0,1:T(8,128)} %param.19) | copy-start | bytes 78340
  470.5 91.0 %copy-start.36 = (f32[384,17]{0,1:T(8,128)S(1)}, f32[384,17]{0,1:T(8,128)}, u32[]{:S(2)}) copy-start(f32[384,17]{0,1:T(8,128)} %param.22) | copy-start | bytes 78340
  470.5 91.0 %copy-start.37 = (f32[384,17]{0,1:T(8,128)S(1)}, f32[384,17]{0,1:T(8,128)}, u32[]{:S(2)}) copy-start(f32[384,17]{0,1:T(8,128)} %param.25) | copy-start | bytes 78340
  (23 other events, 47.7 us)
Sparse Core Ops, SparseCore 0:
  16.5 29.1 all-gather.2
  47.8 15.6 all-gather.4
  335.3 12.5 reduce-scatter.15
  350.7 13.7 reduce-scatter.19
  378.6 15.0 reduce-scatter.17
  396.5 13.8 reduce-scatter.13
  413.2 8.7 reduce-scatter.21
  430.1 284.9 all-reduce.2

commit v2 on v1

--- a/solution.py
+++ b/solution.py
@@ -27,37 +27,6 @@
 masked_score = -1e30
 FACTOR = HD ** (-0.5)
 SCALE2 = FACTOR / math.log(2.0)
-
-
-def matmul(left, right):
-    return jnp.dot(left, right, preferred_element_type=jnp.float32)
-
-
-def matmul_left(left, right):
-    return lax.dot_general(
-        left, right, (((0,), (0,)), ((), ())), preferred_element_type=jnp.float32
-    )
-
-
-def matmul_right(left, right):
-    return lax.dot_general(
-        left, right, (((1,), (1,)), ((), ())), preferred_element_type=jnp.float32
-    )
-
-
-def norm_forward(resid, gain, shift):
-    average = jnp.mean(resid, axis=-1, keepdims=True)
-    centred = resid - average
-    inverse = lax.rsqrt(jnp.mean(centred * centred, axis=-1, keepdims=True) + eps_norm)
-    normed = centred * inverse
-    return (normed * gain + shift, normed, inverse)
-
-
-def norm_backward(upstream, normed, inverse, gain):
-    scaled = upstream * gain
-    centred = scaled - jnp.mean(scaled, axis=-1, keepdims=True)
-    resid_grad = inverse * (centred - normed * jnp.mean(scaled * normed, axis=-1, keepdims=True))
-    return (resid_grad, jnp.sum(upstream * normed, axis=0), jnp.sum(upstream, axis=0))
 
 
 def head_masks(rows):
@@ -301,6 +270,438 @@
     )(block_table, queries, keys_in, values_in, mixed_grad, mixed, lse)
 
 
+ROWS = 256
+
+
+def gelu_pair(x):
+    magnitude = jnp.abs(x)
+    bell = jnp.exp2((x * x) * (-0.5 / math.log(2.0)))
+    t = 1.0 / (1.0 + (0.3275911 * math.sqrt(0.5)) * magnitude)
+    poly = t * (0.127414796 + t * (-0.142248368 + t * (0.7107068705 + t * (-0.7265760135 + t * 0.5307027145))))
+    tail = poly * bell
+    phi_sum = jnp.where(x >= 0.0, 1.0 - tail, tail)
+    return x * phi_sum, phi_sum + x * (bell * (1.0 / math.sqrt(2.0 * math.pi)))
+
+
+def unit_rows(resid):
+    average = jnp.mean(resid, axis=-1, keepdims=True)
+    centred = resid - average
+    inverse = lax.rsqrt(jnp.mean(centred * centred, axis=-1, keepdims=True) + eps_norm)
+    return centred * inverse, inverse
+
+
+def back_rows(upstream, unit, inverse, gain):
+    scaled = upstream * gain
+    centred = scaled - jnp.mean(scaled, axis=-1, keepdims=True)
+    return inverse * (centred - unit * jnp.mean(scaled * unit, axis=-1, keepdims=True))
+
+
+def column_dot(left, right):
+    return lax.dot_general(left, right, (((0,), (0,)), ((), ())), preferred_element_type=jnp.float32)
+
+
+def row_total(value):
+    return jnp.sum(value, axis=0, keepdims=True)
+
+
+def center_kernel(
+    factor, mix_ref, one_ref, cot_ref, co_ref, win_ref, wout_ref, vec_ref,
+    out_ref, two_ref, gmix_ref, tw_ref, tn_ref, tc_ref, sums_ref,
+    low_ref, unit_ref, inv_ref, res_ref, act_ref, slope_ref, acc_ref, gffn_ref, bh_ref, gcross_ref,
+):
+    step = pl.program_id(0)
+    rows = mix_ref.shape[0]
+    blocks = rows // ROWS
+
+    def vec(i):
+        return vec_ref[i : i + 1, :]
+
+    def each(body):
+        def run(r, carry):
+            body(pl.ds(pl.multiple_of(r * ROWS, ROWS), ROWS))
+            return carry
+
+        lax.fori_loop(0, blocks, run, 0)
+
+    @pl.when(step == 0)
+    def _():
+        sums_ref[...] = jnp.zeros_like(sums_ref)
+
+        def body(at):
+            resid = one_ref[at, :] + rows_dot(mix_ref[at, :], co_ref[...]) + vec(5)
+            unit, inverse = unit_rows(resid)
+            unit_ref[at, :] = unit
+            inv_ref[at, :] = jnp.broadcast_to(inverse, (ROWS, 128))
+            normed = unit * vec(12) + vec(15)
+            res_ref[at, :] = normed + vec(10)
+            low_ref[at, :] = normed.astype(jnp.bfloat16)
+
+        each(body)
+
+    @pl.when(step < 4)
+    def _():
+        bias = vec_ref[pl.ds(6 + step, 1), :]
+
+        def body(at):
+            hidden = rows_dot(low_ref[at, :], win_ref[...]) + bias
+            value, slope = gelu_pair(hidden)
+            value = value.astype(jnp.bfloat16)
+            act_ref[step, at, :] = value
+            slope_ref[step, at, :] = slope.astype(jnp.bfloat16)
+            res_ref[at, :] += rows_dot(value, wout_ref[...])
+
+        each(body)
+
+    @pl.when(step == 3)
+    def _():
+        def body(at):
+            unit, inverse = unit_rows(res_ref[at, :])
+            out_ref[at, :] = (unit * vec(13) + vec(16)).astype(jnp.bfloat16)
+            upstream = cot_ref[at, :].astype(jnp.float32)
+            grad = back_rows(upstream, unit, inverse, vec(13))
+            acc_ref[at, :] = grad
+            low = grad.astype(jnp.bfloat16)
+            gffn_ref[at, :] = low
+            sums_ref[13:14, :] += row_total(upstream * unit)
+            sums_ref[16:17, :] += row_total(upstream)
+            sums_ref[10:11, :] += row_total(low.astype(jnp.float32))
+
+        each(body)
+
+    @pl.when(step >= 4)
+    def _():
+        c = step - 4
+
+        def body(at):
+            grad = rows_dot_t(gffn_ref[at, :], wout_ref[...]) * slope_ref[c, at, :].astype(jnp.float32)
+            low = grad.astype(jnp.bfloat16)
+            bh_ref[at, :] = low
+            sums_ref[pl.ds(step + 2, 1), :] += row_total(low.astype(jnp.float32))
+            acc_ref[at, :] += rows_dot_t(low, win_ref[...])
+
+        each(body)
+        tn_ref[...] = (column_dot(act_ref[c], gffn_ref[...]) * factor).astype(jnp.bfloat16)
+        rows_each = tw_ref.shape[1]
+        for s in range(tw_ref.shape[0]):
+            cols = slice(s * rows_each, (s + 1) * rows_each)
+            tw_ref[s] = (column_dot(low_ref[:, cols], bh_ref[...]) * factor).astype(jnp.bfloat16)
+
+    @pl.when(step == 7)
+    def _():
+        def body(at):
+            upstream = acc_ref[at, :]
+            unit = unit_ref[at, :]
+            inverse = inv_ref[at, 0:1]
+            grad = back_rows(upstream, unit, inverse, vec(12))
+            two_ref[at, :] = grad
+            low = grad.astype(jnp.bfloat16)
+            gcross_ref[at, :] = low
+            gmix_ref[at, :] = rows_dot_t(low, co_ref[...]).astype(jnp.bfloat16)
+            sums_ref[12:13, :] += row_total(upstream * unit)
+            sums_ref[15:16, :] += row_total(upstream)
+            sums_ref[5:6, :] += row_total(low.astype(jnp.float32))
+
+        each(body)
+        tc_ref[...] = (column_dot(mix_ref[...], gcross_ref[...]) * factor).astype(jnp.bfloat16)
+
+
+def center(mixed, one, cotangent, wide_full, narrow_full, vec_rows, factor, shards):
+    rows = mixed.shape[0]
+    whole = pl.BlockSpec((rows, D), lambda i: (0, 0))
+    rows_each = D // shards
+    bf16, f32 = jnp.bfloat16, jnp.float32
+    return pl.pallas_call(
+        partial(center_kernel, factor),
+        grid=(8,),
+        in_specs=[
+            whole,
+            whole,
+            whole,
+            pl.BlockSpec((D, D), lambda i: (0, 7)),
+            pl.BlockSpec((D, D), lambda i: (0, 8 + i % 4)),
+            pl.BlockSpec((D, D), lambda i: (i % 4, 0)),
+            pl.BlockSpec(vec_rows.shape, lambda i: (0, 0)),
+        ],
+        out_specs=[
+            whole,
+            whole,
+            whole,
+            pl.BlockSpec((shards, rows_each, D), lambda i: (0, jnp.maximum(i - 4, 0), 0)),
+            pl.BlockSpec((D, D), lambda i: (jnp.maximum(i - 4, 0), 0)),
+            pl.BlockSpec((D, D), lambda i: (0, 0)),
+            pl.BlockSpec((24, D), lambda i: (0, 0)),
+        ],
+        out_shape=[
+            jax.ShapeDtypeStruct((rows, D), bf16),
+            jax.ShapeDtypeStruct((rows, D), f32),
+            jax.ShapeDtypeStruct((rows, D), bf16),
+            jax.ShapeDtypeStruct((shards, 4 * rows_each, D), bf16),
+            jax.ShapeDtypeStruct((FF, D), bf16),
+            jax.ShapeDtypeStruct((D, D), bf16),
+            jax.ShapeDtypeStruct((24, D), f32),
+        ],
+        scratch_shapes=[
+            pltpu.VMEM((rows, D), bf16),
+            pltpu.VMEM((rows, D), f32),
+            pltpu.VMEM((rows, 128), f32),
+            pltpu.VMEM((rows, D), f32),
+            pltpu.VMEM((4, rows, D), bf16),
+            pltpu.VMEM((4, rows, D), bf16),
+            pltpu.VMEM((rows, D), f32),
+            pltpu.VMEM((rows, D), bf16),
+            pltpu.VMEM((rows, D), bf16),
+            pltpu.VMEM((rows, D), bf16),
+        ],
+        compiler_params=pltpu.CompilerParams(vmem_limit_bytes=58 << 20),
+        cost_estimate=pl.CostEstimate(flops=54 * rows * D * D, bytes_accessed=30 << 20, transcendentals=0),
+    )(mixed, one, cotangent, wide_full, wide_full, narrow_full, vec_rows)
+
+
+MESH_ID = pl.DeviceIdType.MESH
+
+
+def peers_of(lanes):
+    rep, shard = lax.axis_index("rep"), lax.axis_index("shard")
+    x, y, z = rep % 2, (rep // 2) % 2, rep // 4
+    base = rep - z * 4
+    others = [(base + 4 * ((z + k) % lanes), shard) for k in range(1, lanes)]
+    first = rep + 1 - 2 * x
+    second = rep + 2 - 4 * y
+    return rep, shard, x, y, z, (rep, 1 - shard), (first, shard), (second, shard), others
+
+
+def enter_barrier(lanes):
+    _, _, _, _, _, sibling, first, second, others = peers_of(lanes)
+    barrier = pltpu.get_barrier_semaphore()
+    for peer in [sibling, first, second] + others:
+        pl.semaphore_signal(barrier, inc=1, device_id=peer, device_id_type=MESH_ID)
+    pl.semaphore_wait(barrier, 2 + lanes)
+
+
+def aligned(value):
+    return pl.multiple_of(value, 16)
+
+
+def bulk_scratch(rows, lanes):
+    block = rows // (4 * lanes)
+    bf16 = jnp.bfloat16
+    return [
+        pltpu.VMEM((rows, D), bf16),
+        pltpu.VMEM((rows, D), bf16),
+        pltpu.VMEM((rows // 2, D), bf16),
+        pltpu.VMEM((rows // 4, D), bf16),
+        pltpu.VMEM((lanes, block, D), bf16),
+        pltpu.SemaphoreType.DMA((5 + 2 * lanes,)),
+        pltpu.SemaphoreType.DMA((5 + 2 * lanes,)),
+        pltpu.SemaphoreType.DMA((2,)),
+    ]
+
+
+def bulk_steps(term_ref, sum_ref, scratch, x_first, lanes):
+    acc, got_core, got_a, got_b, got_z, send_sem, recv_sem, local_sem = scratch
+    full = got_core
+    rows = acc.shape[0]
+    half, quarter, block = rows // 2, rows // 4, rows // (4 * lanes)
+    rep, shard, x, y, z, sibling, peer_x, peer_y, others = peers_of(lanes)
+    here_a, here_b = (x, y) if x_first else (y, x)
+    peer_a, peer_b = (peer_x, peer_y) if x_first else (peer_y, peer_x)
+    mine_a = aligned(here_a * half)
+    theirs_a = aligned((1 - here_a) * half)
+    mine_b = aligned(here_a * half + here_b * quarter)
+    theirs_b = aligned(here_a * half + (1 - here_b) * quarter)
+    mine_z = aligned(mine_b + z * block)
+
+    def remote(index, source, target, peer):
+        return pltpu.make_async_remote_copy(
+            src_ref=source,
+            dst_ref=target,
+            send_sem=send_sem.at[index],
+            recv_sem=recv_sem.at[index],
+            device_id=peer,
+            device_id_type=MESH_ID,
+        )
+
+    core = remote(0, term_ref.at[1 - shard], got_core, sibling)
+    load = pltpu.make_async_copy(term_ref.at[shard], acc, local_sem.at[0])
+    to_a = remote(1, acc.at[pl.ds(theirs_a, half)], got_a, peer_a)
+    to_b = remote(2, acc.at[pl.ds(theirs_b, quarter)], got_b, peer_b)
+    to_z, all_z = [], []
+    for k, peer in enumerate(others):
+        theirs = aligned(mine_b + ((z + k + 1) % lanes) * block)
+        to_z.append(remote(5 + k, acc.at[pl.ds(theirs, block)], got_z.at[z], peer))
+        all_z.append(
+            remote(5 + lanes + k, full.at[pl.ds(mine_z, block)], full.at[pl.ds(mine_z, block)], peer)
+        )
+    all_b = remote(3, full.at[pl.ds(mine_b, quarter)], full.at[pl.ds(mine_b, quarter)], peer_b)
+    all_a = remote(4, full.at[pl.ds(mine_a, half)], full.at[pl.ds(mine_a, half)], peer_a)
+    store = pltpu.make_async_copy(full, sum_ref, local_sem.at[1])
+
+    def add(start, count, got):
+        def body(i, carry):
+            there = pl.ds(aligned(start + i * block), block)
+            total = acc[there, :].astype(jnp.float32) + got[pl.ds(aligned(i * block), block), :].astype(
+                jnp.float32
+            )
+            acc[there, :] = total.astype(jnp.bfloat16)
+            return carry
+
+        lax.fori_loop(0, count // block, body, 0)
+
+    def step_core():
+        core.start()
+        load.start()
+
+    def step_a():
+        load.wait()
+        core.wait()
+        add(0, rows, got_core)
+        to_a.start()
+
+    def step_b():
+        to_a.wait()
+        add(mine_a, half, got_a)
+        to_b.start()
+
+    def step_z():
+        to_b.wait()
+        add(mine_b, quarter, got_b)
+        for copy in to_z:
+            copy.start()
+
+    def step_gather_z():
+        for copy in to_z:
+            copy.wait()
+        there = pl.ds(mine_z, block)
+        total = acc[there, :].astype(jnp.float32)
+        for k in range(1, lanes):
+            total = total + got_z[(z + k) % lanes].astype(jnp.float32)
+        full[there, :] = total.astype(jnp.bfloat16)
+        for copy in all_z:
+            copy.start()
+
+    def step_gather_b():
+        for copy in all_z:
+            copy.wait()
+        all_b.start()
+
+    def step_gather_a():
+        all_b.wait()
+        all_a.start()
+
+    def step_store():
+        all_a.wait()
+        store.start()
+
+    return [
+        step_core, step_a, step_b, step_z, step_gather_z, step_gather_b, step_gather_a, step_store, store.wait,
+    ]
+
+
+def small_scratch(shape, lanes):
+    return [
+        pltpu.VMEM((3,) + shape, jnp.float32),
+        pltpu.VMEM((3,) + shape, jnp.float32),
+        pltpu.VMEM((lanes,) + shape, jnp.float32),
+        pltpu.SemaphoreType.DMA((3 + lanes,)),
+        pltpu.SemaphoreType.DMA((3 + lanes,)),
+    ]
+
+
+def small_steps(term_ref, sum_ref, scratch, lanes):
+    held, got, got_z, send_sem, recv_sem = scratch
+    rep, shard, x, y, z, sibling, peer_x, peer_y, others = peers_of(lanes)
+
+    def remote(index, source, target, peer):
+        return pltpu.make_async_remote_copy(
+            src_ref=source,
+            dst_ref=target,
+            send_sem=send_sem.at[index],
+            recv_sem=recv_sem.at[index],
+            device_id=peer,
+            device_id_type=MESH_ID,
+        )
+
+    core = remote(0, term_ref.at[1 - shard], got.at[0], sibling)
+    to_x = remote(1, held.at[0], got.at[1], peer_x)
+    to_y = remote(2, held.at[1], got.at[2], peer_y)
+    to_z = [remote(3 + k, held.at[2], got_z.at[z], peer) for k, peer in enumerate(others)]
+
+    def step_x():
+        core.wait()
+        held[0] = term_ref[shard] + got[0]
+        to_x.start()
+
+    def step_y():
+        to_x.wait()
+        held[1] = held[0] + got[1]
+        to_y.start()
+
+    def step_z():
+        to_y.wait()
+        held[2] = held[1] + got[2]
+        got_z[z] = held[2]
+        for copy in to_z:
+            copy.start()
+
+    def step_end():
+        for copy in to_z:
+            copy.wait()
+        total = got_z[0]
+        for k in range(1, lanes):
+            total = total + got_z[k]
+        sum_ref[...] = total
+
+    return [core.start, step_x, step_y, step_z, step_end]
+
+
+def interleave(plans):
+    last = max(begin + len(steps) for begin, steps in plans)
+    for tick in range(last):
+        for begin, steps in plans:
+            if 0 <= tick - begin < len(steps):
+                steps[tick - begin]()
+
+
+def reduce_kernel(lanes, count, *refs):
+    terms, small_term = refs[:count], refs[count]
+    sums, small_sum = refs[count + 1], refs[count + 2]
+    scratch = refs[count + 3 :]
+    enter_barrier(lanes)
+    plans = []
+    at = 0
+    for i, term in enumerate(terms):
+        rows = term.shape[1]
+        plans.append(
+            (i // 2, bulk_steps(term, sums.at[pl.ds(at, rows)], scratch[8 * i : 8 * i + 8], i % 2 == 0, lanes))
+        )
+        at += rows
+    plans.append((0, small_steps(small_term, small_sum, scratch[8 * count :], lanes)))
+    interleave(plans)
+
+
+def reduce_all(terms, small, lanes):
+    any_spec, vmem_spec = pl.BlockSpec(memory_space=pl.ANY), pl.BlockSpec(memory_space=pltpu.VMEM)
+    count = len(terms)
+    total = sum(term.shape[1] for term in terms)
+    scratch = []
+    for term in terms:
+        scratch += bulk_scratch(term.shape[1], lanes)
+    scratch += small_scratch(small.shape[1:], lanes)
+    return pl.pallas_call(
+        partial(reduce_kernel, lanes, count),
+        in_specs=[any_spec] * count + [vmem_spec],
+        out_specs=[any_spec, vmem_spec],
+        out_shape=[
+            jax.ShapeDtypeStruct((total, D), jnp.bfloat16),
+            jax.ShapeDtypeStruct(small.shape[1:], jnp.float32),
+        ],
+        scratch_shapes=scratch,
+        compiler_params=pltpu.CompilerParams(
+            collective_id=0, has_side_effects=True, vmem_limit_bytes=56 << 20
+        ),
+    )(*terms, small)
+
+
 def adam_update(master, first, second, gradient, decay_on, rate):
     first_new = beta_one * first + (1.0 - beta_one) * gradient
     second_new = beta_two * second + (1.0 - beta_two) * gradient * gradient
@@ -308,6 +709,94 @@
     second_hat = second_new / (1.0 - beta_two**STEP)
     master_new = master - rate * (first_hat / (jnp.sqrt(second_hat) + eps_adam) + decay_on * master)
     return (master_new, first_new, second_new)
+
+
+def wide_column(i):
+    return jnp.where(i < 4, i + 8, jnp.where(i < 8, 11, jnp.where(i < 12, i - 4, i - 12)))
+
+
+def narrow_row(i):
+    return jnp.clip(i - 4, 0, 3)
+
+
+def adam_kernel(sum_ref, wm, wf, ws, nm, nf, ns, wg, wn, wfn, wsn, wc, ng, nn, nfn, nsn, nc):
+    step = pl.program_id(0)
+
+    def update(master, first, second, grad, new, first_new, second_new, copy):
+        def body(r, carry):
+            at = pl.ds(pl.multiple_of(r * 32, 32), 32)
+            gradient = sum_ref[at, :].astype(jnp.float32)
+            grad[at, :] = gradient
+            value, one, two = adam_update(
+                master[at, :], first[at, :], second[at, :], gradient, weight_decay, learn_rate
+            )
+            new[at, :] = value
+            first_new[at, :] = one
+            second_new[at, :] = two
+            copy[at, :] = value.astype(jnp.bfloat16)
+            return carry
+
+        lax.fori_loop(0, sum_ref.shape[0] // 32, body, 0, unroll=True)
+
+    narrow_step = (step >= 4) & (step < 8)
+
+    @pl.when(jnp.logical_not(narrow_step))
+    def _():
+        update(wm, wf, ws, wg, wn, wfn, wsn, wc)
+
+    @pl.when(narrow_step)
+    def _():
+        update(nm, nf, ns, ng, nn, nfn, nsn, nc)
+
+
+def adam_all(sums, wide, narrow):
+    rows = wide[0].shape[0]
+    spec_w = pl.BlockSpec((rows, D), lambda i: (0, wide_column(i)))
+    spec_n = pl.BlockSpec((rows, D), lambda i: (narrow_row(i), 0))
+    f32, bf16 = jnp.float32, jnp.bfloat16
+
+    def shapes(like):
+        return [jax.ShapeDtypeStruct(like.shape, f32)] * 4 + [jax.ShapeDtypeStruct(like.shape, bf16)]
+
+    return pl.pallas_call(
+        adam_kernel,
+        grid=(16,),
+        in_specs=[pl.BlockSpec((rows, D), lambda i: (i, 0))] + [spec_w] * 3 + [spec_n] * 3,
+        out_specs=[spec_w] * 5 + [spec_n] * 5,
+        out_shape=shapes(wide[0]) + shapes(narrow[0]),
+        compiler_params=pltpu.CompilerParams(vmem_limit_bytes=58 << 20),
+    )(sums, *wide, *narrow)
+
+
+def matmul(left, right):
+    return jnp.dot(left, right, preferred_element_type=jnp.float32)
+
+
+def matmul_left(left, right):
+    return lax.dot_general(
+        left, right, (((0,), (0,)), ((), ())), preferred_element_type=jnp.float32
+    )
+
+
+def matmul_right(left, right):
+    return lax.dot_general(
+        left, right, (((1,), (1,)), ((), ())), preferred_element_type=jnp.float32
+    )
+
+
+def norm_forward(resid, gain, shift):
+    average = jnp.mean(resid, axis=-1, keepdims=True)
+    centred = resid - average
+    inverse = lax.rsqrt(jnp.mean(centred * centred, axis=-1, keepdims=True) + eps_norm)
+    normed = centred * inverse
+    return (normed * gain + shift, normed, inverse)
+
+
+def norm_backward(upstream, normed, inverse, gain):
+    scaled = upstream * gain
+    centred = scaled - jnp.mean(scaled, axis=-1, keepdims=True)
+    resid_grad = inverse * (centred - normed * jnp.mean(scaled * normed, axis=-1, keepdims=True))
+    return (resid_grad, jnp.sum(upstream * normed, axis=0), jnp.sum(upstream, axis=0))
 
 
 def column_sum(matrix):
@@ -332,125 +821,90 @@
     replicas = lax.axis_size("rep")
     shards = lax.axis_size("shard")
     tokens_all = tokens.shape[0] * replicas * shards
-
-    copies = (
-        wide_master.astype(jnp.bfloat16),
-        narrow_master.astype(jnp.bfloat16),
-        vec_master.astype(jnp.bfloat16),
-    )
-    wide_full, narrow_full, vec_full = (
-        lax.all_gather(copies[0], "shard", axis=0, tiled=True),
-        lax.all_gather(copies[1], "shard", axis=0, tiled=True),
-        lax.all_gather(copies[2], "shard", axis=0, tiled=True),
-    )
-    vector = vec_full.astype(jnp.float32)
-    ffn_bias = vector[:, 6:10].T.reshape(FF)
+    factor = float(tokens_all) ** (-0.5)
+    bf16, f32 = jnp.bfloat16, jnp.float32
+
+    def gathered(part):
+        return lax.all_gather(part.astype(bf16), "shard", axis=0, tiled=True)
+
+    wide_full = gathered(wide_master)
+    narrow_full = gathered(narrow_master)
+    vector = gathered(vec_master).astype(f32)
+    vec_rows = jnp.pad(vector.T, ((0, 24 - vector.shape[1]), (0, 0)))
     joint_proj = matmul(tokens, wide_full[:, : 3 * D])
-    queries = (joint_proj[:, :D] + vector[:, 0]).astype(jnp.bfloat16)
-    keys_self = joint_proj[:, D : 2 * D].astype(jnp.bfloat16)
-    values_self = (joint_proj[:, 2 * D :] + vector[:, 1]).astype(jnp.bfloat16)
+    queries = (joint_proj[:, :D] + vector[:, 0]).astype(bf16)
+    keys_self = joint_proj[:, D : 2 * D].astype(bf16)
+    values_self = (joint_proj[:, 2 * D :] + vector[:, 1]).astype(bf16)
     mixed_self, totals_self = attend_forward(queries, keys_self, values_self, block_mask, True)
     branch_one = matmul(mixed_self, wide_full[:, 3 * D : 4 * D]) + vector[:, 2]
     normed_one, unit_one, scale_one = norm_forward(
-        tokens.astype(jnp.float32) + branch_one, vector[:, 11], vector[:, 14]
-    )
-    normed_low = normed_one.astype(jnp.bfloat16)
-    cross_queries = (matmul(normed_low, wide_full[:, 4 * D : 5 * D]) + vector[:, 3]).astype(
-        jnp.bfloat16
-    )
+        tokens.astype(f32) + branch_one, vector[:, 11], vector[:, 14]
+    )
+    normed_low = normed_one.astype(bf16)
+    cross_queries = (matmul(normed_low, wide_full[:, 4 * D : 5 * D]) + vector[:, 3]).astype(bf16)
     enc_proj = matmul(encoder_states, wide_full[:, 5 * D : 7 * D])
-    cross_keys = enc_proj[:, :D].astype(jnp.bfloat16)
-    cross_values = (enc_proj[:, D:] + vector[:, 4]).astype(jnp.bfloat16)
-
+    cross_keys = enc_proj[:, :D].astype(bf16)
+    cross_values = (enc_proj[:, D:] + vector[:, 4]).astype(bf16)
     mixed_cross, totals_cross = attend_forward(
         cross_queries, cross_keys, cross_values, block_mask, False
     )
-    branch_two = matmul(mixed_cross, wide_full[:, 7 * D : 8 * D]) + vector[:, 5]
-    normed_two, unit_two, scale_two = norm_forward(
-        normed_one + branch_two, vector[:, 12], vector[:, 15]
-    )
-    second_low = normed_two.astype(jnp.bfloat16)
-    hidden = matmul(second_low, wide_full[:, 8 * D :]) + ffn_bias
-    active_full, gelu_pull = jax.vjp(partial(jax.nn.gelu, approximate=False), hidden)
-    active = active_full.astype(jnp.bfloat16)
-    branch_three = matmul(active, narrow_full) + vector[:, 10]
-    final_out, unit_three, scale_three = norm_forward(
-        normed_two + branch_three, vector[:, 13], vector[:, 16]
-    )
-    output = final_out.astype(jnp.bfloat16)
-    grad_three, gain_three, shift_three = norm_backward(
-        cotangent.astype(jnp.float32), unit_three, scale_three, vector[:, 13]
-    )
-    grad_ffn = grad_three.astype(jnp.bfloat16)
-    grad_narrow = matmul_left(active, grad_ffn)
-    grad_hidden = gelu_pull(matmul_right(grad_ffn, narrow_full))[0].astype(jnp.bfloat16)
-    grad_ffn_in = matmul_left(second_low, grad_hidden)
-    grad_two, gain_two, shift_two = norm_backward(
-        grad_three + matmul_right(grad_hidden, wide_full[:, 8 * D :]),
-        unit_two,
-        scale_two,
-        vector[:, 12],
-    )
-    grad_cross = grad_two.astype(jnp.bfloat16)
-    grad_cross_out = matmul_left(mixed_cross, grad_cross)
-    grad_cross_mix = matmul_right(grad_cross, wide_full[:, 7 * D : 8 * D]).astype(jnp.bfloat16)
-
-    grad_cross_queries, grad_cross_keys, grad_cross_values = attend_backward(
+    output, grad_two, grad_cross_mix, term_in, term_narrow, term_co, sums = center(
+        mixed_cross, normed_one, cotangent, wide_full, narrow_full, vec_rows, factor, shards
+    )
+    grad_cq, grad_ck, grad_cv = attend_backward(
         cross_queries, cross_keys, cross_values, block_mask, False, mixed_cross, totals_cross, grad_cross_mix
     )
-    grad_enc_proj = jnp.concatenate([grad_cross_keys, grad_cross_values], 1)
-    grad_cross_query = matmul_left(normed_low, grad_cross_queries)
-    grad_cross_pair = matmul_left(encoder_states, grad_enc_proj)
-    enc_grad = matmul_right(grad_enc_proj, wide_full[:, 5 * D : 7 * D]).astype(jnp.bfloat16)
+
+    def split(term):
+        return term.reshape(shards, -1, D)
+
+    def units(*pairs):
+        return jnp.concatenate(
+            [split((matmul_left(left, right) * factor).astype(bf16)) for left, right in pairs], 1
+        )
+
+    terms = [term_in, split(term_narrow)]
+    terms.append(units((normed_low, grad_cq), (encoder_states, grad_ck)))
+    terms.append(jnp.concatenate([units((encoder_states, grad_cv)), split(term_co)], 1))
+    enc_grad = (
+        matmul_right(grad_ck, wide_full[:, 5 * D : 6 * D]) + matmul_right(grad_cv, wide_full[:, 6 * D : 7 * D])
+    ).astype(bf16)
     grad_one, gain_one, shift_one = norm_backward(
-        grad_two + matmul_right(grad_cross_queries, wide_full[:, 4 * D : 5 * D]),
-        unit_one,
-        scale_one,
-        vector[:, 11],
-    )
-    grad_self = grad_one.astype(jnp.bfloat16)
-    grad_self_out = matmul_left(mixed_self, grad_self)
-    grad_self_mix = matmul_right(grad_self, wide_full[:, 3 * D : 4 * D]).astype(jnp.bfloat16)
-
-    grad_queries, grad_keys, grad_values = attend_backward(
+        grad_two + matmul_right(grad_cq, wide_full[:, 4 * D : 5 * D]), unit_one, scale_one, vector[:, 11]
+    )
+    grad_self = grad_one.astype(bf16)
+    grad_self_mix = matmul_right(grad_self, wide_full[:, 3 * D : 4 * D]).astype(bf16)
+    grad_q, grad_k, grad_v = attend_backward(
         queries, keys_self, values_self, block_mask, True, mixed_self, totals_self, grad_self_mix
     )
-    grad_joint_proj = jnp.concatenate([grad_queries, grad_keys, grad_values], 1)
-    grad_joint = matmul_left(tokens, grad_joint_proj)
-    in_grad = (grad_one + matmul_right(grad_joint_proj, wide_full[:, : 3 * D])).astype(jnp.bfloat16)
-    factor = float(tokens_all) ** (-0.5)
-
-    def summed(term):
-        owned = lax.psum_scatter(
-            (term * factor).astype(jnp.bfloat16), "shard", scatter_dimension=0, tiled=True
-        )
-        return lax.psum(owned, "rep").astype(jnp.float32)
-
-    ffn_sum = summed(grad_ffn_in)
-    narrow_grad = summed(grad_narrow)
-    cross_sum = summed(jnp.concatenate([grad_self_out, grad_cross_query, grad_cross_pair, grad_cross_out], 1))
-    joint_sum = summed(grad_joint)
-    wide_grad = jnp.concatenate([joint_sum, cross_sum, ffn_sum], 1)
-    bias_front = jnp.stack(
-        [
-            column_sum(grad_joint_proj[:, :D]),
-            column_sum(grad_joint_proj[:, 2 * D :]),
-            column_sum(grad_self),
-            column_sum(grad_cross_queries),
-            column_sum(grad_enc_proj[:, D:]),
-            column_sum(grad_cross),
-        ],
-        1,
-    )
-    bias_back = jnp.stack(
-        [column_sum(grad_ffn), gain_one, gain_two, gain_three, shift_one, shift_two, shift_three], 1
-    )
-    vec_grad = summed(jnp.concatenate([bias_front, column_sum(grad_hidden).reshape(4, D).T, bias_back], 1))
-    wide_new, wide_first_new, wide_second_new = adam_update(
-        wide_master, wide_first, wide_second, wide_grad, weight_decay, learn_rate
-    )
-    narrow_new, narrow_first_new, narrow_second_new = adam_update(
-        narrow_master, narrow_first, narrow_second, narrow_grad, weight_decay, learn_rate
+    terms.append(units((tokens, grad_q), (tokens, grad_k)))
+    terms.append(units((tokens, grad_v), (mixed_self, grad_self)))
+    in_grad = (
+        grad_one
+        + matmul_right(grad_q, wide_full[:, :D])
+        + matmul_right(grad_k, wide_full[:, D : 2 * D])
+        + matmul_right(grad_v, wide_full[:, 2 * D : 3 * D])
+    ).astype(bf16)
+    fresh = jnp.zeros((24, D), f32)
+    for row, value in (
+        (0, column_sum(grad_q)),
+        (1, column_sum(grad_v)),
+        (2, column_sum(grad_self)),
+        (3, column_sum(grad_cq)),
+        (4, column_sum(grad_cv)),
+        (11, gain_one),
+        (14, shift_one),
+    ):
+        fresh = fresh.at[row].set(value)
+    term_vec = (sums + fresh) * factor
+    term_vec = term_vec.reshape(24, shards, -1).transpose(1, 0, 2)
+    total, vec_sum = all_summed(terms, term_vec, replicas, shards)
+    vec_grad = vec_sum[: vec_master.shape[1]].T
+    (
+        wide_grad, wide_new, wide_first_new, wide_second_new, wide_copy,
+        narrow_grad, narrow_new, narrow_first_new, narrow_second_new, narrow_copy,
+    ) = adam_all(
+        total, (wide_master, wide_first, wide_second), (narrow_master, narrow_first, narrow_second)
     )
     vec_new, vec_first_new, vec_second_new = adam_update(
         vec_master, vec_first, vec_second, vec_grad, 0.0, vec_rate
@@ -471,10 +925,21 @@
         wide_second_new,
         narrow_second_new,
         vec_second_new,
-        wide_new.astype(jnp.bfloat16),
-        narrow_new.astype(jnp.bfloat16),
-        vec_new.astype(jnp.bfloat16),
-    )
+        wide_copy,
+        narrow_copy,
+        vec_new.astype(bf16),
+    )
+
+
+def all_summed(terms, small, replicas, shards):
+    lanes = replicas // 4
+    if shards == 2 and replicas % 4 == 0 and all(t.shape[1] % (64 * lanes) == 0 for t in terms):
+        return reduce_all(terms, small, lanes)
+
+    def summed(term):
+        return lax.psum(lax.psum_scatter(term, "shard", scatter_dimension=0), "rep")
+
+    return jnp.concatenate([summed(term) for term in terms], 0), summed(small)
 
 
 def solution(mesh):

time: 861 us -> 629 us (0.73)
  Pallas kernels: 141 us -> 453 us
  local copies, waits for them, and re-layouts: 177 us -> 25.4 us
  waiting for transfers between devices: 172 us -> 22.6 us
  matrix products: 168 us -> 69.3 us
  blocking collectives: 82.7 us -> 1.95 us
  other arithmetic: 95.3 us -> 32.5 us
    pallas_call x0 -> x3, Pallas kernels: none -> 313 us  [the longest x1 194 us: reduce_all(): pl.pallas_call(partial(reduce_kernel, lanes, count), in_specs=[any_spec]...]
    unnamed x148 -> x82, local copies, waits for them, and re-layouts: 173 us -> 9.03 us
    psum x1 -> x0, waiting for transfers between devices: 153 us -> none  [summed(): return lax.psum(owned, 'rep').astype(jnp.float32)]
    psum x1 -> x0, blocking collectives: 80.8 us -> none  [summed(): return lax.psum(owned, 'rep').astype(jnp.float32)]
    dot_general x7 -> x4, matrix products: 72.1 us -> 21.1 us  [matmul(): return jnp.dot(left, right, preferred_element_type=jnp.float32)]
    convert_element_type x11 -> x6, other arithmetic: 68.6 us -> 21.8 us  [the longest x3 13.1 us: gathered(): return lax.all_gather(part.astype(bf16), 'shard', axis=0, tiled=True)]
    dot_general x7, matrix products: 61.4 us -> 26.4 us  [matmul_right(): lax.dot_general(left, right, (((1,), (1,)), ((), ())), preferred_element_...]
    dot_general x7, matrix products: 34.5 us -> 21.7 us  [matmul_left(): lax.dot_general(left, right, (((0,), (0,)), ((), ())), preferred_element_...]
  transfers between devices with their start and end apart: 8 -> 2, of which waited for: 3 -> 1; matrix products, arithmetic and copies ran while one was open for 25% -> 6% of each run, Pallas kernels for 5% -> 7%
where the time goes in v2:
time: 629 us; the launch traced here: 620 us
  Pallas kernels  453 us (72%)
  matrix products  69.3 us (11%)
  other arithmetic  32.5 us (5%)
  local copies, waits for them, and re-layouts  25.4 us (4%)
  waiting for transfers between devices  22.6 us (4%)
  between operations  14.9 us (2%)
    pallas_call x1, Pallas kernels, reduce_all(): pl.pallas_call(partial(reduce_kernel, lanes, count), in_specs=[any_spec]...  194 us
    pallas_call x2, Pallas kernels, attend_backward(): pl.pallas_call(partial(backward_kernel, causal), grid_spec=pltpu.Prefetch...  100 us
    pallas_call x1, Pallas kernels, center(): pl.pallas_call(partial(center_kernel, factor), grid=(8,), in_specs=[whole...  66 us
    pallas_call x1, Pallas kernels, adam_all(): pl.pallas_call(adam_kernel, grid=(16,), in_specs=[pl.BlockSpec((rows, D),...  52.5 us
    pallas_call x2, Pallas kernels, attend_forward(): pl.pallas_call(partial(forward_kernel, causal), grid_spec=pltpu.PrefetchS...  40.7 us
    dot_general x7, matrix products, matmul_right(): lax.dot_general(left, right, (((1,), (1,)), ((), ())), preferred_element_...  26.4 us
    all_gather x2, waiting for transfers between devices, gathered(): return lax.all_gather(part.astype(bf16), 'shard', axis=0, tiled=True)  22.6 us
    dot_general x7, matrix products, matmul_left(): lax.dot_general(left, right, (((0,), (0,)), ((), ())), preferred_element_...  21.7 us
  transfers between devices with their start and end apart: 2, of which 1 were waited for; matrix products, arithmetic and copies ran while one was open for 6% of the time, Pallas kernels for 7%

profile of v2, /device:TPU:0, one launch (start us, length us, event | category | flops | bytes accessed | tf_op | source)
XLA Modules:
  0.0 620.2 jit_solution(11416060662914897221)
XLA Ops:
  7.2 9.1 %convert_element_type.101 = bf16[384,9216]{1,0:T(8,128)(2,1)} convert(f32[384,9216]{1,0:T(8,128)} %wm.1) | non-fusion elementwise | flops 3538944 | bytes 21233664 | tf_op jit(solution)/shard_map/convert_element_type | solution.py:828
  16.5 4.0 convert_element_type.109
  20.5 1.9 all_gather.10
  23.2 22.6 %all-gather.3.cloned.1.call-done.co_ref.win_ref = bf16[768,9216]{1,0:T(8,128)(2,1)} async-done(((bf16[384,9216]{1,0:T(8,128)(2,1)}), bf16[768,9216]{1,0:T(8,128)(2,1)}) %all-gather.3.cloned.1.call-update) | async-done | bytes 14155792 | tf_op jit(solution)/shard_map/all_gather | solution.py:828
  45.7 6.3 %fusion.1 = f32[1024,2304]{1,0:T(8,128)S(1)} fusion(bf16[1024,768]{1,0:T(8,128)(2,1)} %param.27, bf16[768,9216]{1,0:T(8,128)(2,1)} %all-gather.3.cloned.1.call-done.co_ref.win_ref), kind=kOutput, calls=%fused_computation.5 | convolution fusion | flops 3623878656 | bytes 14548992 | tf_op jit(solution)/shard_map/dot_general | solution.py:772
  52.2 1.7 fusion.3
  53.9 12.7 %shard_map.268 = (bf16[1024,768]{1,0:T(8,128)(2,1)S(1)}, f32[1,6,8,1024]{3,2,1,0:T(8,128)S(1)}) custom-call(s32[1,4,4]{2,1,0:T(4,128)S(1)} %copy-done.7, bf16[1024,768]{1,0:T(8,128)(2,1)S(1)} %get-tuple-element.179.q_ref, bf16[1024,768]{1,0:T(8,128)(2,1)S(1)} %slice.260.k_ref, bf16[1024,768]{1,0:T(8,128)(2,1)} %get-tuple-element.178.v_ref), custom_call_target="tpu_custom_call" | custom-call | flops 6442450944 | bytes 3145728 | tf_op jit(solution)/shard_map/pallas_call | solution.py:144
  66.6 7.5 %fusion.5 = f32[2048,1536]{1,0:T(8,128)S(1)} fusion(bf16[2048,768]{1,0:T(8,128)(2,1)S(1)} %copy-done, bf16[768,9216]{1,0:T(8,128)(2,1)} %all-gather.3.cloned.1.call-done.co_ref.win_ref), kind=kOutput, calls=%fused_computation.26 | convolution fusion | flops 4831838208 | bytes 18087936 | tf_op jit(solution)/shard_map/dot_general | solution.py:772
  74.2 3.8 fusion.31
  77.9 1.0 copy-done.20
  78.9 2.3 slice.259.k_ref
  82.3 3.6 add_convert_fusion.2.q_ref
  85.9 5.5 fusion.v_ref
  91.5 28.0 %shard_map.269 = (bf16[1024,768]{1,0:T(8,128)(2,1)S(1)}, f32[1,6,8,1024]{3,2,1,0:T(8,128)S(1)}) custom-call(s32[1,4,4]{2,1,0:T(4,128)S(1)} %copy-done.7, bf16[1024,768]{1,0:T(8,128)(2,1)S(1)} %add_convert_fusion.2.q_ref, bf16[2048,768]{1,0:T(8,128)(2,1)} %slice.259.k_ref, bf16[2048,768]{1,0:T(8,128)(2,1)} %fusion.v_ref), custom_call_target="tpu_custom_call" | custom-call | flops 25769803776 | bytes 3145728 | tf_op jit(solution)/shard_map/pallas_call | solution.py:144
  119.5 1.1 copy-done.14
  120.6 66.0 %shard_map.270 = (bf16[1024,768]{1,0:T(8,128)(2,1)}, f32[1024,768]{1,0:T(8,128)}, bf16[1024,768]{1,0:T(8,128)(2,1)}, bf16[2,1536,768]{2,1,0:T(8,128)(2,1)}, bf16...) custom-call(bf16[1024,768]{1,0:T(8,128)(2,1)} %copy-done.14, f32[1024,768]{1,0:T(8,128)} %copy-done.26, ...), custom_call_target="tpu_custom_call" | custom-call | flops 32614907904 | bytes 31457280 | tf_op jit(solution)/shard_map/pallas_call | solution.py:413
  186.7 1.4 copy-done.15
  188.1 64.1 %shard_map.271 = (bf16[1024,768]{1,0:T(8,128)(2,1)S(1)}, bf16[2048,768]{1,0:T(8,128)(2,1)}, bf16[2048,768]{1,0:T(8,128)(2,1)}) custom-call(s32[1,4,4]{2,1,0:T(4,128)S(1)} %copy-done.7, bf16[1024,768]{1,0:T(8,128)(2,1)S(1)} %copy-done.11, bf16[2048,768]{1,0:T(8,128)(2,1)} %slice.259.k_ref, bf16[2048,768]{1,0:T(8,128)(2,1)} %fusion.v_ref, ...), custom_call_target="tpu_custom_call" | custom-call | flops 64424509440 | bytes 3145728 | tf_op jit(solution)/shard_map/pallas_call | solution.py:243
  252.2 2.5 multiply_convert_fusion.6
  255.5 3.4 multiply_reduce_fusion
  258.9 1.1 convert_reduce_fusion.2
  260.3 2.5 multiply_convert_fusion
  262.8 3.8 convolution_convert_fusion.m_ref
  266.6 35.9 %shard_map.272 = (bf16[1024,768]{1,0:T(8,128)(2,1)S(1)}, bf16[1024,768]{1,0:T(8,128)(2,1)S(1)}, bf16[1024,768]{1,0:T(8,128)(2,1)S(1)}) custom-call(s32[1,4,4]{2,1,0:T(4,128)S(1)} %copy-done.7, bf16[1024,768]{1,0:T(8,128)(2,1)} %copy-done.6, bf16[1024,768]{1,0:T(8,128)(2,1)} %copy-done.5, bf16[1024,768]{1,0:T(8,128)(2,1)} %get-tuple-element.178.v_ref, ...), custom_call_target="tpu_custom_call" | custom-call | flops 16106127360 | bytes 3145728 | tf_op jit(solution)/shard_map/pallas_call | solution.py:243
  302.6 2.5 fusion.9
  305.4 2.5 fusion.11
  308.4 1.3 copy-done.24
  309.8 3.7 fusion.8
  314.0 1.4 copy-done.39
  315.4 3.7 fusion.7
  319.1 2.4 copy.44
  321.5 2.4 copy.46
  323.9 4.3 fusion.10
  328.2 2.4 copy.50
  330.6 2.4 copy.48
  333.0 2.5 copy.52
  336.9 3.2 pad_maximum_fusion.2.refs_4_
  340.1 1.6 pad_maximum_fusion.3.refs_5_
  341.7 0.8 copy-done.22
  343.3 2.3 pad_maximum_fusion
  345.6 194.3 %shard_map.273 = (bf16[6144,768]{1,0:T(8,128)(2,1)}, f32[24,384]{1,0:T(8,128)}) custom-call(bf16[2,1536,768]{2,1,0:T(8,128)(2,1)} %get-tuple-element.144.refs_0_, bf16[2,1536,768]{2,1,0:T(8,128)(2,1)} %bitcast.57, bf16[2,768,768]{2,1,0:T(8,128)(2,1)} %get-tuple-element.187.refs_2_, bf16[2,768,768]{2,1,0:T(8,128)(2,1)} %get-tuple-element.188.refs_3_, ...), custom_call_target="tpu_custom_call" | custom-call | tf_op jit(solution)/shard_map/pallas_call | solution.py:690
  539.9 1.4 fusion.29
  541.4 52.5 %shard_map.274 = (f32[384,9216]{1,0:T(8,128)}, f32[384,9216]{1,0:T(8,128)}, f32[384,9216]{1,0:T(8,128)}, f32[384,9216]{1,0:T(8,128)}, bf16[384,9216]{1,0:T(8,128...) custom-call(bf16[6144,768]{1,0:T(8,128)(2,1)} %get-tuple-element.148, ...), custom_call_target="tpu_custom_call" | custom-call | tf_op jit(solution)/shard_map/pallas_call | solution.py:761
  593.9 2.8 fusion.16
  596.7 2.8 fusion.18
  599.6 4.1 fusion.13
  603.8 5.5 add_convert_fusion
  609.3 3.9 add_convert_fusion.1
  (111 shorter events, 6.6 us)
Async XLA Ops:
  7.2 59.4 %copy-start = (bf16[2048,768]{1,0:T(8,128)(2,1)S(1)}, bf16[2048,768]{1,0:T(8,128)(2,1)}, u32[]{:S(2)}) copy-start(bf16[2048,768]{1,0:T(8,128)(2,1)} %param.28) | copy-start | bytes 9437188
  7.2 38.5 %all-gather.3.cloned.1.call-start = ((), (), s32[]{:S(2)}) async-start(), calls=%async_computation | async-start | bytes 21233664 | tf_op jit(solution)/shard_map/all_gather | solution.py:828
  16.4 4.1 copy-start.31
  16.4 104.2 %all-gather.5.cloned.1.call-start = ((), (), s32[]{:S(2)}) async-start(), calls=%async_computation.1 | async-start | bytes 7077888 | tf_op jit(solution)/shard_map/all_gather | solution.py:828
  52.2 1.7 copy-start.5
  52.2 1.7 copy-start.7
  53.9 12.7 %copy-start.6 = (bf16[1024,768]{1,0:T(8,128)(2,1)}, bf16[1024,768]{1,0:T(8,128)(2,1)S(1)}, u32[]{:S(2)}) copy-start(bf16[1024,768]{1,0:T(8,128)(2,1)S(1)} %get-tuple-element.179.q_ref) | copy-start | bytes 4718596
  66.6 7.5 %copy-start.12 = (bf16[1024,768]{1,0:T(8,128)(2,1)}, bf16[1024,768]{1,0:T(8,128)(2,1)S(1)}, u32[]{:S(2)}) copy-start(bf16[1024,768]{1,0:T(8,128)(2,1)S(1)} %get-tuple-element.131.x_ref) | copy-start | bytes 4718596
  66.6 7.5 %copy-start.36 = (bf16[1024,768]{1,0:T(8,128)(2,1)S(1)}, bf16[1024,768]{1,0:T(8,128)(2,1)}, u32[]{:S(2)}) copy-start(bf16[1024,768]{1,0:T(8,128)(2,1)} %param.27) | copy-start | bytes 4718596
  74.1 4.8 copy-start.20
  78.9 2.9 copy-start.16
  82.3 3.6 copy-start.26
  85.9 5.5 copy-start.10
  119.5 1.1 copy-start.14
  120.6 66.0 %copy-start.11 = (bf16[1024,768]{1,0:T(8,128)(2,1)S(1)}, bf16[1024,768]{1,0:T(8,128)(2,1)}, u32[]{:S(2)}) copy-start(bf16[1024,768]{1,0:T(8,128)(2,1)} %copy-done.10) | copy-start | bytes 4718596
  186.7 1.4 copy-start.15
  188.1 64.1 %copy-start.27 = (f32[1024,768]{1,0:T(8,128)S(1)}, f32[1024,768]{1,0:T(8,128)}, u32[]{:S(2)}) copy-start(f32[1024,768]{1,0:T(8,128)} %copy-done.26) | copy-start | bytes 9437188
  252.2 2.5 copy-start.17
  252.2 3.3 copy-start.38
  258.9 1.4 copy-start.13
  260.0 2.7 copy-start.18
  266.6 36.0 %copy-start.37 = (bf16[1024,768]{1,0:T(8,128)(2,1)S(1)}, bf16[1024,768]{1,0:T(8,128)(2,1)}, u32[]{:S(2)}) copy-start(bf16[1024,768]{1,0:T(8,128)(2,1)} %param.27) | copy-start | bytes 4718596
  302.5 2.6 copy-start.3
  302.6 2.6 copy-start.8
  302.6 5.3 copy-start.1
  307.9 1.9 copy-start.24
  313.5 1.9 copy-start.39
  328.2 8.0 %copy-start.33 = (f32[24,768]{1,0:T(8,128)S(1)}, f32[24,768]{1,0:T(8,128)}, u32[]{:S(2)}) copy-start(f32[24,768]{1,0:T(8,128)} %get-tuple-element.147) | copy-start | bytes 221188
  336.2 3.9 copy-start.23
  336.2 3.9 copy-start.30
  340.1 1.6 copy-start.21
  340.1 2.5 copy-start.22
  340.1 2.8 copy-start.28
  340.1 3.2 copy-start.29
  345.6 194.3 %copy-start.32 = (f32[384,17]{0,1:T(8,128)S(1)}, f32[384,17]{0,1:T(8,128)}, u32[]{:S(2)}) copy-start(f32[384,17]{0,1:T(8,128)} %param.33) | copy-start | bytes 78340
  345.6 194.3 %copy-start.34 = (f32[384,17]{0,1:T(8,128)S(1)}, f32[384,17]{0,1:T(8,128)}, u32[]{:S(2)}) copy-start(f32[384,17]{0,1:T(8,128)} %param.36) | copy-start | bytes 78340
  345.6 194.3 %copy-start.35 = (f32[384,17]{0,1:T(8,128)S(1)}, f32[384,17]{0,1:T(8,128)}, u32[]{:S(2)}) copy-start(f32[384,17]{0,1:T(8,128)} %param.39) | copy-start | bytes 78340
  541.4 52.5 %copy-start.9 = (bf16[1024,768]{1,0:T(8,128)(2,1)S(1)}, bf16[1024,768]{1,0:T(8,128)(2,1)}, u32[]{:S(2)}) copy-start(bf16[1024,768]{1,0:T(8,128)(2,1)} %copy-done.8) | copy-start | bytes 4718596
  593.9 2.8 copy-start.4
  596.7 2.9 copy-start.40
  599.6 4.2 copy-start.25
  603.8 5.5 copy-start.2
  603.8 5.5 copy-start.19
Sparse Core Ops, SparseCore 0:
  16.5 29.1 all-gather.2
  47.8 15.5 all-gather.4

commit v3 on v2

--- a/solution.py
+++ b/solution.py
@@ -27,6 +27,44 @@
 masked_score = -1e30
 FACTOR = HD ** (-0.5)
 SCALE2 = FACTOR / math.log(2.0)
+
+
+CROSS_TABLE = {
+    (0, 1): ((0, 0), (1, 0), (2, 0), (3, 0)),
+    (0, 7): ((0, 1), (1, 1), (2, 1), (3, 1)),
+    (1, 7): ((0, 2), (1, 2), (2, 2), (3, 2)),
+    (1, 13): ((4, 0), (5, 0), (6, 0), (7, 0)),
+    (2, 7): ((0, 3), (1, 3), (2, 3), (3, 3), (4, 1), (5, 1), (6, 1), (7, 1)),
+    (3, 7): ((0, 4), (1, 4), (2, 4), (3, 4), (4, 2), (5, 2), (6, 2), (7, 2)),
+    (4, 7): ((0, 5), (1, 5), (2, 5), (3, 5), (4, 3), (5, 3), (6, 3), (7, 3)),
+    (5, 7): ((0, 6), (1, 6), (2, 6), (3, 6), (4, 4), (5, 4), (6, 4), (7, 4)),
+    (5, 13): ((0, 7), (1, 7), (2, 7), (3, 7), (0, 8), (1, 8), (2, 8), (3, 8)),
+}
+
+
+SELF_TABLE = {
+    (0, 1): ((0, 0), (1, 0), (2, 0), (3, 0)),
+    (0, 5): ((2, 1), (3, 1)),
+    (1, 3): ((0, 1), (1, 1)),
+    (2, 3): ((0, 2), (1, 2), (2, 2), (3, 2)),
+    (3, 5): ((2, 3), (3, 3)),
+    (4, 3): ((0, 3), (1, 3)),
+    (4, 8): ((0, 4), (1, 4), (2, 4), (3, 4)),
+}
+
+
+TAIL_ORDER = (
+    (10, 0), (0, 0), (1, 0), (2, 0), (3, 0), (4, 0), (5, 0), (4, 1),
+    (5, 1), (4, 2), (10, 1), (5, 2), (6, 0), (7, 0), (0, 1), (1, 1),
+    (2, 1), (3, 1), (6, 1), (7, 1), (10, 2), (4, 3), (5, 3), (0, 2),
+    (1, 2), (2, 2), (3, 2), (8, 0), (9, 0), (4, 4), (10, 3), (5, 4),
+    (8, 1), (9, 1), (6, 2), (7, 2), (4, 5), (5, 5), (6, 3), (7, 3),
+    (10, 4), (0, 3), (1, 3), (2, 3), (3, 3), (4, 6), (5, 6), (8, 2),
+    (9, 2), (0, 4), (1, 4), (2, 4), (3, 4), (6, 4), (7, 4), (8, 3),
+    (9, 3), (4, 7), (5, 7), (4, 8), (5, 8), (6, 5), (7, 5), (8, 4),
+    (9, 4), (6, 6), (7, 6), (8, 5), (9, 5), (6, 7), (7, 7), (6, 8),
+    (7, 8), (8, 6), (9, 6), (8, 7), (9, 7), (8, 8), (9, 8),
+)
 
 
 def head_masks(rows):
@@ -137,25 +175,22 @@
 def attend_forward(queries, keys_in, values_in, block_table, causal):
     seqs = block_table.shape[0]
     rows, keys = queries.shape[0] // seqs, keys_in.shape[0] // seqs
-    spec_q = pl.BlockSpec((rows, 128), lambda s, i, m: (s, i))
-    spec_k = pl.BlockSpec((keys, 128), lambda s, i, m: (s, i))
-    spec_l = pl.BlockSpec((1, 1, 8, rows), lambda s, i, m: (s, i, 0, 0))
+    spec_q = pl.BlockSpec((rows, 128), lambda s, i: (s, i))
+    spec_k = pl.BlockSpec((keys, 128), lambda s, i: (s, i))
+    spec_l = pl.BlockSpec((1, 1, 8, rows), lambda s, i: (s, i, 0, 0))
     area = rows * keys * H * HD * seqs
     return pl.pallas_call(
         partial(forward_kernel, causal),
-        grid_spec=pltpu.PrefetchScalarGridSpec(
-            num_scalar_prefetch=1,
-            grid=(seqs, D // 128),
-            in_specs=[spec_q, spec_k, spec_k],
-            out_specs=[spec_q, spec_l],
-            scratch_shapes=[
-                pltpu.VMEM((2, rows, 128), jnp.bfloat16),
-                pltpu.VMEM((128, keys), jnp.bfloat16),
-                pltpu.VMEM((2, HD, rows), jnp.float32),
-                pltpu.VMEM((2, rows), jnp.float32),
-                pltpu.VMEM((2, rows), jnp.float32),
-            ],
-        ),
+        grid=(seqs, D // 128),
+        in_specs=[pl.BlockSpec(memory_space=pltpu.SMEM), spec_q, spec_k, spec_k],
+        out_specs=[spec_q, spec_l],
+        scratch_shapes=[
+            pltpu.VMEM((2, rows, 128), jnp.bfloat16),
+            pltpu.VMEM((128, keys), jnp.bfloat16),
+            pltpu.VMEM((2, HD, rows), jnp.float32),
+            pltpu.VMEM((2, rows), jnp.float32),
+            pltpu.VMEM((2, rows), jnp.float32),
+        ],
         out_shape=[
             jax.ShapeDtypeStruct(queries.shape, jnp.bfloat16),
             jax.ShapeDtypeStruct((seqs, D // 128, 8, rows), jnp.float32),
@@ -165,109 +200,6 @@
             flops=(8 if causal else 16) * area, bytes_accessed=4 * queries.size, transcendentals=0
         ),
     )(block_table, queries, keys_in, values_in)
-
-
-def backward_kernel(
-    causal, mask_ref, q_ref, k_ref, v_ref, m_ref, x_ref, lse_ref, dq_ref, dk_ref, dv_ref,
-    qm_ref, mm_ref, qt_ref, mt_ref, col_ref, acc_ref, dkt_ref, dvt_ref,
-):
-    rows, keys = q_ref.shape[0], k_ref.shape[0]
-    seq = pl.program_id(0)
-    step, tile = (BLK, BLK) if causal else (2 * BLK, 2 * BLK)
-    masks = head_masks(rows)
-    masks_k = head_masks(tile)
-    queries, grads = q_ref[...], m_ref[...]
-    qt_ref[...] = queries.T
-    mt_ref[...] = grads.T
-    product = grads.astype(jnp.float32) * x_ref[...].astype(jnp.float32)
-    lse = lse_ref[0, 0].T
-    for head in range(2):
-        qm_ref[head] = keep(masks[head], queries)
-        mm_ref[head] = keep(masks[head], grads)
-        centre = jnp.sum(keep(masks[head], product), axis=1, keepdims=True)
-        col_ref[head] = jnp.broadcast_to(centre, (rows, 128))
-        col_ref[2 + head] = jnp.broadcast_to(lse[:, head : head + 1], (rows, 128))
-    if causal:
-        below = lax.broadcasted_iota(jnp.int32, (BLK, BLK), 0) >= lax.broadcasted_iota(
-            jnp.int32, (BLK, BLK), 1
-        )
-
-    def widen(column):
-        return jnp.concatenate([column] * (tile // 128), axis=1)
-
-    for j in range(keys // tile):
-        key_rows = slice(j * tile, (j + 1) * tile)
-        key, value = k_ref[key_rows, :], v_ref[key_rows, :]
-        key_masked = [keep(mask, key) for mask in masks_k]
-        total_k, total_v = [None, None], [None, None]
-        first_step = j if causal else 0
-        for i in range(first_step, rows // step):
-            here = slice(i * step, (i + 1) * step)
-            for head in range(2):
-                scores = rows_dot_t(qm_ref[head, here, :], key)
-                prob_grad = rows_dot_t(mm_ref[head, here, :], value)
-                level = col_ref[2 + head, here]
-                if causal and i > j:
-                    level = level + jnp.where(mask_ref[seq, i, j] > 0, 0.0, -masked_score)
-                probs = jnp.exp2(scores * SCALE2 - widen(level))
-                if causal and i == j:
-                    probs = jnp.where(below, probs, 0.0)
-                score_grad = (probs * (prob_grad - widen(col_ref[head, here]))).astype(jnp.bfloat16)
-                probs = probs.astype(jnp.bfloat16)
-                part = slice(head * HD, (head + 1) * HD)
-                add_v = rows_dot(mt_ref[part, here], probs)
-                add_k = rows_dot(qt_ref[part, here], score_grad)
-                total_v[head] = add_v if total_v[head] is None else total_v[head] + add_v
-                total_k[head] = add_k if total_k[head] is None else total_k[head] + add_k
-                add_q = rows_dot(score_grad, key_masked[head])
-                if j == 0 and head == 0:
-                    acc_ref[here, :] = add_q
-                else:
-                    acc_ref[here, :] += add_q
-        for head in range(2):
-            part = slice(head * HD, (head + 1) * HD)
-            dkt_ref[part, key_rows] = total_k[head] * FACTOR
-            dvt_ref[part, key_rows] = total_v[head]
-    dq_ref[...] = (acc_ref[...] * FACTOR).astype(jnp.bfloat16)
-    dk_ref[...] = dkt_ref[...].T.astype(jnp.bfloat16)
-    dv_ref[...] = dvt_ref[...].T.astype(jnp.bfloat16)
-
-
-def attend_backward(queries, keys_in, values_in, block_table, causal, mixed, lse, mixed_grad):
-    seqs = block_table.shape[0]
-    rows, keys = queries.shape[0] // seqs, keys_in.shape[0] // seqs
-    spec_q = pl.BlockSpec((rows, 128), lambda s, i, m: (s, i))
-    spec_k = pl.BlockSpec((keys, 128), lambda s, i, m: (s, i))
-    spec_l = pl.BlockSpec((1, 1, 8, rows), lambda s, i, m: (s, i, 0, 0))
-    area = rows * keys * H * HD * seqs
-    return pl.pallas_call(
-        partial(backward_kernel, causal),
-        grid_spec=pltpu.PrefetchScalarGridSpec(
-            num_scalar_prefetch=1,
-            grid=(seqs, D // 128),
-            in_specs=[spec_q, spec_k, spec_k, spec_q, spec_q, spec_l],
-            out_specs=[spec_q, spec_k, spec_k],
-            scratch_shapes=[
-                pltpu.VMEM((2, rows, 128), jnp.bfloat16),
-                pltpu.VMEM((2, rows, 128), jnp.bfloat16),
-                pltpu.VMEM((128, rows), jnp.bfloat16),
-                pltpu.VMEM((128, rows), jnp.bfloat16),
-                pltpu.VMEM((4, rows, 128), jnp.float32),
-                pltpu.VMEM((rows, 128), jnp.float32),
-                pltpu.VMEM((128, keys), jnp.float32),
-                pltpu.VMEM((128, keys), jnp.float32),
-            ],
-        ),
-        out_shape=[
-            jax.ShapeDtypeStruct(queries.shape, jnp.bfloat16),
-            jax.ShapeDtypeStruct(keys_in.shape, jnp.bfloat16),
-            jax.ShapeDtypeStruct(keys_in.shape, jnp.bfloat16),
-        ],
-        compiler_params=pltpu.CompilerParams(vmem_limit_bytes=48 << 20),
-        cost_estimate=pl.CostEstimate(
-            flops=(20 if causal else 40) * area, bytes_accessed=4 * queries.size, transcendentals=0
-        ),
-    )(block_table, queries, keys_in, values_in, mixed_grad, mixed, lse)
 
 
 ROWS = 256
@@ -458,6 +390,8 @@
 
 
 MESH_ID = pl.DeviceIdType.MESH
+UNIT = 384
+HALF = 384
 
 
 def peers_of(lanes):
@@ -478,113 +412,149 @@
     pl.semaphore_wait(barrier, 2 + lanes)
 
 
-def aligned(value):
-    return pl.multiple_of(value, 16)
-
-
-def bulk_scratch(rows, lanes):
-    block = rows // (4 * lanes)
+def aligned(value, by=16):
+    return pl.multiple_of(value, by)
+
+
+def remote_copy(sems, index, source, target, peer):
+    return pltpu.make_async_remote_copy(
+        src_ref=source,
+        dst_ref=target,
+        send_sem=sems[0].at[index],
+        recv_sem=sems[1].at[index],
+        device_id=peer,
+        device_id_type=MESH_ID,
+    )
+
+
+def unit_scratch(mode, lanes):
     bf16 = jnp.bfloat16
-    return [
-        pltpu.VMEM((rows, D), bf16),
-        pltpu.VMEM((rows, D), bf16),
-        pltpu.VMEM((rows // 2, D), bf16),
-        pltpu.VMEM((rows // 4, D), bf16),
-        pltpu.VMEM((lanes, block, D), bf16),
+    block = UNIT // (2 * lanes)
+    shapes = [pltpu.VMEM((UNIT, D), bf16), pltpu.VMEM((block, HALF), bf16)]
+    if mode != "gather":
+        shapes += [
+            pltpu.VMEM((UNIT, D), bf16),
+            pltpu.VMEM((UNIT, HALF), bf16),
+            pltpu.VMEM((UNIT // 2, HALF), bf16),
+            pltpu.VMEM((lanes, block, HALF), bf16),
+        ]
+    return shapes + [
         pltpu.SemaphoreType.DMA((5 + 2 * lanes,)),
         pltpu.SemaphoreType.DMA((5 + 2 * lanes,)),
-        pltpu.SemaphoreType.DMA((2,)),
+        pltpu.SemaphoreType.DMA((3,)),
     ]
 
 
-def bulk_steps(term_ref, sum_ref, scratch, x_first, lanes):
-    acc, got_core, got_a, got_b, got_z, send_sem, recv_sem, local_sem = scratch
-    full = got_core
-    rows = acc.shape[0]
-    half, quarter, block = rows // 2, rows // 4, rows // (4 * lanes)
+def unit_places(x_first, lanes):
     rep, shard, x, y, z, sibling, peer_x, peer_y, others = peers_of(lanes)
     here_a, here_b = (x, y) if x_first else (y, x)
     peer_a, peer_b = (peer_x, peer_y) if x_first else (peer_y, peer_x)
-    mine_a = aligned(here_a * half)
-    theirs_a = aligned((1 - here_a) * half)
-    mine_b = aligned(here_a * half + here_b * quarter)
-    theirs_b = aligned(here_a * half + (1 - here_b) * quarter)
-    mine_z = aligned(mine_b + z * block)
-
-    def remote(index, source, target, peer):
-        return pltpu.make_async_remote_copy(
-            src_ref=source,
-            dst_ref=target,
-            send_sem=send_sem.at[index],
-            recv_sem=recv_sem.at[index],
-            device_id=peer,
-            device_id_type=MESH_ID,
+    return shard, z, here_a, here_b, sibling, peer_a, peer_b, others
+
+
+def scatter_steps(term, row, scratch, x_first, lanes, block_out):
+    got, block_ref, acc, got_a, got_b, got_z = scratch[:6]
+    sems, local_sem = scratch[-3:-1], scratch[-1]
+    shard, z, here_a, here_b, sibling, peer_a, peer_b, others = unit_places(x_first, lanes)
+    half_rows, block = UNIT // 2, UNIT // (2 * lanes)
+    mine_cols = pl.ds(aligned(here_a * HALF, 128), HALF)
+    their_cols = pl.ds(aligned((1 - here_a) * HALF, 128), HALF)
+    mine_b = aligned(here_b * half_rows)
+    core = remote_copy(sems, 0, term.at[1 - shard, pl.ds(row, UNIT)], got, sibling)
+    load = pltpu.make_async_copy(term.at[shard, pl.ds(row, UNIT)], acc, local_sem.at[0])
+    to_a = remote_copy(sems, 1, acc.at[:, their_cols], got_a, peer_a)
+    to_b = remote_copy(
+        sems, 2, acc.at[pl.ds(aligned((1 - here_b) * half_rows), half_rows), mine_cols], got_b, peer_b
+    )
+    to_z = [
+        remote_copy(
+            sems, 5 + k, acc.at[pl.ds(aligned(mine_b + ((z + k + 1) % lanes) * block), block), mine_cols],
+            got_z.at[z], peer,
         )
-
-    core = remote(0, term_ref.at[1 - shard], got_core, sibling)
-    load = pltpu.make_async_copy(term_ref.at[shard], acc, local_sem.at[0])
-    to_a = remote(1, acc.at[pl.ds(theirs_a, half)], got_a, peer_a)
-    to_b = remote(2, acc.at[pl.ds(theirs_b, quarter)], got_b, peer_b)
-    to_z, all_z = [], []
-    for k, peer in enumerate(others):
-        theirs = aligned(mine_b + ((z + k + 1) % lanes) * block)
-        to_z.append(remote(5 + k, acc.at[pl.ds(theirs, block)], got_z.at[z], peer))
-        all_z.append(
-            remote(5 + lanes + k, full.at[pl.ds(mine_z, block)], full.at[pl.ds(mine_z, block)], peer)
-        )
-    all_b = remote(3, full.at[pl.ds(mine_b, quarter)], full.at[pl.ds(mine_b, quarter)], peer_b)
-    all_a = remote(4, full.at[pl.ds(mine_a, half)], full.at[pl.ds(mine_a, half)], peer_a)
-    store = pltpu.make_async_copy(full, sum_ref, local_sem.at[1])
-
-    def add(start, count, got):
-        def body(i, carry):
-            there = pl.ds(aligned(start + i * block), block)
-            total = acc[there, :].astype(jnp.float32) + got[pl.ds(aligned(i * block), block), :].astype(
-                jnp.float32
-            )
-            acc[there, :] = total.astype(jnp.bfloat16)
-            return carry
-
-        lax.fori_loop(0, count // block, body, 0)
-
-    def step_core():
+        for k, peer in enumerate(others)
+    ]
+    f32, bf16 = jnp.float32, jnp.bfloat16
+
+    def start():
         core.start()
         load.start()
 
     def step_a():
         load.wait()
         core.wait()
-        add(0, rows, got_core)
+
+        def body(i, carry):
+            at = pl.ds(aligned(i * block), block)
+            acc[at, :] = (acc[at, :].astype(f32) + got[at, :].astype(f32)).astype(bf16)
+            return carry
+
+        lax.fori_loop(0, UNIT // block, body, 0)
         to_a.start()
 
     def step_b():
         to_a.wait()
-        add(mine_a, half, got_a)
+
+        def body(i, carry):
+            at = pl.ds(aligned(i * block), block)
+            acc[at, mine_cols] = (acc[at, mine_cols].astype(f32) + got_a[at, :].astype(f32)).astype(bf16)
+            return carry
+
+        lax.fori_loop(0, UNIT // block, body, 0)
         to_b.start()
 
     def step_z():
         to_b.wait()
-        add(mine_b, quarter, got_b)
+
+        def body(i, carry):
+            at = pl.ds(aligned(mine_b + i * block), block)
+            other = got_b[pl.ds(aligned(i * block), block), :].astype(f32)
+            acc[at, mine_cols] = (acc[at, mine_cols].astype(f32) + other).astype(bf16)
+            return carry
+
+        lax.fori_loop(0, half_rows // block, body, 0)
         for copy in to_z:
             copy.start()
 
-    def step_gather_z():
+    def step_own():
         for copy in to_z:
             copy.wait()
-        there = pl.ds(mine_z, block)
-        total = acc[there, :].astype(jnp.float32)
+        total = acc[pl.ds(aligned(mine_b + z * block), block), mine_cols].astype(f32)
         for k in range(1, lanes):
-            total = total + got_z[(z + k) % lanes].astype(jnp.float32)
-        full[there, :] = total.astype(jnp.bfloat16)
+            total = total + got_z[(z + k) % lanes].astype(f32)
+        block_ref[...] = total.astype(bf16)
+        if block_out is not None:
+            block_out[...] = total.astype(bf16)
+
+    return [start, step_a, step_b, step_z, step_own]
+
+
+def gather_steps(block_in, sum_out, scratch, x_first, lanes):
+    full, block_ref = scratch[:2]
+    sems, local_sem = scratch[-3:-1], scratch[-1]
+    shard, z, here_a, here_b, sibling, peer_a, peer_b, others = unit_places(x_first, lanes)
+    half_rows, block = UNIT // 2, UNIT // (2 * lanes)
+    mine_cols = pl.ds(aligned(here_a * HALF, 128), HALF)
+    mine_b = aligned(here_b * half_rows)
+    mine_z = full.at[pl.ds(aligned(mine_b + z * block), block), mine_cols]
+    mine_half = full.at[pl.ds(mine_b, half_rows), mine_cols]
+    mine_all = full.at[:, mine_cols]
+    all_z = [remote_copy(sems, 5 + lanes + k, mine_z, mine_z, peer) for k, peer in enumerate(others)]
+    all_b = remote_copy(sems, 3, mine_half, mine_half, peer_b)
+    all_a = remote_copy(sems, 4, mine_all, mine_all, peer_a)
+    store = pltpu.make_async_copy(full, sum_out, local_sem.at[1])
+
+    def start():
+        source = block_ref if block_in is None else block_in
+        full[pl.ds(aligned(mine_b + z * block), block), mine_cols] = source[...]
         for copy in all_z:
             copy.start()
 
-    def step_gather_b():
+    def step_b():
         for copy in all_z:
             copy.wait()
         all_b.start()
 
-    def step_gather_a():
+    def step_a():
         all_b.wait()
         all_a.start()
 
@@ -592,9 +562,17 @@
         all_a.wait()
         store.start()
 
-    return [
-        step_core, step_a, step_b, step_z, step_gather_z, step_gather_b, step_gather_a, step_store, store.wait,
-    ]
+    return [start, step_b, step_a, step_store, store.wait]
+
+
+def joined_steps(scatter, gather):
+    own, begin = scatter[-1], gather[0]
+
+    def both():
+        own()
+        begin()
+
+    return scatter[:-1] + [both] + gather[1:]
 
 
 def small_scratch(shape, lanes):
@@ -608,23 +586,13 @@
 
 
 def small_steps(term_ref, sum_ref, scratch, lanes):
-    held, got, got_z, send_sem, recv_sem = scratch
+    held, got, got_z = scratch[:3]
+    sems = scratch[3:]
     rep, shard, x, y, z, sibling, peer_x, peer_y, others = peers_of(lanes)
-
-    def remote(index, source, target, peer):
-        return pltpu.make_async_remote_copy(
-            src_ref=source,
-            dst_ref=target,
-            send_sem=send_sem.at[index],
-            recv_sem=recv_sem.at[index],
-            device_id=peer,
-            device_id_type=MESH_ID,
-        )
-
-    core = remote(0, term_ref.at[1 - shard], got.at[0], sibling)
-    to_x = remote(1, held.at[0], got.at[1], peer_x)
-    to_y = remote(2, held.at[1], got.at[2], peer_y)
-    to_z = [remote(3 + k, held.at[2], got_z.at[z], peer) for k, peer in enumerate(others)]
+    core = remote_copy(sems, 0, term_ref.at[1 - shard], got.at[0], sibling)
+    to_x = remote_copy(sems, 1, held.at[0], got.at[1], peer_x)
+    to_y = remote_copy(sems, 2, held.at[1], got.at[2], peer_y)
+    to_z = [remote_copy(sems, 3 + k, held.at[2], got_z.at[z], peer) for k, peer in enumerate(others)]
 
     def step_x():
         core.wait()
@@ -654,52 +622,359 @@
     return [core.start, step_x, step_y, step_z, step_end]
 
 
-def interleave(plans):
-    last = max(begin + len(steps) for begin, steps in plans)
-    for tick in range(last):
-        for begin, steps in plans:
-            if 0 <= tick - begin < len(steps):
-                steps[tick - begin]()
-
-
-def reduce_kernel(lanes, count, *refs):
-    terms, small_term = refs[:count], refs[count]
-    sums, small_sum = refs[count + 1], refs[count + 2]
-    scratch = refs[count + 3 :]
-    enter_barrier(lanes)
-    plans = []
-    at = 0
-    for i, term in enumerate(terms):
-        rows = term.shape[1]
-        plans.append(
-            (i // 2, bulk_steps(term, sums.at[pl.ds(at, rows)], scratch[8 * i : 8 * i + 8], i % 2 == 0, lanes))
+class Traffic:
+    def __init__(self, modes, lanes, terms=(), places=(), blocks=None, small=None):
+        self.modes, self.lanes, self.terms, self.places = modes, lanes, list(terms), list(places)
+        self.blocks, self.small = blocks, small
+        self.n_scatter = sum(mode == "scatter" for mode in modes)
+        self.n_sum = len(modes) - self.n_scatter
+
+    def operands(self):
+        return self.terms + ([self.blocks] if self.blocks is not None else []) + (
+            [self.small] if self.small is not None else []
         )
-        at += rows
-    plans.append((0, small_steps(small_term, small_sum, scratch[8 * count :], lanes)))
-    interleave(plans)
-
-
-def reduce_all(terms, small, lanes):
-    any_spec, vmem_spec = pl.BlockSpec(memory_space=pl.ANY), pl.BlockSpec(memory_space=pltpu.VMEM)
-    count = len(terms)
-    total = sum(term.shape[1] for term in terms)
-    scratch = []
-    for term in terms:
-        scratch += bulk_scratch(term.shape[1], lanes)
-    scratch += small_scratch(small.shape[1:], lanes)
+
+    def in_specs(self):
+        vmem = pl.BlockSpec(memory_space=pltpu.VMEM)
+        return [pl.BlockSpec(memory_space=pl.ANY)] * len(self.terms) + [vmem] * (
+            (self.blocks is not None) + (self.small is not None)
+        )
+
+    def out_specs(self):
+        specs = []
+        if self.n_scatter:
+            specs.append(pl.BlockSpec(memory_space=pltpu.VMEM))
+        if self.n_sum:
+            specs.append(pl.BlockSpec(memory_space=pl.ANY))
+        if self.small is not None:
+            specs.append(pl.BlockSpec(memory_space=pltpu.VMEM))
+        return specs
+
+    def out_shape(self):
+        shapes = []
+        if self.n_scatter:
+            shapes.append(
+                jax.ShapeDtypeStruct((self.n_scatter, UNIT // (2 * self.lanes), HALF), jnp.bfloat16)
+            )
+        if self.n_sum:
+            shapes.append(jax.ShapeDtypeStruct((self.n_sum * UNIT, D), jnp.bfloat16))
+        if self.small is not None:
+            shapes.append(jax.ShapeDtypeStruct(self.small.shape[1:], jnp.float32))
+        return shapes
+
+    def scratch(self):
+        shapes = []
+        for mode in self.modes:
+            shapes += unit_scratch(mode, self.lanes)
+        if self.small is not None:
+            shapes += small_scratch(self.small.shape[1:], self.lanes)
+        return shapes
+
+    def steps(self, ins, outs, scratch):
+        ins, outs, scratch = list(ins), list(outs), list(scratch)
+        terms = [ins.pop(0) for _ in self.terms]
+        blocks = ins.pop(0) if self.blocks is not None else None
+        small = ins.pop(0) if self.small is not None else None
+        block_out = outs.pop(0) if self.n_scatter else None
+        sum_out = outs.pop(0) if self.n_sum else None
+        small_out = outs.pop(0) if small is not None else None
+        found = []
+        n_block = n_sum = n_in = n_place = 0
+        for i, mode in enumerate(self.modes):
+            count = len(unit_scratch(mode, self.lanes))
+            mine, scratch = scratch[:count], scratch[count:]
+            x_first = None
+            if mode != "gather":
+                which, row, x_first = self.places[n_place]
+                target = block_out.at[n_block] if mode == "scatter" else None
+                scatter = scatter_steps(terms[which], row, mine, x_first, self.lanes, target)
+                n_block += mode == "scatter"
+            else:
+                x_first = self.places[n_place]
+            n_place += 1
+            if mode != "scatter":
+                source = None
+                if mode == "gather":
+                    source = blocks.at[n_in]
+                    n_in += 1
+                gather = gather_steps(
+                    source, sum_out.at[pl.ds(n_sum * UNIT, UNIT)], mine, x_first, self.lanes
+                )
+                n_sum += 1
+            found.append(
+                scatter if mode == "scatter" else gather if mode == "gather" else joined_steps(scatter, gather)
+            )
+        if small is not None:
+            found.append(small_steps(small, small_out, scratch, self.lanes))
+        return found
+
+
+def traffic_kernel(traffic, order, *refs):
+    n_in, n_out = len(traffic.in_specs()), len(traffic.out_specs())
+    steps = traffic.steps(refs[:n_in], refs[n_in : n_in + n_out], refs[n_in + n_out :])
+    enter_barrier(traffic.lanes)
+    for which, step in order:
+        steps[which][step]()
+
+
+def run_traffic(traffic, order, collective_id):
     return pl.pallas_call(
-        partial(reduce_kernel, lanes, count),
-        in_specs=[any_spec] * count + [vmem_spec],
-        out_specs=[any_spec, vmem_spec],
-        out_shape=[
-            jax.ShapeDtypeStruct((total, D), jnp.bfloat16),
-            jax.ShapeDtypeStruct(small.shape[1:], jnp.float32),
-        ],
+        partial(traffic_kernel, traffic, order),
+        in_specs=traffic.in_specs(),
+        out_specs=traffic.out_specs(),
+        out_shape=traffic.out_shape(),
+        scratch_shapes=traffic.scratch(),
+        compiler_params=pltpu.CompilerParams(
+            collective_id=collective_id, has_side_effects=True, vmem_limit_bytes=58 << 20
+        ),
+    )(*traffic.operands())
+
+
+def backward_kernel(causal, traffic, table, factor, *refs):
+    refs = list(refs)
+    take = lambda count: [refs.pop(0) for _ in range(count)]
+    mask_ref, q_ref, k_ref, v_ref, m_ref, x_ref, lse_ref, left_q_ref, up_ref, wq_ref, wk_ref, wv_ref = take(12)
+    if not causal:
+        left_k_ref, wo_ref, res_ref, mixo_ref, vec_ref = take(5)
+    traffic_in = take(len(traffic.in_specs()) if traffic else 0)
+    tq_ref, tk_ref, tv_ref, pair_sums_ref, grad_ref = take(5)
+    if not causal:
+        encg_ref, gmix_ref, to_ref, norm_sums_ref = take(4)
+    traffic_out = take(len(traffic.out_specs()) if traffic else 0)
+    qm_ref, mm_ref, qt_ref, mt_ref, col_ref, acc_ref, dkt_ref, dvt_ref, total_ref, up_sem = take(10)
+    if not causal:
+        total_k_ref, low_ref = take(2)
+    bf16, f32 = jnp.bfloat16, jnp.float32
+    rows, keys = q_ref.shape[0], k_ref.shape[0]
+    pair = pl.program_id(0)
+    step, tile = (BLK, BLK) if causal else (2 * BLK, 2 * BLK)
+    slot = [0]
+    if traffic:
+        steps = traffic.steps(traffic_in, traffic_out, refs)
+
+        @pl.when(pair == 0)
+        def _():
+            enter_barrier(traffic.lanes)
+
+    def hook():
+        if traffic:
+            for at_pair in range(D // 128):
+                todo = table.get((at_pair, slot[0]), ())
+                if todo:
+
+                    @pl.when(pair == at_pair)
+                    def _():
+                        for which, index in todo:
+                            steps[which][index]()
+
+        slot[0] += 1
+
+    def each(count, size, body):
+        def run(r, carry):
+            body(pl.ds(pl.multiple_of(r * size, size), size))
+            return carry
+
+        lax.fori_loop(0, count // size, run, 0)
+
+    hook()
+
+    @pl.when(pair == 0)
+    def _():
+        load = pltpu.make_async_copy(up_ref, total_ref, up_sem)
+        load.start()
+        load.wait()
+        if not causal:
+            total_k_ref[...] = jnp.zeros_like(total_k_ref)
+
+    masks = head_masks(rows)
+    masks_k = head_masks(tile)
+    queries, grads = q_ref[...], m_ref[...]
+    qt_ref[...] = queries.T
+    mt_ref[...] = grads.T
+    product = grads.astype(f32) * x_ref[...].astype(f32)
+    lse = lse_ref[0].T
+    for head in range(2):
+        qm_ref[head] = keep(masks[head], queries)
+        mm_ref[head] = keep(masks[head], grads)
+        centre = jnp.sum(keep(masks[head], product), axis=1, keepdims=True)
+        col_ref[head] = jnp.broadcast_to(centre, (rows, 128))
+        col_ref[2 + head] = jnp.broadcast_to(lse[:, head : head + 1], (rows, 128))
+    if causal:
+        below = lax.broadcasted_iota(jnp.int32, (BLK, BLK), 0) >= lax.broadcasted_iota(
+            jnp.int32, (BLK, BLK), 1
+        )
+
+    def widen(column):
+        return jnp.concatenate([column] * (tile // 128), axis=1)
+
+    def level_of(head, j, begin, end):
+        level = col_ref[2 + head, begin:end]
+        if not causal:
+            return level
+        pieces = [level[:BLK]] if begin == j * BLK else []
+        for i in range(begin // BLK + len(pieces), end // BLK):
+            off = jnp.where(mask_ref[0, i, j] > 0, 0.0, -masked_score)
+            pieces.append(level[i * BLK - begin : (i + 1) * BLK - begin] + off)
+        return jnp.concatenate(pieces, axis=0) if len(pieces) > 1 else pieces[0]
+
+    for j in range(keys // tile):
+        key_rows = slice(j * tile, (j + 1) * tile)
+        key, value = k_ref[key_rows, :], v_ref[key_rows, :]
+        key_masked = [keep(mask, key) for mask in masks_k]
+        total_k, total_v = [None, None], [None, None]
+        cuts = (j * tile, rows) if causal else tuple(range(0, rows + 1, step))
+        for begin, end in zip(cuts[:-1], cuts[1:]):
+            here = slice(begin, end)
+            hook()
+            for head in range(2):
+                scores = rows_dot_t(qm_ref[head, here, :], key)
+                prob_grad = rows_dot_t(mm_ref[head, here, :], value)
+                scores = scores * SCALE2 - widen(level_of(head, j, begin, end))
+                if causal:
+                    top = jnp.where(below, scores[:BLK], masked_score)
+                    scores = top if end == begin + BLK else jnp.concatenate([top, scores[BLK:]], axis=0)
+                probs = jnp.exp2(scores)
+                score_grad = (probs * (prob_grad - widen(col_ref[head, here]))).astype(bf16)
+                probs = probs.astype(bf16)
+                part = slice(head * HD, (head + 1) * HD)
+                add_v = rows_dot(mt_ref[part, here], probs)
+                add_k = rows_dot(qt_ref[part, here], score_grad)
+                total_v[head] = add_v if total_v[head] is None else total_v[head] + add_v
+                total_k[head] = add_k if total_k[head] is None else total_k[head] + add_k
+                add_q = rows_dot(score_grad, key_masked[head])
+                if j == 0 and head == 0:
+                    acc_ref[here, :] = add_q
+                else:
+                    acc_ref[here, :] += add_q
+        for head in range(2):
+            part = slice(head * HD, (head + 1) * HD)
+            dkt_ref[part, key_rows] = (total_k[head] * FACTOR).astype(bf16)
+            dvt_ref[part, key_rows] = total_v[head].astype(bf16)
+    hook()
+    grad_q = (acc_ref[...] * FACTOR).astype(bf16)
+    grad_qt = grad_q.T
+    pair_sums_ref[0:1, :] = row_total(grad_q.astype(f32))
+    pair_sums_ref[1:2, :] = jnp.sum(dvt_ref[...].astype(f32), axis=1, keepdims=True).T
+
+    def put(target, transposed):
+        target[...] = (transposed * factor).T.astype(bf16)
+
+    grad_k, grad_v = dkt_ref[...].T, dvt_ref[...].T
+    if causal:
+        joined = jnp.concatenate([grad_qt, dkt_ref[...], dvt_ref[...]], axis=0)
+        found = rows_dot(joined, left_q_ref[...])
+        put(tq_ref, found[:128])
+        put(tk_ref, found[128:256])
+        put(tv_ref, found[256:])
+        hook()
+        weights = jnp.concatenate([wq_ref[...], wk_ref[...], wv_ref[...]], axis=1)
+        total_ref[...] += rows_dot_t(jnp.concatenate([grad_q, grad_k, grad_v], axis=1), weights)
+        hook()
+
+        @pl.when(pair == D // 128 - 1)
+        def _():
+            grad_ref[...] = total_ref[...].astype(bf16)
+    else:
+        put(tq_ref, rows_dot(grad_qt, left_q_ref[...]))
+        total_ref[...] += rows_dot_t(grad_q, wq_ref[...])
+        hook()
+        found = rows_dot(jnp.concatenate([dkt_ref[...], dvt_ref[...]], axis=0), left_k_ref[...])
+        put(tk_ref, found[:128])
+        put(tv_ref, found[128:])
+        hook()
+        weights = jnp.concatenate([wk_ref[...], wv_ref[...]], axis=1)
+        total_k_ref[...] += rows_dot_t(jnp.concatenate([grad_k, grad_v], axis=1), weights)
+        hook()
+
+        @pl.when(pair == D // 128 - 1)
+        def _():
+            encg_ref[...] = total_k_ref[...].astype(bf16)
+            norm_sums_ref[...] = jnp.zeros_like(norm_sums_ref)
+
+            def body(at):
+                unit, inverse = unit_rows(res_ref[at, :])
+                upstream = total_ref[at, :]
+                grad = back_rows(upstream, unit, inverse, vec_ref[11:12, :])
+                grad_ref[at, :] = grad
+                low = grad.astype(bf16)
+                low_ref[at, :] = low
+                gmix_ref[at, :] = rows_dot_t(low, wo_ref[...]).astype(bf16)
+                norm_sums_ref[0:1, :] += row_total(upstream * unit)
+                norm_sums_ref[1:2, :] += row_total(upstream)
+                norm_sums_ref[2:3, :] += row_total(low.astype(f32))
+
+            each(rows, ROWS, body)
+            to_ref[...] = (column_dot(mixo_ref[...], low_ref[...]) * factor).astype(bf16)
+
+    hook()
+
+
+def attend_backward(
+    queries, keys_in, values_in, block_table, causal, mixed, lse, mixed_grad, left_q, upstream, wide_full,
+    factor, extra, traffic, table, collective_id,
+):
+    rows, keys = queries.shape[0], keys_in.shape[0]
+    bf16, f32 = jnp.bfloat16, jnp.float32
+    first = 0 if causal else 4
+
+    def columns(count):
+        return pl.BlockSpec((count, 128), lambda i: (0, i))
+
+    def whole(shape):
+        return pl.BlockSpec(shape, lambda i: (0,) * len(shape), pipeline_mode=pl.Buffered(1))
+
+    def weight(unit):
+        return pl.BlockSpec((D, 128), lambda i: (0, unit * (D // 128) + i))
+
+    spec_q, spec_k = columns(rows), columns(keys)
+    in_specs = [pl.BlockSpec(memory_space=pltpu.SMEM), spec_q, spec_k, spec_k, spec_q, spec_q]
+    in_specs += [pl.BlockSpec((1, 8, rows), lambda i: (i, 0, 0)), whole((rows, D)), pl.BlockSpec(memory_space=pl.ANY)]
+    in_specs += [weight(first), weight(first + 1), weight(first + 2)]
+    operands = [block_table, queries, keys_in, values_in, mixed_grad, mixed, lse, left_q, upstream]
+    operands += [wide_full] * 3
+    shape = jax.ShapeDtypeStruct
+    out_specs = [columns(D)] * 3 + [columns(8), whole((rows, D))]
+    out_shape = [shape((D, D), bf16)] * 3 + [shape((8, D), f32), shape((rows, D), bf16 if causal else f32)]
+    scratch = [
+        pltpu.VMEM((2, rows, 128), bf16),
+        pltpu.VMEM((2, rows, 128), bf16),
+        pltpu.VMEM((128, rows), bf16),
+        pltpu.VMEM((128, rows), bf16),
+        pltpu.VMEM((4, rows, 128), f32),
+        pltpu.VMEM((rows, 128), f32),
+        pltpu.VMEM((128, keys), bf16),
+        pltpu.VMEM((128, keys), bf16),
+        pltpu.VMEM((rows, D), f32),
+        pltpu.SemaphoreType.DMA,
+    ]
+    if not causal:
+        states, resid, mixed_self, vec_rows = extra
+        in_specs += [whole((keys, D)), pl.BlockSpec((D, D), lambda i: (0, 3), pipeline_mode=pl.Buffered(1)), whole((rows, D)), whole((rows, D))]
+        in_specs += [whole(vec_rows.shape)]
+        operands += [states, wide_full, resid, mixed_self, vec_rows]
+        out_specs += [whole((keys, D)), whole((rows, D)), whole((D, D)), whole((8, D))]
+        out_shape += [shape((keys, D), bf16), shape((rows, D), bf16), shape((D, D), bf16), shape((8, D), f32)]
+        scratch += [pltpu.VMEM((keys, D), f32), pltpu.VMEM((rows, D), bf16)]
+    params = dict(vmem_limit_bytes=62 << 20)
+    if traffic:
+        in_specs += traffic.in_specs()
+        operands += traffic.operands()
+        out_specs += traffic.out_specs()
+        out_shape += traffic.out_shape()
+        scratch += traffic.scratch()
+        params.update(collective_id=collective_id, has_side_effects=True)
+    return pl.pallas_call(
+        partial(backward_kernel, causal, traffic, table, factor),
+        grid=(D // 128,),
+        in_specs=in_specs,
+        out_specs=out_specs,
+        out_shape=out_shape,
         scratch_shapes=scratch,
-        compiler_params=pltpu.CompilerParams(
-            collective_id=0, has_side_effects=True, vmem_limit_bytes=56 << 20
+        compiler_params=pltpu.CompilerParams(**params),
+        cost_estimate=pl.CostEstimate(
+            flops=(20 if causal else 40) * rows * keys * D, bytes_accessed=4 * queries.size, transcendentals=0
         ),
-    )(*terms, small)
+    )(*operands)
 
 
 def adam_update(master, first, second, gradient, decay_on, rate):
@@ -712,17 +987,19 @@
 
 
 def wide_column(i):
-    return jnp.where(i < 4, i + 8, jnp.where(i < 8, 11, jnp.where(i < 12, i - 4, i - 12)))
+    late = jnp.where(i < 10, i - 4, jnp.where(i == 10, 7, jnp.where(i == 11, 6, jnp.where(i == 12, 3, i - 13))))
+    return jnp.where(i < 4, i + 8, jnp.where(i < 8, 11, late))
 
 
 def narrow_row(i):
     return jnp.clip(i - 4, 0, 3)
 
 
-def adam_kernel(sum_ref, wm, wf, ws, nm, nf, ns, wg, wn, wfn, wsn, wc, ng, nn, nfn, nsn, nc):
+def adam_kernel(in_ref, mid_ref, late_ref, wm, wf, ws, nm, nf, ns, wg, wn, wfn, wsn, wc, ng, nn, nfn, nsn, nc):
     step = pl.program_id(0)
-
-    def update(master, first, second, grad, new, first_new, second_new, copy):
+    rows = in_ref.shape[0]
+
+    def update(sum_ref, master, first, second, grad, new, first_new, second_new, copy):
         def body(r, carry):
             at = pl.ds(pl.multiple_of(r * 32, 32), 32)
             gradient = sum_ref[at, :].astype(jnp.float32)
@@ -736,17 +1013,26 @@
             copy[at, :] = value.astype(jnp.bfloat16)
             return carry
 
-        lax.fori_loop(0, sum_ref.shape[0] // 32, body, 0, unroll=True)
-
-    narrow_step = (step >= 4) & (step < 8)
-
-    @pl.when(jnp.logical_not(narrow_step))
+        lax.fori_loop(0, rows // 32, body, 0, unroll=True)
+
+    wide_refs = (wm, wf, ws, wg, wn, wfn, wsn, wc)
+    narrow_refs = (nm, nf, ns, ng, nn, nfn, nsn, nc)
+
+    @pl.when(step < 4)
     def _():
-        update(wm, wf, ws, wg, wn, wfn, wsn, wc)
-
-    @pl.when(narrow_step)
+        update(in_ref, *wide_refs)
+
+    @pl.when((step == 4) | (step == 5))
     def _():
-        update(nm, nf, ns, ng, nn, nfn, nsn, nc)
+        update(mid_ref, *narrow_refs)
+
+    @pl.when((step == 6) | (step == 7))
+    def _():
+        update(late_ref, *narrow_refs)
+
+    @pl.when(step >= 8)
+    def _():
+        update(late_ref, *wide_refs)
 
 
 def adam_all(sums, wide, narrow):
@@ -761,11 +1047,15 @@
     return pl.pallas_call(
         adam_kernel,
         grid=(16,),
-        in_specs=[pl.BlockSpec((rows, D), lambda i: (i, 0))] + [spec_w] * 3 + [spec_n] * 3,
+        in_specs=[
+            pl.BlockSpec((rows, D), lambda i: (jnp.minimum(i, 3), 0)),
+            pl.BlockSpec((rows, D), lambda i: (jnp.clip(i - 4, 0, 1), 0)),
+            pl.BlockSpec((rows, D), lambda i: (jnp.maximum(i - 6, 0), 0)),
+        ] + [spec_w] * 3 + [spec_n] * 3,
         out_specs=[spec_w] * 5 + [spec_n] * 5,
         out_shape=shapes(wide[0]) + shapes(narrow[0]),
         compiler_params=pltpu.CompilerParams(vmem_limit_bytes=58 << 20),
-    )(sums, *wide, *narrow)
+    )(*sums, *wide, *narrow)
 
 
 def matmul(left, right):
@@ -789,18 +1079,7 @@
     centred = resid - average
     inverse = lax.rsqrt(jnp.mean(centred * centred, axis=-1, keepdims=True) + eps_norm)
     normed = centred * inverse
-    return (normed * gain + shift, normed, inverse)
-
-
-def norm_backward(upstream, normed, inverse, gain):
-    scaled = upstream * gain
-    centred = scaled - jnp.mean(scaled, axis=-1, keepdims=True)
-    resid_grad = inverse * (centred - normed * jnp.mean(scaled * normed, axis=-1, keepdims=True))
-    return (resid_grad, jnp.sum(upstream * normed, axis=0), jnp.sum(upstream, axis=0))
-
-
-def column_sum(matrix):
-    return jnp.sum(matrix.astype(jnp.float32), axis=0)
+    return normed * gain + shift
 
 
 def on_device(
@@ -836,10 +1115,8 @@
     keys_self = joint_proj[:, D : 2 * D].astype(bf16)
     values_self = (joint_proj[:, 2 * D :] + vector[:, 1]).astype(bf16)
     mixed_self, totals_self = attend_forward(queries, keys_self, values_self, block_mask, True)
-    branch_one = matmul(mixed_self, wide_full[:, 3 * D : 4 * D]) + vector[:, 2]
-    normed_one, unit_one, scale_one = norm_forward(
-        tokens.astype(f32) + branch_one, vector[:, 11], vector[:, 14]
-    )
+    resid_one = tokens.astype(f32) + matmul(mixed_self, wide_full[:, 3 * D : 4 * D]) + vector[:, 2]
+    normed_one = norm_forward(resid_one, vector[:, 11], vector[:, 14])
     normed_low = normed_one.astype(bf16)
     cross_queries = (matmul(normed_low, wide_full[:, 4 * D : 5 * D]) + vector[:, 3]).astype(bf16)
     enc_proj = matmul(encoder_states, wide_full[:, 5 * D : 7 * D])
@@ -851,60 +1128,68 @@
     output, grad_two, grad_cross_mix, term_in, term_narrow, term_co, sums = center(
         mixed_cross, normed_one, cotangent, wide_full, narrow_full, vec_rows, factor, shards
     )
-    grad_cq, grad_ck, grad_cv = attend_backward(
-        cross_queries, cross_keys, cross_values, block_mask, False, mixed_cross, totals_cross, grad_cross_mix
-    )
 
     def split(term):
         return term.reshape(shards, -1, D)
 
-    def units(*pairs):
-        return jnp.concatenate(
-            [split((matmul_left(left, right) * factor).astype(bf16)) for left, right in pairs], 1
-        )
-
-    terms = [term_in, split(term_narrow)]
-    terms.append(units((normed_low, grad_cq), (encoder_states, grad_ck)))
-    terms.append(jnp.concatenate([units((encoder_states, grad_cv)), split(term_co)], 1))
-    enc_grad = (
-        matmul_right(grad_ck, wide_full[:, 5 * D : 6 * D]) + matmul_right(grad_cv, wide_full[:, 6 * D : 7 * D])
-    ).astype(bf16)
-    grad_one, gain_one, shift_one = norm_backward(
-        grad_two + matmul_right(grad_cq, wide_full[:, 4 * D : 5 * D]), unit_one, scale_one, vector[:, 11]
-    )
-    grad_self = grad_one.astype(bf16)
-    grad_self_mix = matmul_right(grad_self, wide_full[:, 3 * D : 4 * D]).astype(bf16)
-    grad_q, grad_k, grad_v = attend_backward(
-        queries, keys_self, values_self, block_mask, True, mixed_self, totals_self, grad_self_mix
-    )
-    terms.append(units((tokens, grad_q), (tokens, grad_k)))
-    terms.append(units((tokens, grad_v), (mixed_self, grad_self)))
-    in_grad = (
-        grad_one
-        + matmul_right(grad_q, wide_full[:, :D])
-        + matmul_right(grad_k, wide_full[:, D : 2 * D])
-        + matmul_right(grad_v, wide_full[:, 2 * D : 3 * D])
-    ).astype(bf16)
-    fresh = jnp.zeros((24, D), f32)
-    for row, value in (
-        (0, column_sum(grad_q)),
-        (1, column_sum(grad_v)),
-        (2, column_sum(grad_self)),
-        (3, column_sum(grad_cq)),
-        (4, column_sum(grad_cv)),
-        (11, gain_one),
-        (14, shift_one),
-    ):
-        fresh = fresh.at[row].set(value)
-    term_vec = (sums + fresh) * factor
-    term_vec = term_vec.reshape(24, shards, -1).transpose(1, 0, 2)
-    total, vec_sum = all_summed(terms, term_vec, replicas, shards)
+    carried = shards == 2 and replicas % 4 == 0 and UNIT % (32 * (replicas // 4)) == 0
+    lanes = replicas // 4
+    early = [term_in, split(term_narrow), split(term_co)]
+    traffic = None
+    if carried:
+        places = [(0, UNIT * i, i % 2 == 0) for i in range(4)] + [(1, UNIT * i, i % 2 == 0) for i in range(4)]
+        traffic = Traffic(["both"] * 4 + ["scatter"] * 4, lanes, early[:2], places)
+    found = attend_backward(
+        cross_queries, cross_keys, cross_values, block_mask, False, mixed_cross, totals_cross[0],
+        grad_cross_mix, normed_low, grad_two, wide_full, factor,
+        (encoder_states, resid_one, mixed_self, vec_rows), traffic, CROSS_TABLE, 1,
+    )
+    term_cq, term_ck, term_cv, cross_sums, grad_one, enc_grad, grad_self_mix, term_wo, norm_sums = found[:9]
+    middle = [split(term) for term in (term_cq, term_ck, term_cv, term_wo)]
+    if carried:
+        blocks, sum_in = found[9:]
+        places = [True, False, (0, 0, True), (1, 0, False)]
+        traffic = Traffic(["gather"] * 2 + ["scatter"] * 2, lanes, middle[:2], places, blocks[:2])
+    found = attend_backward(
+        queries, keys_self, values_self, block_mask, True, mixed_self, totals_self[0],
+        grad_self_mix, tokens, grad_one, wide_full, factor, None, traffic, SELF_TABLE, 2,
+    )
+    late = [split(term) for term in found[:3]]
+    self_sums, in_grad = found[3:5]
+    term_vec = jnp.concatenate(
+        [
+            self_sums[0:2],
+            norm_sums[2:3],
+            cross_sums[0:2],
+            sums[5:11],
+            norm_sums[0:1],
+            sums[12:14],
+            norm_sums[1:2],
+            sums[15:],
+        ],
+        0,
+    )
+    term_vec = (term_vec * factor).reshape(24, shards, -1).transpose(1, 0, 2)
+    last = [early[2], middle[2], middle[3]] + late
+    if carried:
+        blocks_self, sum_mid = found[5:]
+        modes = ["gather"] * 4 + ["both"] * 6
+        places = [i % 2 == 0 for i in range(4)] + [(i, 0, i % 2 == 0) for i in range(6)]
+        traffic = Traffic(modes, lanes, last, places, jnp.concatenate([blocks[2:], blocks_self], 0), term_vec)
+        sum_late, vec_sum = run_traffic(traffic, TAIL_ORDER, 0)
+        totals = [sum_in, sum_mid, sum_late]
+    else:
+        narrow_sum = whole_sum(early[1])
+        cut = narrow_sum.shape[0] // 2
+        rest = [narrow_sum[cut:]] + [whole_sum(term) for term in middle[:2] + last]
+        totals = [whole_sum(early[0]), narrow_sum[:cut], jnp.concatenate(rest, 0)]
+        vec_sum = lax.psum(lax.psum_scatter(term_vec, "shard", scatter_dimension=0), "rep")
     vec_grad = vec_sum[: vec_master.shape[1]].T
     (
         wide_grad, wide_new, wide_first_new, wide_second_new, wide_copy,
         narrow_grad, narrow_new, narrow_first_new, narrow_second_new, narrow_copy,
     ) = adam_all(
-        total, (wide_master, wide_first, wide_second), (narrow_master, narrow_first, narrow_second)
+        totals, (wide_master, wide_first, wide_second), (narrow_master, narrow_first, narrow_second)
     )
     vec_new, vec_first_new, vec_second_new = adam_update(
         vec_master, vec_first, vec_second, vec_grad, 0.0, vec_rate
@@ -931,15 +1216,8 @@
     )
 
 
-def all_summed(terms, small, replicas, shards):
-    lanes = replicas // 4
-    if shards == 2 and replicas % 4 == 0 and all(t.shape[1] % (64 * lanes) == 0 for t in terms):
-        return reduce_all(terms, small, lanes)
-
-    def summed(term):
-        return lax.psum(lax.psum_scatter(term, "shard", scatter_dimension=0), "rep")
-
-    return jnp.concatenate([summed(term) for term in terms], 0), summed(small)
+def whole_sum(term):
+    return lax.psum(lax.psum_scatter(term, "shard", scatter_dimension=0), "rep")
 
 
 def solution(mesh):

time: 629 us -> 531 us (0.84)
  matrix products: 69.3 us -> 20.3 us
  Pallas kernels: 453 us -> 424 us
  local copies, waits for them, and re-layouts: 25.4 us -> 15.8 us
  other arithmetic: 32.5 us -> 23.9 us
    dot_general x14 -> x0, matrix products: 48.2 us -> none  [the longest x7 26.4 us: matmul_right(): lax.dot_general(left, right, (((1,), (1,)), ((), ())), preferred_element_...]
    pallas_call x5, Pallas kernels: 335 us -> 306 us  [the longest x2 167 us: attend_backward(): pl.pallas_call(partial(backward_kernel, causal, traffic, table, factor),...]
    convert_element_type x5 -> x0, local copies, waits for them, and re-layouts: 12 us -> none  [units(): (matmul_left(left, right) * factor).astype(bf16)]
  transfers between devices with their start and end apart: 2 -> 2, of which waited for: 1 -> 1; matrix products, arithmetic and copies ran while one was open for 6% -> 7% of each run, Pallas kernels for 7% -> 8%
where the time goes in v3:
time: 531 us; the launch traced here: 524 us
  Pallas kernels  424 us (80%)
  other arithmetic  23.9 us (5%)
  waiting for transfers between devices  22.5 us (4%)
  matrix products  20.3 us (4%)
  local copies, waits for them, and re-layouts  15.8 us (3%)
  between operations  14.8 us (3%)
    pallas_call x2, Pallas kernels, attend_backward(): pl.pallas_call(partial(backward_kernel, causal, traffic, table, factor),...  167 us
    pallas_call x1, Pallas kernels, run_traffic(): pl.pallas_call(partial(traffic_kernel, traffic, order), in_specs=traffic....  98.5 us
    pallas_call x1, Pallas kernels, center(): pl.pallas_call(partial(center_kernel, factor), grid=(8,), in_specs=[whole...  65.5 us
    pallas_call x1, Pallas kernels, adam_all(): pl.pallas_call(adam_kernel, grid=(16,), in_specs=[pl.BlockSpec((rows, D),...  52.7 us
    pallas_call x2, Pallas kernels, attend_forward(): pl.pallas_call(partial(forward_kernel, causal), grid=(seqs, D // 128), in...  40.3 us
    all_gather x2, waiting for transfers between devices, gathered(): return lax.all_gather(part.astype(bf16), 'shard', axis=0, tiled=True)  22.4 us
    dot_general x4, matrix products, matmul(): return jnp.dot(left, right, preferred_element_type=jnp.float32)  20.3 us
    convert_element_type x3, other arithmetic, gathered(): return lax.all_gather(part.astype(bf16), 'shard', axis=0, tiled=True)  13.1 us
  transfers between devices with their start and end apart: 2, of which 1 were waited for; matrix products, arithmetic and copies ran while one was open for 7% of the time, Pallas kernels for 8%

profile of v3, /device:TPU:0, one launch (start us, length us, event | category | flops | bytes accessed | tf_op | source)
XLA Modules:
  0.0 523.7 jit_solution(17192778456300741399)
XLA Ops:
  7.2 0.0 all-gather.3.cloned.1.call-start
  7.2 9.0 %convert_element_type.38 = bf16[384,9216]{1,0:T(8,128)(2,1)} convert(f32[384,9216]{1,0:T(8,128)} %wm.1) | non-fusion elementwise | flops 3538944 | bytes 21233664 | tf_op jit(solution)/shard_map/convert_element_type | solution.py:1107
  16.2 0.0 all-gather.3.cloned.1.call-update
  16.2 0.0 copy-start.12
  16.3 0.0 copy-start.16
  16.3 0.0 all-gather.5.cloned.1.call-start
  16.3 4.1 convert_element_type.46
  20.4 0.0 all-gather.5.cloned.1.call-update
  20.5 1.9 all_gather.10
  22.4 0.1 slice_reduce_fusion
  22.5 0.6 pad.4.vec_ref.refs_16_
  23.1 22.4 %all-gather.3.cloned.1.call-done.co_ref.win_ref.refs_9_.refs_10_.refs_11_.refs_13_ = bf16[768,9216]{1,0:T(8,128)(2,1)} async-done(((bf16[384,9216]{1,0:T(8,128)(2,1)}), bf16[768,9216]{1,0:T(8,128)(2,1)}) %all-gather.3.cloned.1.call-update) | async-done | bytes 14155792 | tf_op jit(solution)/shard_map/all_gather | solution.py:1107
  45.5 5.8 %fusion.1 = f32[1024,2304]{1,0:T(8,128)S(1)} fusion(bf16[1024,768]{1,0:T(8,128)(2,1)S(1)} %copy-done.16, bf16[768,9216]{1,0:T(8,128)(2,1)} %all-gather.3.cloned.1.call-done.co_ref.win_ref.refs_9_.refs_10_.refs_11_.refs_13_), kind=kOutput, calls=%fused_computation.3 | convolution fusion | flops 3623878656 | bytes 14548992 | tf_op jit(solution)/shard_map/dot_general | solution.py:1062
  51.4 0.2 slice.154.k_ref.refs_2_
  51.5 0.0 copy-start
  51.6 0.0 copy-start.2
  51.6 1.7 fusion.3
  53.3 12.3 %shard_map.268 = (bf16[1024,768]{1,0:T(8,128)(2,1)S(1)}, f32[1,6,8,1024]{3,2,1,0:T(8,128)S(1)}) custom-call(s32[1,4,4]{2,1,0:T(4,128)S(1)} %copy-done.2, bf16[1024,768]{1,0:T(8,128)(2,1)S(1)} %get-tuple-element.115.q_ref.refs_1_, bf16[1024,768]{1,0:T(8,128)(2,1)S(1)} %slice.154.k_ref.refs_2_, bf16[1024,768]{1,0:T(8,128)(2,1)} %get-tuple-element.114.v_ref.refs_3_), custom_call_target="tpu_custom_call" | custom-call | flops 6442450944 | bytes 3145728 | tf_op jit(solution)/shard_map/pallas_call | solution.py:182
  65.6 0.0 copy-start.17
  65.7 8.4 %fusion.5 = f32[2048,1536]{1,0:T(8,128)S(1)} fusion(bf16[2048,768]{1,0:T(8,128)(2,1)} %refs_12_.1, bf16[768,9216]{1,0:T(8,128)(2,1)} %all-gather.3.cloned.1.call-done.co_ref.win_ref.refs_9_.refs_10_.refs_11_.refs_13_), kind=kOutput, calls=%fused_computation.14 | convolution fusion | flops 4831838208 | bytes 18087936 | tf_op jit(solution)/shard_map/dot_general | solution.py:1062
  74.1 2.8 fusion.15
  77.0 2.4 slice.153.k_ref.refs_2_
  79.3 0.5 multiply_reduce_fusion
  79.9 2.3 fusion.12
  82.2 3.2 add_convert_fusion.q_ref.refs_1_
  85.4 2.6 fusion.v_ref.refs_3_
  88.0 28.0 %shard_map.269 = (bf16[1024,768]{1,0:T(8,128)(2,1)S(1)}, f32[1,6,8,1024]{3,2,1,0:T(8,128)S(1)}) custom-call(s32[1,4,4]{2,1,0:T(4,128)S(1)} %copy-done.2, bf16[1024,768]{1,0:T(8,128)(2,1)S(1)} %add_convert_fusion.q_ref.refs_1_, bf16[2048,768]{1,0:T(8,128)(2,1)} %slice.153.k_ref.refs_2_, bf16[2048,768]{1,0:T(8,128)(2,1)} %fusion.v_ref.refs_3_), custom_call_target="tpu_custom_call" | custom-call | flops 25769803776 | bytes 3145728 | tf_op jit(solution)/shard_map/pallas_call | solution.py:182
  116.1 0.7 copy-done.4
  116.7 1.1 copy-done.7
  117.9 65.5 %shard_map.270 = (bf16[1024,768]{1,0:T(8,128)(2,1)}, f32[1024,768]{1,0:T(8,128)}, bf16[1024,768]{1,0:T(8,128)(2,1)}, bf16[2,1536,768]{2,1,0:T(8,128)(2,1)}, bf16...) custom-call(bf16[1024,768]{1,0:T(8,128)(2,1)} %copy-done.7, ...), custom_call_target="tpu_custom_call" | custom-call | flops 32614907904 | bytes 31457280 | tf_op jit(solution)/shard_map/pallas_call | solution.py:345
  183.4 0.8 slice.104
  184.2 0.7 slice.106
  184.9 0.8 slice.108
  185.7 114.0 %shard_map.271 = (bf16[768,768]{1,0:T(8,128)(2,1)}, bf16[768,768]{1,0:T(8,128)(2,1)}, bf16[768,768]{1,0:T(8,128)(2,1)}, f32[8,768]{1,0:T(8,128)}, f32[1024,768]{...) custom-call(s32[1,4,4]{2,1,0:T(4,128)} %refs_0_.3, ...), custom_call_target="tpu_custom_call" | custom-call | flops 64424509440 | bytes 3145728 | tf_op jit(solution)/shard_map/pallas_call | solution.py:966
  299.8 1.6 fusion.13
  301.3 53.3 %shard_map.272 = (bf16[768,768]{1,0:T(8,128)(2,1)}, bf16[768,768]{1,0:T(8,128)(2,1)}, bf16[768,768]{1,0:T(8,128)(2,1)}, f32[8,768]{1,0:T(8,128)}, bf16[1024,768]...) custom-call(s32[1,4,4]{2,1,0:T(4,128)} %refs_0_.3, bf16[1024,768]{1,0:T(8,128)(2,1)} %copy-done.1, ...), custom_call_target="tpu_custom_call" | custom-call | flops 16106127360 | bytes 3145728 | tf_op jit(solution)/shard_map/pallas_call | solution.py:966
  354.6 0.7 slice.101
  355.4 0.9 fusion.14
  356.3 0.7 slice.103
  357.0 0.3 concatenate.32
  357.3 0.6 multiply_bitcast_fusion.refs_7_
  358.0 1.6 pad_maximum_fusion.refs_6_
  359.5 98.5 %shard_map.273 = (bf16[3840,768]{1,0:T(8,128)(2,1)}, f32[24,384]{1,0:T(8,128)}) custom-call(bf16[2,384,768]{2,1,0:T(8,128)(2,1)} %bitcast.31, bf16[2,384,768]{2,1,0:T(8,128)(2,1)} %bitcast.32, bf16[2,384,768]{2,1,0:T(8,128)(2,1)} %bitcast.33, bf16[2,384,768]{2,1,0:T(8,128)(2,1)} %bitcast.34, bf16[2,384,768]{2,1,0:T(8,128)(2,1)} %bitcast.35, ...), custom_call_target="tpu_custom_call" | custom-call | tf_op jit(solution)/shard_map/pallas_call | solution.py:721
  458.1 1.4 fusion.10
  459.5 52.7 %shard_map.274 = (f32[384,9216]{1,0:T(8,128)}, f32[384,9216]{1,0:T(8,128)}, f32[384,9216]{1,0:T(8,128)}, f32[384,9216]{1,0:T(8,128)}, bf16[384,9216]{1,0:T(8,128...) custom-call(bf16[1536,768]{1,0:T(8,128)(2,1)} %get-tuple-element.75., ...), custom_call_target="tpu_custom_call" | custom-call | tf_op jit(solution)/shard_map/pallas_call | solution.py:1047
  512.3 1.1 copy.37
  513.4 1.3 copy-done.9
  514.7 1.7 copy.38
  (35 shorter events, 0.1 us)
Async XLA Ops:
  7.2 38.4 %all-gather.3.cloned.1.call-start = ((), (), s32[]{:S(2)}) async-start(), calls=%async_computation | async-start | bytes 21233664 | tf_op jit(solution)/shard_map/all_gather | solution.py:1107
  16.2 4.2 copy-start.12
  16.3 29.3 %copy-start.16 = (bf16[1024,768]{1,0:T(8,128)(2,1)S(1)}, bf16[1024,768]{1,0:T(8,128)(2,1)}, u32[]{:S(2)}) copy-start(bf16[1024,768]{1,0:T(8,128)(2,1)} %refs_7_.1) | copy-start | bytes 4718596
  16.3 101.6 %all-gather.5.cloned.1.call-start = ((), (), s32[]{:S(2)}) async-start(), calls=%async_computation.1 | async-start | bytes 7077888 | tf_op jit(solution)/shard_map/all_gather | solution.py:1107
  51.5 1.8 copy-start
  51.6 1.8 copy-start.2
  53.3 12.3 %copy-start.1 = (bf16[1024,768]{1,0:T(8,128)(2,1)}, bf16[1024,768]{1,0:T(8,128)(2,1)S(1)}, u32[]{:S(2)}) copy-start(bf16[1024,768]{1,0:T(8,128)(2,1)S(1)} %get-tuple-element.115.q_ref.refs_1_) | copy-start | bytes 4718596
  65.6 8.5 %copy-start.3 = (f32[1,6,8,1024]{3,2,1,0:T(8,128)}, f32[1,6,8,1024]{3,2,1,0:T(8,128)S(1)}, u32[]{:S(2)}) copy-start(f32[1,6,8,1024]{3,2,1,0:T(8,128)S(1)} %get-tuple-element.68) | copy-start | bytes 589828
  65.6 8.5 %copy-start.5 = (bf16[1024,768]{1,0:T(8,128)(2,1)}, bf16[1024,768]{1,0:T(8,128)(2,1)S(1)}, u32[]{:S(2)}) copy-start(bf16[1024,768]{1,0:T(8,128)(2,1)S(1)} %get-tuple-element.59.refs_15_.refs_5_) | copy-start | bytes 4718596
  65.6 8.5 %copy-start.17 = (bf16[1024,768]{1,0:T(8,128)(2,1)S(1)}, bf16[1024,768]{1,0:T(8,128)(2,1)}, u32[]{:S(2)}) copy-start(bf16[1024,768]{1,0:T(8,128)(2,1)} %refs_7_.1) | copy-start | bytes 4718596
  76.9 2.9 copy-start.8
  82.2 3.2 copy-start.11
  85.4 2.6 copy-start.6
  116.0 0.7 copy-start.4
  116.7 1.1 copy-start.7
  359.5 98.5 %copy-start.13 = (f32[384,17]{0,1:T(8,128)S(1)}, f32[384,17]{0,1:T(8,128)}, u32[]{:S(2)}) copy-start(f32[384,17]{0,1:T(8,128)} %param.19) | copy-start | bytes 78340
  359.5 98.5 %copy-start.14 = (f32[384,17]{0,1:T(8,128)S(1)}, f32[384,17]{0,1:T(8,128)}, u32[]{:S(2)}) copy-start(f32[384,17]{0,1:T(8,128)} %param.22) | copy-start | bytes 78340
  359.5 98.5 %copy-start.15 = (f32[384,17]{0,1:T(8,128)S(1)}, f32[384,17]{0,1:T(8,128)}, u32[]{:S(2)}) copy-start(f32[384,17]{0,1:T(8,128)} %param.25) | copy-start | bytes 78340
  459.5 52.8 %copy-start.10 = (bf16[1024,768]{1,0:T(8,128)(2,1)S(1)}, bf16[1024,768]{1,0:T(8,128)(2,1)}, u32[]{:S(2)}) copy-start(bf16[1024,768]{1,0:T(8,128)(2,1)} %get-tuple-element.144) | copy-start | bytes 4718596
  512.3 2.5 copy-start.9
Sparse Core Ops, SparseCore 0:
  16.4 29.1 all-gather.2
  47.7 15.6 all-gather.4

commit v4 on v3

--- a/solution.py
+++ b/solution.py
@@ -27,29 +27,39 @@
 masked_score = -1e30
 FACTOR = HD ** (-0.5)
 SCALE2 = FACTOR / math.log(2.0)
+WIDE_UNITS = 12
+ALL_UNITS = 16
+N_BOTH = 4
+N_SCATTER = 4
+N_GATHER = 2
+N_MIDDLE = 2
 
 
 CROSS_TABLE = {
-    (0, 1): ((0, 0), (1, 0), (2, 0), (3, 0)),
-    (0, 7): ((0, 1), (1, 1), (2, 1), (3, 1)),
-    (1, 7): ((0, 2), (1, 2), (2, 2), (3, 2)),
-    (1, 13): ((4, 0), (5, 0), (6, 0), (7, 0)),
-    (2, 7): ((0, 3), (1, 3), (2, 3), (3, 3), (4, 1), (5, 1), (6, 1), (7, 1)),
-    (3, 7): ((0, 4), (1, 4), (2, 4), (3, 4), (4, 2), (5, 2), (6, 2), (7, 2)),
-    (4, 7): ((0, 5), (1, 5), (2, 5), (3, 5), (4, 3), (5, 3), (6, 3), (7, 3)),
-    (5, 7): ((0, 6), (1, 6), (2, 6), (3, 6), (4, 4), (5, 4), (6, 4), (7, 4)),
-    (5, 13): ((0, 7), (1, 7), (2, 7), (3, 7), (0, 8), (1, 8), (2, 8), (3, 8)),
+    (0, 0): ((0, 0), (1, 0), (2, 0), (3, 0)),
+    (0, 9): ((0, 1), (1, 1), (2, 1), (3, 1)),
+    (1, 9): ((0, 2), (1, 2), (2, 2), (3, 2)),
+    (2, 0): ((4, 0), (5, 0), (6, 0), (7, 0)),
+    (2, 5): ((0, 3), (1, 3), (2, 3), (3, 3)),
+    (2, 9): ((4, 1), (5, 1), (6, 1), (7, 1)),
+    (3, 5): ((0, 4), (1, 4), (2, 4), (3, 4)),
+    (3, 9): ((4, 2), (5, 2), (6, 2), (7, 2)),
+    (4, 5): ((0, 5), (1, 5), (2, 5), (3, 5), (4, 3), (5, 3), (6, 3), (7, 3)),
+    (5, 0): ((0, 6), (1, 6), (2, 6), (3, 6)),
+    (5, 5): ((4, 4), (5, 4), (6, 4), (7, 4)),
+    (5, 9): ((0, 7), (1, 7), (2, 7), (3, 7), (0, 8), (1, 8), (2, 8), (3, 8)),
 }
 
 
 SELF_TABLE = {
-    (0, 1): ((0, 0), (1, 0), (2, 0), (3, 0)),
-    (0, 5): ((2, 1), (3, 1)),
+    (0, 0): ((0, 0), (1, 0), (2, 0), (3, 0)),
+    (0, 8): ((2, 1), (3, 1)),
     (1, 3): ((0, 1), (1, 1)),
-    (2, 3): ((0, 2), (1, 2), (2, 2), (3, 2)),
-    (3, 5): ((2, 3), (3, 3)),
-    (4, 3): ((0, 3), (1, 3)),
-    (4, 8): ((0, 4), (1, 4), (2, 4), (3, 4)),
+    (2, 8): ((0, 2), (1, 2), (2, 2), (3, 2)),
+    (4, 3): ((2, 3), (3, 3)),
+    (4, 8): ((0, 3), (1, 3)),
+    (5, 3): ((0, 4), (1, 4)),
+    (5, 8): ((2, 4), (3, 4)),
 }
 
 
@@ -58,12 +68,11 @@
     (5, 1), (4, 2), (10, 1), (5, 2), (6, 0), (7, 0), (0, 1), (1, 1),
     (2, 1), (3, 1), (6, 1), (7, 1), (10, 2), (4, 3), (5, 3), (0, 2),
     (1, 2), (2, 2), (3, 2), (8, 0), (9, 0), (4, 4), (10, 3), (5, 4),
-    (8, 1), (9, 1), (6, 2), (7, 2), (4, 5), (5, 5), (6, 3), (7, 3),
-    (10, 4), (0, 3), (1, 3), (2, 3), (3, 3), (4, 6), (5, 6), (8, 2),
-    (9, 2), (0, 4), (1, 4), (2, 4), (3, 4), (6, 4), (7, 4), (8, 3),
-    (9, 3), (4, 7), (5, 7), (4, 8), (5, 8), (6, 5), (7, 5), (8, 4),
-    (9, 4), (6, 6), (7, 6), (8, 5), (9, 5), (6, 7), (7, 7), (6, 8),
-    (7, 8), (8, 6), (9, 6), (8, 7), (9, 7), (8, 8), (9, 8),
+    (0, 3), (1, 3), (2, 3), (3, 3), (6, 2), (7, 2), (8, 1), (9, 1),
+    (10, 4), (4, 5), (5, 5), (6, 3), (7, 3), (8, 2), (9, 2), (4, 6),
+    (5, 6), (6, 4), (7, 4), (4, 7), (5, 7), (8, 3), (9, 3), (6, 5),
+    (7, 5), (8, 4), (9, 4), (6, 6), (7, 6), (6, 7), (7, 7), (8, 5),
+    (9, 5), (8, 6), (9, 6), (8, 7), (9, 7),
 )
 
 
@@ -86,10 +95,22 @@
     )
 
 
-def forward_kernel(causal, mask_ref, q_ref, k_ref, v_ref, o_ref, lse_ref, qm_ref, vt_ref, acc_ref, sum_ref, top_ref):
+def forward_kernel(
+    causal, mask_ref, left_q_ref, left_k_ref, wq_ref, wk_ref, wv_ref, vec_ref,
+    o_ref, lse_ref, q_ref, k_ref, v_ref, qm_ref, vt_ref, acc_ref, sum_ref, top_ref,
+):
     rows, keys = q_ref.shape[0], k_ref.shape[0]
     tile = BLK
-    seq = pl.program_id(0)
+    bias_q, bias_v = (vec_ref[0:1, :], vec_ref[1:2, :]) if causal else (vec_ref[3:4, :], vec_ref[4:5, :])
+    weights = jnp.concatenate([wk_ref[...], wv_ref[...]], axis=1)
+    for at in range(0, rows, 2 * BLK):
+        here = slice(at, at + 2 * BLK)
+        q_ref[here, :] = (rows_dot(left_q_ref[here, :], wq_ref[...]) + bias_q).astype(jnp.bfloat16)
+    for at in range(0, keys, 2 * BLK):
+        here = slice(at, at + 2 * BLK)
+        both = rows_dot(left_k_ref[here, :], weights)
+        k_ref[here, :] = both[:, :128].astype(jnp.bfloat16)
+        v_ref[here, :] = (both[:, 128:] + bias_v).astype(jnp.bfloat16)
     queries = q_ref[...]
     for head, mask in enumerate(head_masks(rows)):
         qm_ref[head] = keep(mask, queries)
@@ -108,7 +129,7 @@
         if causal:
             pieces = [jnp.where(below, scores[:, :BLK], masked_score)]
             for i in range(j + 1, rows // BLK):
-                off = jnp.where(mask_ref[seq, i, j] > 0, 0.0, masked_score)
+                off = jnp.where(mask_ref[0, i, j] > 0, 0.0, masked_score)
                 pieces.append(scores[:, (i - j) * BLK : (i - j + 1) * BLK] + off)
             scores = jnp.concatenate(pieces, axis=1)
         return scores
@@ -136,7 +157,7 @@
             lse = jnp.log2(total)
             if shifts is not None:
                 lse = lse + shifts[head]
-            lse_ref[0, 0, head : head + 1, :] = lse
+            lse_ref[0, head : head + 1, :] = lse
             both.append(acc_ref[head] * (1.0 / total))
         o_ref[...] = jnp.concatenate(both, axis=0).T.astype(jnp.bfloat16)
 
@@ -172,37 +193,50 @@
         finish(shifts)
 
 
-def attend_forward(queries, keys_in, values_in, block_table, causal):
-    seqs = block_table.shape[0]
-    rows, keys = queries.shape[0] // seqs, keys_in.shape[0] // seqs
-    spec_q = pl.BlockSpec((rows, 128), lambda s, i: (s, i))
-    spec_k = pl.BlockSpec((keys, 128), lambda s, i: (s, i))
-    spec_l = pl.BlockSpec((1, 1, 8, rows), lambda s, i: (s, i, 0, 0))
-    area = rows * keys * H * HD * seqs
+def attend_forward(left_q, left_k, block_table, wide_full, vec_rows, causal):
+    rows, keys = left_q.shape[0], left_k.shape[0]
+    first = 0 if causal else 4
+    bf16, f32 = jnp.bfloat16, jnp.float32
+
+    def columns(count):
+        return pl.BlockSpec((count, 128), lambda i: (0, i))
+
+    def whole(count):
+        return pl.BlockSpec((count, D), lambda i: (0, 0), pipeline_mode=pl.Buffered(1))
+
+    def weight(unit):
+        return pl.BlockSpec((D, 128), lambda i: (0, unit * (D // 128) + i))
+
     return pl.pallas_call(
         partial(forward_kernel, causal),
-        grid=(seqs, D // 128),
-        in_specs=[pl.BlockSpec(memory_space=pltpu.SMEM), spec_q, spec_k, spec_k],
-        out_specs=[spec_q, spec_l],
+        grid=(D // 128,),
+        in_specs=[pl.BlockSpec(memory_space=pltpu.SMEM), whole(rows), whole(keys)]
+        + [weight(first), weight(first + 1), weight(first + 2), columns(vec_rows.shape[0])],
+        out_specs=[columns(rows), pl.BlockSpec((1, 8, rows), lambda i: (i, 0, 0)), columns(rows)]
+        + [columns(keys)] * 2,
+        out_shape=[
+            jax.ShapeDtypeStruct((rows, D), bf16),
+            jax.ShapeDtypeStruct((D // 128, 8, rows), f32),
+            jax.ShapeDtypeStruct((rows, D), bf16),
+            jax.ShapeDtypeStruct((keys, D), bf16),
+            jax.ShapeDtypeStruct((keys, D), bf16),
+        ],
         scratch_shapes=[
-            pltpu.VMEM((2, rows, 128), jnp.bfloat16),
-            pltpu.VMEM((128, keys), jnp.bfloat16),
-            pltpu.VMEM((2, HD, rows), jnp.float32),
-            pltpu.VMEM((2, rows), jnp.float32),
-            pltpu.VMEM((2, rows), jnp.float32),
-        ],
-        out_shape=[
-            jax.ShapeDtypeStruct(queries.shape, jnp.bfloat16),
-            jax.ShapeDtypeStruct((seqs, D // 128, 8, rows), jnp.float32),
+            pltpu.VMEM((2, rows, 128), bf16),
+            pltpu.VMEM((128, keys), bf16),
+            pltpu.VMEM((2, HD, rows), f32),
+            pltpu.VMEM((2, rows), f32),
+            pltpu.VMEM((2, rows), f32),
         ],
         compiler_params=pltpu.CompilerParams(vmem_limit_bytes=48 << 20),
         cost_estimate=pl.CostEstimate(
-            flops=(8 if causal else 16) * area, bytes_accessed=4 * queries.size, transcendentals=0
+            flops=(8 if causal else 16) * rows * keys * D, bytes_accessed=4 * left_q.size, transcendentals=0
         ),
-    )(block_table, queries, keys_in, values_in)
+    )(block_table, left_q, left_k, wide_full, wide_full, wide_full, vec_rows)
 
 
 ROWS = 256
+UNROLL = 4
 
 
 def gelu_pair(x):
@@ -253,7 +287,7 @@
             body(pl.ds(pl.multiple_of(r * ROWS, ROWS), ROWS))
             return carry
 
-        lax.fori_loop(0, blocks, run, 0)
+        lax.fori_loop(0, blocks, run, 0, unroll=UNROLL)
 
     @pl.when(step == 0)
     def _():
@@ -485,10 +519,10 @@
 
         def body(i, carry):
             at = pl.ds(aligned(i * block), block)
-            acc[at, :] = (acc[at, :].astype(f32) + got[at, :].astype(f32)).astype(bf16)
+            acc[at, :] = acc[at, :] + got[at, :]
             return carry
 
-        lax.fori_loop(0, UNIT // block, body, 0)
+        lax.fori_loop(0, UNIT // block, body, 0, unroll=True)
         to_a.start()
 
     def step_b():
@@ -496,10 +530,10 @@
 
         def body(i, carry):
             at = pl.ds(aligned(i * block), block)
-            acc[at, mine_cols] = (acc[at, mine_cols].astype(f32) + got_a[at, :].astype(f32)).astype(bf16)
+            acc[at, mine_cols] = acc[at, mine_cols] + got_a[at, :]
             return carry
 
-        lax.fori_loop(0, UNIT // block, body, 0)
+        lax.fori_loop(0, UNIT // block, body, 0, unroll=True)
         to_b.start()
 
     def step_z():
@@ -507,11 +541,10 @@
 
         def body(i, carry):
             at = pl.ds(aligned(mine_b + i * block), block)
-            other = got_b[pl.ds(aligned(i * block), block), :].astype(f32)
-            acc[at, mine_cols] = (acc[at, mine_cols].astype(f32) + other).astype(bf16)
+            acc[at, mine_cols] = acc[at, mine_cols] + got_b[pl.ds(aligned(i * block), block), :]
             return carry
 
-        lax.fori_loop(0, half_rows // block, body, 0)
+        lax.fori_loop(0, half_rows // block, body, 0, unroll=True)
         for copy in to_z:
             copy.start()
 
@@ -528,7 +561,7 @@
     return [start, step_a, step_b, step_z, step_own]
 
 
-def gather_steps(block_in, sum_out, scratch, x_first, lanes):
+def gather_steps(block_in, sum_out, scratch, x_first, lanes, entire):
     full, block_ref = scratch[:2]
     sems, local_sem = scratch[-3:-1], scratch[-1]
     shard, z, here_a, here_b, sibling, peer_a, peer_b, others = unit_places(x_first, lanes)
@@ -537,11 +570,11 @@
     mine_b = aligned(here_b * half_rows)
     mine_z = full.at[pl.ds(aligned(mine_b + z * block), block), mine_cols]
     mine_half = full.at[pl.ds(mine_b, half_rows), mine_cols]
-    mine_all = full.at[:, mine_cols]
     all_z = [remote_copy(sems, 5 + lanes + k, mine_z, mine_z, peer) for k, peer in enumerate(others)]
     all_b = remote_copy(sems, 3, mine_half, mine_half, peer_b)
+    mine_all = full.at[:, mine_cols]
     all_a = remote_copy(sems, 4, mine_all, mine_all, peer_a)
-    store = pltpu.make_async_copy(full, sum_out, local_sem.at[1])
+    store = pltpu.make_async_copy(full if entire else mine_all, sum_out, local_sem.at[1])
 
     def start():
         source = block_ref if block_in is None else block_in
@@ -559,10 +592,10 @@
         all_a.start()
 
     def step_store():
-        all_a.wait()
+        (all_a if entire else all_b).wait()
         store.start()
 
-    return [start, step_b, step_a, step_store, store.wait]
+    return [start, step_b] + [step_a] * entire + [step_store, store.wait]
 
 
 def joined_steps(scatter, gather):
@@ -623,16 +656,16 @@
 
 
 class Traffic:
-    def __init__(self, modes, lanes, terms=(), places=(), blocks=None, small=None):
-        self.modes, self.lanes, self.terms, self.places = modes, lanes, list(terms), list(places)
+    def __init__(self, items, lanes, entire, terms=(), blocks=None, small=None):
+        self.items, self.lanes, self.entire, self.terms = items, lanes, entire, list(terms)
         self.blocks, self.small = blocks, small
-        self.n_scatter = sum(mode == "scatter" for mode in modes)
-        self.n_sum = len(modes) - self.n_scatter
+        self.n_scatter = sum(item[0] == "scatter" for item in items)
+        summed = [item for item in items if item[0] != "scatter"]
+        self.n_x = len(summed) if entire else sum(item[1] for item in summed)
+        self.n_y = len(summed) - self.n_x
 
     def operands(self):
-        return self.terms + ([self.blocks] if self.blocks is not None else []) + (
-            [self.small] if self.small is not None else []
-        )
+        return self.terms + [x for x in (self.blocks, self.small) if x is not None]
 
     def in_specs(self):
         vmem = pl.BlockSpec(memory_space=pltpu.VMEM)
@@ -640,70 +673,66 @@
             (self.blocks is not None) + (self.small is not None)
         )
 
+    def outputs(self):
+        vmem, anywhere = pl.BlockSpec(memory_space=pltpu.VMEM), pl.BlockSpec(memory_space=pl.ANY)
+        shape, bf16 = jax.ShapeDtypeStruct, jnp.bfloat16
+        found = []
+        if self.n_scatter:
+            found.append((vmem, shape((self.n_scatter, UNIT // (2 * self.lanes), HALF), bf16)))
+        for count in (self.n_x, self.n_y):
+            if count:
+                found.append((anywhere, shape((count, UNIT, D if self.entire else HALF), bf16)))
+        if self.small is not None:
+            found.append((vmem, shape(self.small.shape[1:], jnp.float32)))
+        return found
+
     def out_specs(self):
-        specs = []
-        if self.n_scatter:
-            specs.append(pl.BlockSpec(memory_space=pltpu.VMEM))
-        if self.n_sum:
-            specs.append(pl.BlockSpec(memory_space=pl.ANY))
-        if self.small is not None:
-            specs.append(pl.BlockSpec(memory_space=pltpu.VMEM))
-        return specs
+        return [spec for spec, _ in self.outputs()]
 
     def out_shape(self):
-        shapes = []
-        if self.n_scatter:
-            shapes.append(
-                jax.ShapeDtypeStruct((self.n_scatter, UNIT // (2 * self.lanes), HALF), jnp.bfloat16)
-            )
-        if self.n_sum:
-            shapes.append(jax.ShapeDtypeStruct((self.n_sum * UNIT, D), jnp.bfloat16))
-        if self.small is not None:
-            shapes.append(jax.ShapeDtypeStruct(self.small.shape[1:], jnp.float32))
-        return shapes
+        return [shape for _, shape in self.outputs()]
 
     def scratch(self):
         shapes = []
-        for mode in self.modes:
-            shapes += unit_scratch(mode, self.lanes)
+        for item in self.items:
+            shapes += unit_scratch(item[0], self.lanes)
         if self.small is not None:
             shapes += small_scratch(self.small.shape[1:], self.lanes)
         return shapes
 
+    def unpack(self, outs):
+        outs = list(outs)
+        blocks = outs.pop(0) if self.n_scatter else None
+        halves = [outs.pop(0) if count else None for count in (self.n_x, self.n_y)]
+        return blocks, halves, outs.pop(0) if self.small is not None else None
+
     def steps(self, ins, outs, scratch):
-        ins, outs, scratch = list(ins), list(outs), list(scratch)
+        ins, scratch = list(ins), list(scratch)
         terms = [ins.pop(0) for _ in self.terms]
         blocks = ins.pop(0) if self.blocks is not None else None
         small = ins.pop(0) if self.small is not None else None
-        block_out = outs.pop(0) if self.n_scatter else None
-        sum_out = outs.pop(0) if self.n_sum else None
-        small_out = outs.pop(0) if small is not None else None
+        block_out, halves, small_out = self.unpack(outs)
         found = []
-        n_block = n_sum = n_in = n_place = 0
-        for i, mode in enumerate(self.modes):
+        n_block, n_in, n_half = 0, 0, [0, 0]
+        for mode, x_first, which, row in self.items:
             count = len(unit_scratch(mode, self.lanes))
             mine, scratch = scratch[:count], scratch[count:]
-            x_first = None
+            scatter, gather = [], []
             if mode != "gather":
-                which, row, x_first = self.places[n_place]
                 target = block_out.at[n_block] if mode == "scatter" else None
                 scatter = scatter_steps(terms[which], row, mine, x_first, self.lanes, target)
                 n_block += mode == "scatter"
-            else:
-                x_first = self.places[n_place]
-            n_place += 1
             if mode != "scatter":
                 source = None
                 if mode == "gather":
                     source = blocks.at[n_in]
                     n_in += 1
+                kind = 0 if self.entire or x_first else 1
                 gather = gather_steps(
-                    source, sum_out.at[pl.ds(n_sum * UNIT, UNIT)], mine, x_first, self.lanes
+                    source, halves[kind].at[n_half[kind]], mine, x_first, self.lanes, self.entire
                 )
-                n_sum += 1
-            found.append(
-                scatter if mode == "scatter" else gather if mode == "gather" else joined_steps(scatter, gather)
-            )
+                n_half[kind] += 1
+            found.append(joined_steps(scatter, gather) if mode == "both" else scatter + gather)
         if small is not None:
             found.append(small_steps(small, small_out, scratch, self.lanes))
         return found
@@ -728,6 +757,76 @@
             collective_id=collective_id, has_side_effects=True, vmem_limit_bytes=58 << 20
         ),
     )(*traffic.operands())
+
+
+def gather_kernel(wide_ref, narrow_ref, wide_out, narrow_out, held, send_sem, recv_sem, local_sem):
+    step = pl.program_id(0)
+    rep, shard = lax.axis_index("rep"), lax.axis_index("shard")
+    sibling = (rep, 1 - shard)
+
+    @pl.when(step == 0)
+    def _():
+        barrier = pltpu.get_barrier_semaphore()
+        pl.semaphore_signal(barrier, inc=1, device_id=sibling, device_id_type=MESH_ID)
+        pl.semaphore_wait(barrier, 1)
+
+    def copies(unit, target):
+        local = pltpu.make_async_copy(held.at[unit], target, local_sem.at[unit])
+        return local, remote_copy((send_sem, recv_sem), unit, held.at[unit], target, sibling)
+
+    def wide_copies(unit):
+        target = wide_out.at[
+            pl.ds(aligned(shard * UNIT), UNIT), pl.ds(aligned(unit * D, 128), D)
+        ]
+        return copies(unit, target)
+
+    def narrow_copies(unit):
+        row = aligned(shard * (FF // 2) + (unit - WIDE_UNITS) * UNIT)
+        return copies(unit, narrow_out.at[pl.ds(row, UNIT)])
+
+    @pl.when(step < WIDE_UNITS)
+    def _():
+        held[step] = wide_ref[...].astype(jnp.bfloat16)
+        for copy in wide_copies(step):
+            copy.start()
+
+    @pl.when(step >= WIDE_UNITS)
+    def _():
+        held[step] = narrow_ref[...].astype(jnp.bfloat16)
+        for copy in narrow_copies(step):
+            copy.start()
+
+    @pl.when(step == ALL_UNITS - 1)
+    def _():
+        for unit in range(ALL_UNITS):
+            for copy in wide_copies(unit) if unit < WIDE_UNITS else narrow_copies(unit):
+                copy.wait()
+
+
+def gather_weights(wide_master, narrow_master):
+    bf16 = jnp.bfloat16
+    return pl.pallas_call(
+        gather_kernel,
+        grid=(ALL_UNITS,),
+        in_specs=[
+            pl.BlockSpec((UNIT, D), lambda i: (0, jnp.minimum(i, WIDE_UNITS - 1))),
+            pl.BlockSpec((UNIT, D), lambda i: (jnp.maximum(i - WIDE_UNITS, 0), 0)),
+        ],
+        out_specs=[pl.BlockSpec(memory_space=pl.ANY)] * 2,
+        out_shape=[
+            jax.ShapeDtypeStruct((D, wide_master.shape[1]), bf16),
+            jax.ShapeDtypeStruct((FF, D), bf16),
+        ],
+        scratch_shapes=[
+            pltpu.VMEM((ALL_UNITS, UNIT, D), bf16),
+            pltpu.SemaphoreType.DMA((ALL_UNITS,)),
+            pltpu.SemaphoreType.DMA((ALL_UNITS,)),
+            pltpu.SemaphoreType.DMA((ALL_UNITS,)),
+        ],
+        compiler_params=pltpu.CompilerParams(
+            collective_id=3, has_side_effects=True, vmem_limit_bytes=40 << 20
+        ),
+    )(wide_master, narrow_master)
 
 
 def backward_kernel(causal, traffic, table, factor, *refs):
@@ -774,7 +873,7 @@
             body(pl.ds(pl.multiple_of(r * size, size), size))
             return carry
 
-        lax.fori_loop(0, count // size, run, 0)
+        lax.fori_loop(0, count // size, run, 0, unroll=True)
 
     hook()
 
@@ -986,23 +1085,17 @@
     return (master_new, first_new, second_new)
 
 
-def wide_column(i):
-    late = jnp.where(i < 10, i - 4, jnp.where(i == 10, 7, jnp.where(i == 11, 6, jnp.where(i == 12, 3, i - 13))))
-    return jnp.where(i < 4, i + 8, jnp.where(i < 8, 11, late))
-
-
-def narrow_row(i):
-    return jnp.clip(i - 4, 0, 3)
-
-
-def adam_kernel(in_ref, mid_ref, late_ref, wm, wf, ws, nm, nf, ns, wg, wn, wfn, wsn, wc, ng, nn, nfn, nsn, nc):
+def adam_kernel(spans, aliased, table_ref, *refs):
     step = pl.program_id(0)
-    rows = in_ref.shape[0]
+    count = 1 + max(span[0] for span in spans)
+    sums = refs[:count]
+    masters = refs[count : count + 6]
+    outs = refs[count + 6 + aliased :]
 
     def update(sum_ref, master, first, second, grad, new, first_new, second_new, copy):
         def body(r, carry):
             at = pl.ds(pl.multiple_of(r * 32, 32), 32)
-            gradient = sum_ref[at, :].astype(jnp.float32)
+            gradient = sum_ref[0, at, :].astype(jnp.float32)
             grad[at, :] = gradient
             value, one, two = adam_update(
                 master[at, :], first[at, :], second[at, :], gradient, weight_decay, learn_rate
@@ -1013,49 +1106,85 @@
             copy[at, :] = value.astype(jnp.bfloat16)
             return carry
 
-        lax.fori_loop(0, rows // 32, body, 0, unroll=True)
-
-    wide_refs = (wm, wf, ws, wg, wn, wfn, wsn, wc)
-    narrow_refs = (nm, nf, ns, ng, nn, nfn, nsn, nc)
-
-    @pl.when(step < 4)
-    def _():
-        update(in_ref, *wide_refs)
-
-    @pl.when((step == 4) | (step == 5))
-    def _():
-        update(mid_ref, *narrow_refs)
-
-    @pl.when((step == 6) | (step == 7))
-    def _():
-        update(late_ref, *narrow_refs)
-
-    @pl.when(step >= 8)
-    def _():
-        update(late_ref, *wide_refs)
-
-
-def adam_all(sums, wide, narrow):
-    rows = wide[0].shape[0]
-    spec_w = pl.BlockSpec((rows, D), lambda i: (0, wide_column(i)))
-    spec_n = pl.BlockSpec((rows, D), lambda i: (narrow_row(i), 0))
+        lax.fori_loop(0, UNIT // 32, body, 0, unroll=3)
+
+    for which, begin, end, wide in spans:
+
+        @pl.when((step >= begin) & (step < end))
+        def _():
+            if wide:
+                update(sums[which], *masters[:3], *outs[:5])
+            else:
+                update(sums[which], *masters[3:], *outs[5:])
+
+
+def adam_halves(parts, x, y, wide, narrow, before):
+    spans, starts, wides, narrow_rows, narrow_cols = [], [], [], [], []
+    step = 0
+    for which, (array, names, by_x, own) in enumerate(parts):
+        starts.append(step)
+        here = x if by_x else y
+        entire = array.shape[2] == D
+        for k, (kind, index) in enumerate([n for n in names for _ in range(1 + entire)]):
+            half = k % 2 if entire else here if own else 1 - here
+            is_wide = kind == "wide"
+            if spans and spans[-1][0] == which and spans[-1][3] == is_wide:
+                spans[-1] = (which, spans[-1][1], step + 1, is_wide)
+            else:
+                spans.append((which, step, step + 1, is_wide))
+            wides.append(2 * index + half if is_wide else None)
+            narrow_rows.append(None if is_wide else index)
+            narrow_cols.append(None if is_wide else half)
+            step += 1
+
+    def filled(values):
+        last = next((v for v in values if v is not None), 0)
+        found = []
+        for v in values:
+            last = last if v is None else v
+            found.append(jnp.asarray(last, jnp.int32))
+        return jnp.stack(found)
+
+    table = jnp.stack([filled(wides), filled(narrow_rows), filled(narrow_cols)])
     f32, bf16 = jnp.float32, jnp.bfloat16
+    spec_w = pl.BlockSpec((UNIT, HALF), lambda i, t: (0, t[0, i]))
+    spec_n = pl.BlockSpec((UNIT, HALF), lambda i, t: (t[1, i], t[2, i]))
+
+    def spec_sum(start, array):
+        halves = array.shape[2] // HALF
+
+        def place(i, t):
+            at = jnp.clip(i - start, 0, array.shape[0] * halves - 1)
+            return (at // halves, 0, at % halves)
+
+        return pl.BlockSpec((1, UNIT, HALF), place)
 
     def shapes(like):
         return [jax.ShapeDtypeStruct(like.shape, f32)] * 4 + [jax.ShapeDtypeStruct(like.shape, bf16)]
 
+    operands = [part[0] for part in parts] + list(wide) + list(narrow)
+    in_specs = [spec_sum(start, part[0]) for start, part in zip(starts, parts)]
+    in_specs += [spec_w] * 3 + [spec_n] * 3
+    aliases = {}
+    if before is not None:
+        aliases = {1 + len(operands) + i: i for i in range(10)}
+        operands += list(before)
+        in_specs += [pl.BlockSpec(memory_space=pl.ANY)] * 10
     return pl.pallas_call(
-        adam_kernel,
-        grid=(16,),
-        in_specs=[
-            pl.BlockSpec((rows, D), lambda i: (jnp.minimum(i, 3), 0)),
-            pl.BlockSpec((rows, D), lambda i: (jnp.clip(i - 4, 0, 1), 0)),
-            pl.BlockSpec((rows, D), lambda i: (jnp.maximum(i - 6, 0), 0)),
-        ] + [spec_w] * 3 + [spec_n] * 3,
-        out_specs=[spec_w] * 5 + [spec_n] * 5,
+        partial(adam_kernel, tuple(spans), 0 if before is None else 10),
+        grid_spec=pltpu.PrefetchScalarGridSpec(
+            num_scalar_prefetch=1,
+            grid=(step,),
+            in_specs=in_specs,
+            out_specs=[spec_w] * 5 + [spec_n] * 5,
+        ),
         out_shape=shapes(wide[0]) + shapes(narrow[0]),
+        input_output_aliases=aliases,
         compiler_params=pltpu.CompilerParams(vmem_limit_bytes=58 << 20),
-    )(*sums, *wide, *narrow)
+        cost_estimate=pl.CostEstimate(
+            flops=30 * step * UNIT * HALF, bytes_accessed=32 * step * UNIT * HALF, transcendentals=0
+        ),
+    )(table, *operands)
 
 
 def matmul(left, right):
@@ -1106,24 +1235,20 @@
     def gathered(part):
         return lax.all_gather(part.astype(bf16), "shard", axis=0, tiled=True)
 
-    wide_full = gathered(wide_master)
-    narrow_full = gathered(narrow_master)
+    if shards == 2:
+        wide_full, narrow_full = gather_weights(wide_master, narrow_master)
+    else:
+        wide_full, narrow_full = gathered(wide_master), gathered(narrow_master)
     vector = gathered(vec_master).astype(f32)
     vec_rows = jnp.pad(vector.T, ((0, 24 - vector.shape[1]), (0, 0)))
-    joint_proj = matmul(tokens, wide_full[:, : 3 * D])
-    queries = (joint_proj[:, :D] + vector[:, 0]).astype(bf16)
-    keys_self = joint_proj[:, D : 2 * D].astype(bf16)
-    values_self = (joint_proj[:, 2 * D :] + vector[:, 1]).astype(bf16)
-    mixed_self, totals_self = attend_forward(queries, keys_self, values_self, block_mask, True)
+    mixed_self, totals_self, queries, keys_self, values_self = attend_forward(
+        tokens, tokens, block_mask, wide_full, vec_rows, True
+    )
     resid_one = tokens.astype(f32) + matmul(mixed_self, wide_full[:, 3 * D : 4 * D]) + vector[:, 2]
     normed_one = norm_forward(resid_one, vector[:, 11], vector[:, 14])
     normed_low = normed_one.astype(bf16)
-    cross_queries = (matmul(normed_low, wide_full[:, 4 * D : 5 * D]) + vector[:, 3]).astype(bf16)
-    enc_proj = matmul(encoder_states, wide_full[:, 5 * D : 7 * D])
-    cross_keys = enc_proj[:, :D].astype(bf16)
-    cross_values = (enc_proj[:, D:] + vector[:, 4]).astype(bf16)
-    mixed_cross, totals_cross = attend_forward(
-        cross_queries, cross_keys, cross_values, block_mask, False
+    mixed_cross, totals_cross, cross_queries, cross_keys, cross_values = attend_forward(
+        normed_low, encoder_states, block_mask, wide_full, vec_rows, False
     )
     output, grad_two, grad_cross_mix, term_in, term_narrow, term_co, sums = center(
         mixed_cross, normed_one, cotangent, wide_full, narrow_full, vec_rows, factor, shards
@@ -1132,26 +1257,53 @@
     def split(term):
         return term.reshape(shards, -1, D)
 
-    carried = shards == 2 and replicas % 4 == 0 and UNIT % (32 * (replicas // 4)) == 0
     lanes = replicas // 4
-    early = [term_in, split(term_narrow), split(term_co)]
+    carried = shards == 2 and replicas % 4 == 0 and UNIT % (32 * lanes) == 0
+    terms = [term_in, split(term_narrow), split(term_co)]
+    names = [("wide", 8 + i) for i in range(4)] + [("narrow", i) for i in range(4)] + [("wide", 7)]
+    names += [("wide", i) for i in (4, 5, 6, 3, 0, 1, 2)]
+    x_first = [i % 2 == 0 for i in range(9)] + [i % 2 == 1 for i in range(4)] + [i % 2 == 1 for i in range(3)]
+    spots = [(0, UNIT * i) for i in range(4)] + [(1, UNIT * i) for i in range(4)] + [(2, 0)]
+    parts_own, parts_far = [], []
+
+    def item(mode, unit, which=0, row=0):
+        return (mode, x_first[unit], which, row)
+
+    def collect(traffic, outs, units):
+        blocks, halves, small = traffic.unpack(outs)
+        if traffic.entire:
+            summed = [names[u] for u, it in zip(units, traffic.items) if it[0] != "scatter"]
+            parts_own.append((halves[0], summed, True, True))
+            return blocks, small
+        for by_x, array in zip((True, False), halves):
+            if array is None:
+                continue
+            mine = [names[u] for u, it in zip(units, traffic.items) if it[0] != "scatter" and it[1] == by_x]
+            pairs = [(r, r ^ (1 if by_x else 2)) for r in range(replicas)]
+            parts_own.append((array, mine, by_x, True))
+            parts_far.append((lax.ppermute(array, "rep", pairs), mine, by_x, False))
+        return blocks, small
+
     traffic = None
+    units = list(range(N_BOTH + N_SCATTER))
     if carried:
-        places = [(0, UNIT * i, i % 2 == 0) for i in range(4)] + [(1, UNIT * i, i % 2 == 0) for i in range(4)]
-        traffic = Traffic(["both"] * 4 + ["scatter"] * 4, lanes, early[:2], places)
+        items = [item("both" if u < N_BOTH else "scatter", u, *spots[u]) for u in units]
+        traffic = Traffic(items, lanes, True, terms)
     found = attend_backward(
-        cross_queries, cross_keys, cross_values, block_mask, False, mixed_cross, totals_cross[0],
+        cross_queries, cross_keys, cross_values, block_mask, False, mixed_cross, totals_cross,
         grad_cross_mix, normed_low, grad_two, wide_full, factor,
         (encoder_states, resid_one, mixed_self, vec_rows), traffic, CROSS_TABLE, 1,
     )
     term_cq, term_ck, term_cv, cross_sums, grad_one, enc_grad, grad_self_mix, term_wo, norm_sums = found[:9]
     middle = [split(term) for term in (term_cq, term_ck, term_cv, term_wo)]
     if carried:
-        blocks, sum_in = found[9:]
-        places = [True, False, (0, 0, True), (1, 0, False)]
-        traffic = Traffic(["gather"] * 2 + ["scatter"] * 2, lanes, middle[:2], places, blocks[:2])
+        blocks, _ = collect(traffic, found[9:], units)
+        units = list(range(N_BOTH, N_BOTH + N_GATHER)) + list(range(9, 9 + N_MIDDLE))
+        items = [item("gather", u) for u in units[:N_GATHER]]
+        items += [item("scatter", 9 + i, i) for i in range(N_MIDDLE)]
+        traffic = Traffic(items, lanes, True, middle[:N_MIDDLE], blocks[:N_GATHER])
     found = attend_backward(
-        queries, keys_self, values_self, block_mask, True, mixed_self, totals_self[0],
+        queries, keys_self, values_self, block_mask, True, mixed_self, totals_self,
         grad_self_mix, tokens, grad_one, wide_full, factor, None, traffic, SELF_TABLE, 2,
     )
     late = [split(term) for term in found[:3]]
@@ -1170,27 +1322,39 @@
         0,
     )
     term_vec = (term_vec * factor).reshape(24, shards, -1).transpose(1, 0, 2)
-    last = [early[2], middle[2], middle[3]] + late
+    wide = (wide_master, wide_first, wide_second)
+    narrow = (narrow_master, narrow_first, narrow_second)
     if carried:
-        blocks_self, sum_mid = found[5:]
-        modes = ["gather"] * 4 + ["both"] * 6
-        places = [i % 2 == 0 for i in range(4)] + [(i, 0, i % 2 == 0) for i in range(6)]
-        traffic = Traffic(modes, lanes, last, places, jnp.concatenate([blocks[2:], blocks_self], 0), term_vec)
-        sum_late, vec_sum = run_traffic(traffic, TAIL_ORDER, 0)
-        totals = [sum_in, sum_mid, sum_late]
+        blocks_self, _ = collect(traffic, found[5:], units)
+        kept = list(range(N_BOTH + N_GATHER, N_BOTH + N_SCATTER)) + list(range(9, 9 + N_MIDDLE))
+        fresh = list(range(N_BOTH + N_SCATTER, 9))
+        items = [item("gather", u) for u in kept] + [item("both", u, *spots[u]) for u in fresh]
+        others = middle[N_MIDDLE:] + late
+        items += [item("both", 9 + N_MIDDLE + i, 3 + i) for i in range(len(others))]
+        held = jnp.concatenate([blocks[N_GATHER:], blocks_self], 0)
+        traffic = Traffic(items, lanes, False, terms + others, held, term_vec)
+        _, vec_sum = collect(
+            traffic, run_traffic(traffic, TAIL_ORDER, 0), kept + fresh + list(range(9 + N_MIDDLE, 16))
+        )
+        rep = lax.axis_index("rep")
+        x, y = rep % 2, (rep // 2) % 2
+        updated = adam_halves(parts_own, x, y, wide, narrow, None)
+        updated = adam_halves(parts_far, x, y, wide, narrow, updated)
     else:
-        narrow_sum = whole_sum(early[1])
-        cut = narrow_sum.shape[0] // 2
-        rest = [narrow_sum[cut:]] + [whole_sum(term) for term in middle[:2] + last]
-        totals = [whole_sum(early[0]), narrow_sum[:cut], jnp.concatenate(rest, 0)]
+        by_column = late + [middle[3]] + middle[:3] + [terms[2]]
+        by_column += [term_in[:, i * (D // shards) : (i + 1) * (D // shards)] for i in range(4)]
+        wide_sum = jnp.concatenate([whole_sum(term) for term in by_column], 1).astype(f32)
+        narrow_sum = whole_sum(terms[1]).astype(f32)
         vec_sum = lax.psum(lax.psum_scatter(term_vec, "shard", scatter_dimension=0), "rep")
-    vec_grad = vec_sum[: vec_master.shape[1]].T
+        updated = []
+        for gradient, state in ((wide_sum, wide), (narrow_sum, narrow)):
+            new, first_new, second_new = adam_update(*state, gradient, weight_decay, learn_rate)
+            updated += [gradient, new, first_new, second_new, new.astype(bf16)]
     (
         wide_grad, wide_new, wide_first_new, wide_second_new, wide_copy,
         narrow_grad, narrow_new, narrow_first_new, narrow_second_new, narrow_copy,
-    ) = adam_all(
-        totals, (wide_master, wide_first, wide_second), (narrow_master, narrow_first, narrow_second)
-    )
+    ) = updated
+    vec_grad = vec_sum[: vec_master.shape[1]].T
     vec_new, vec_first_new, vec_second_new = adam_update(
         vec_master, vec_first, vec_second, vec_grad, 0.0, vec_rate
     )

time: 531 us -> 477 us (0.90)
  waiting for transfers between devices: 22.5 us -> 0.01 us
  matrix products: 20.3 us -> 3.72 us
  other arithmetic: 23.9 us -> 7.59 us
  between operations: 14.8 us -> 1.33 us
  Pallas kernels: 424 us -> 432 us
    pallas_call x3 -> x5, Pallas kernels: 93 us -> 144 us  [the longest x2 68 us: adam_halves(): pl.pallas_call(partial(adam_kernel, tuple(spans), 0 if before is None els...]
    pallas_call x1, Pallas kernels: 98.5 us -> 74.5 us  [run_traffic(): pl.pallas_call(partial(traffic_kernel, traffic, order), in_specs=traffic....]
    all_gather x2 -> x0, waiting for transfers between devices: 22.4 us -> none  [gathered(): return lax.all_gather(part.astype(bf16), 'shard', axis=0, tiled=True)]
    dot_general x4 -> x1, matrix products: 20.3 us -> 3.72 us  [matmul(): return jnp.dot(left, right, preferred_element_type=jnp.float32)]
    convert_element_type x3 -> x1, other arithmetic: 13.1 us -> 0.77 us  [gathered(): return lax.all_gather(part.astype(bf16), 'shard', axis=0, tiled=True)]
    pallas_call x1, Pallas kernels: 65.5 us -> 55.9 us  [center(): pl.pallas_call(partial(center_kernel, factor), grid=(8,), in_specs=[whole...]
    pallas_call x2, Pallas kernels: 167 us -> 158 us  [attend_backward(): pl.pallas_call(partial(backward_kernel, causal, traffic, table, factor),...]
    unnamed x38 -> x50, local copies, waits for them, and re-layouts: 5.98 us -> 13.2 us
  transfers between devices with their start and end apart: 2 -> 2, of which waited for: 1 -> 0; matrix products, arithmetic and copies ran while one was open for 7% -> 0% of each run, Pallas kernels for 8% -> 10%
where the time goes in v4:
time: 477 us; the launch traced here: 469 us
  Pallas kernels  432 us (91%)
  local copies, waits for them, and re-layouts  20.2 us (4%)
  other arithmetic  7.59 us (2%)
    pallas_call x2, Pallas kernels, attend_backward(): pl.pallas_call(partial(backward_kernel, causal, traffic, table, factor),...  158 us
    pallas_call x1, Pallas kernels, run_traffic(): pl.pallas_call(partial(traffic_kernel, traffic, order), in_specs=traffic....  74.5 us
    pallas_call x2, Pallas kernels, adam_halves(): pl.pallas_call(partial(adam_kernel, tuple(spans), 0 if before is None els...  68 us
    pallas_call x2, Pallas kernels, attend_forward(): pl.pallas_call(partial(forward_kernel, causal), grid=(D // 128,), in_spec...  58.7 us
    pallas_call x1, Pallas kernels, center(): pl.pallas_call(partial(center_kernel, factor), grid=(8,), in_specs=[whole...  55.9 us
    pallas_call x1, Pallas kernels, gather_weights(): pl.pallas_call(gather_kernel, grid=(ALL_UNITS,), in_specs=[pl.BlockSpec((...  17 us
    unnamed x50, local copies, waits for them, and re-layouts  13.2 us
  transfers between devices with their start and end apart: 2, of which 0 were waited for; matrix products, arithmetic and copies ran while one was open for 0% of the time, Pallas kernels for 10%

profile of v4, /device:TPU:0, one launch (start us, length us, event | category | flops | bytes accessed | tf_op | source)
XLA Modules:
  0.0 469.0 jit_solution(6009663625911821441)
XLA Ops:
  0.7 0.8 convert_element_type.18
  1.4 1.9 all_gather.3
  3.4 0.0 copy-start
  3.4 2.3 copy-done
  5.8 17.0 %shard_map.268 = (bf16[768,9216]{1,0:T(8,128)(2,1)}, bf16[3072,768]{1,0:T(8,128)(2,1)S(1)}) custom-call(f32[384,9216]{1,0:T(8,128)} %refs_2_.1, f32[1536,768]{1,0:T(8,128)S(1)} %copy-done), custom_call_target="tpu_custom_call" | custom-call | tf_op jit(solution)/shard_map/pallas_call | solution.py:808
  22.8 0.0 copy-start.4
  22.8 2.2 copy-done.4
  25.0 0.0 copy-start.13
  25.0 19.8 %shard_map.269 = (bf16[1024,768]{1,0:T(8,128)(2,1)S(1)}, f32[6,8,1024]{2,1,0:T(8,128)S(1)}, bf16[1024,768]{1,0:T(8,128)(2,1)S(1)}, bf16[1024,768]{1,0:T(8,128)(2,1)S(1)}, bf16[1024,768]{1,0:T(8,128)(2,1)}) custom-call(s32[1,4,4]{2,1,0:T(4,128)S(1)} %copy-done.3, bf16[1024,768]{1,0:T(8,128)(2,1)} %refs_7_.3, bf16[1024,768]{1,0:T(8,128)(2,1)} %refs_7_.3, ...), custom_call_target="tpu_custom_call" | custom-call | flops 6442450944 | bytes 3145728 | tf_op jit(solution)/shard_map/pallas_call | solution.py:210
  44.9 3.7 fusion.7
  48.7 0.0 copy-start.12
  48.7 0.5 multiply_reduce_fusion
  49.2 2.3 fusion.4
  51.5 38.9 %shard_map.270 = (bf16[1024,768]{1,0:T(8,128)(2,1)S(1)}, f32[6,8,1024]{2,1,0:T(8,128)S(1)}, bf16[1024,768]{1,0:T(8,128)(2,1)S(1)}, bf16[2048,768]{1,0:T(8,128)(2,1)}, bf16[2048,768]{1,0:T(8,128)(2,1)}) custom-call(s32[1,4,4]{2,1,0:T(4,128)S(1)} %copy-done.3, bf16[1024,768]{1,0:T(8,128)(2,1)S(1)} %get-tuple-element.146.left_q_ref.refs_7_, ...), custom_call_target="tpu_custom_call" | custom-call | flops 25769803776 | bytes 3145728 | tf_op jit(solution)/shard_map/pallas_call | solution.py:210
  90.3 1.1 copy-done.9
  91.5 1.1 copy-done.10
  92.6 0.7 copy-done.11
  93.3 55.9 %shard_map.271 = (bf16[1024,768]{1,0:T(8,128)(2,1)}, f32[1024,768]{1,0:T(8,128)}, bf16[1024,768]{1,0:T(8,128)(2,1)}, bf16[2,1536,768]{2,1,0:T(8,128)(2,1)}, bf16...) custom-call(bf16[1024,768]{1,0:T(8,128)(2,1)} %copy-done.9, ...), custom_call_target="tpu_custom_call" | custom-call | flops 32614907904 | bytes 31457280 | tf_op jit(solution)/shard_map/pallas_call | solution.py:379
  149.2 0.8 slice.54
  150.0 0.7 slice.56
  150.8 0.8 slice.58
  151.6 111.3 %shard_map.272 = (bf16[768,768]{1,0:T(8,128)(2,1)}, bf16[768,768]{1,0:T(8,128)(2,1)}, bf16[768,768]{1,0:T(8,128)(2,1)}, f32[8,768]{1,0:T(8,128)}, f32[1024,768]{...) custom-call(s32[1,4,4]{2,1,0:T(4,128)} %refs_0_.3, ...), custom_call_target="tpu_custom_call" | custom-call | flops 64424509440 | bytes 3145728 | tf_op jit(solution)/shard_map/pallas_call | solution.py:1065
  262.9 1.6 fusion.5
  264.4 46.8 %shard_map.273 = (bf16[768,768]{1,0:T(8,128)(2,1)}, bf16[768,768]{1,0:T(8,128)(2,1)}, bf16[768,768]{1,0:T(8,128)(2,1)}, f32[8,768]{1,0:T(8,128)}, bf16[1024,768]...) custom-call(s32[1,4,4]{2,1,0:T(4,128)} %refs_0_.3, bf16[1024,768]{1,0:T(8,128)(2,1)} %copy-done.6, ...), custom_call_target="tpu_custom_call" | custom-call | flops 16106127360 | bytes 3145728 | tf_op jit(solution)/shard_map/pallas_call | solution.py:1065
  311.3 0.7 slice.51
  312.0 0.9 fusion.6
  312.9 0.7 slice.53
  313.6 0.3 concatenate.32
  313.9 0.6 multiply_bitcast_fusion.refs_9_
  314.6 1.6 pad_maximum_fusion.refs_8_
  316.1 74.5 %shard_map.274 = (bf16[5,384,384]{2,1,0:T(8,128)(2,1)}, bf16[5,384,384]{2,1,0:T(8,128)(2,1)}, f32[24,384]{1,0:T(8,128)}) custom-call(bf16[2,1536,768]{2,1,0:T(8,128)(2,1)} %get-tuple-element.92.refs_17_.refs_0_, bf16[2,1536,768]{2,1,0:T(8,128)(2,1)} %bitcast.47, bf16[2,384,768]{2,1,0:T(8,128)(2,1)} %bitcast.49, bf16[2,384,768]{2,1,0:T(8,128)(2,1)} %bitcast.50, ...), custom_call_target="tpu_custom_call" | custom-call | tf_op jit(solution)/shard_map/pallas_call | solution.py:750
  390.6 1.6 collective-permute-start
  392.2 0.4 collective-permute-start.1
  392.6 0.1 stack.116
  392.7 0.1 stack.130
  392.8 0.1 stack.113
  392.9 0.1 stack.127
  393.0 0.6 pad_add_fusion.1.table_ref
  393.6 45.5 %shard_map.275 = (f32[384,9216]{1,0:T(8,128)}, f32[384,9216]{1,0:T(8,128)}, f32[384,9216]{1,0:T(8,128)}, f32[384,9216]{1,0:T(8,128)}, bf16[384,9216]{1,0:T(8,128...) custom-call(s32[3,22]{1,0:T(4,128)} %pad_add_fusion.1.table_ref, ...), custom_call_target="tpu_custom_call" | custom-call | flops 97320960 | bytes 103809024 | tf_op jit(solution)/shard_map/pallas_call | solution.py:1173
  439.2 0.6 pad_add_fusion.table_ref
  439.8 0.7 fusion.2
  440.4 0.0 copy-start.17
  440.4 1.1 copy-done.16
  441.5 0.5 copy-done.17
  442.0 22.5 %shard_map.276 = (f32[384,9216]{1,0:T(8,128)}, f32[384,9216]{1,0:T(8,128)}, f32[384,9216]{1,0:T(8,128)}, f32[384,9216]{1,0:T(8,128)}, bf16[384,9216]{1,0:T(8,128...) custom-call(s32[3,10]{1,0:T(4,128)} %pad_add_fusion.table_ref, ...), custom_call_target="tpu_custom_call", output_to_operand_aliasing={{0}: (9, {}), {1}: (10, {}), {2}: (11, {}), {3}: (12, {}), ... | custom-call | flops 44236800 | bytes 47185920 | tf_op jit(solution)/shard_map/pallas_call | solution.py:1173
  464.5 1.1 copy.57
  465.7 1.3 copy-done.14
  467.0 1.7 copy.58
  (47 shorter events, 0.2 us)
Async XLA Ops:
  3.4 2.3 copy-start
  5.8 19.3 %copy-start.3 = (s32[1,4,4]{2,1,0:T(4,128)S(1)}, s32[1,4,4]{2,1,0:T(4,128)}, u32[]{:S(2)}) copy-start(s32[1,4,4]{2,1,0:T(4,128)} %refs_0_.3) | copy-start | bytes 196
  22.8 2.2 copy-start.4
  25.0 26.5 %copy-start.2 = (f32[24,768]{1,0:T(8,128)}, f32[24,768]{1,0:T(8,128)S(1)}, u32[]{:S(2)}) copy-start(f32[24,768]{1,0:T(8,128)S(1)} %pad.4.vec_ref.refs_16_) | copy-start | bytes 221188
  25.0 19.9 %copy-start.13 = (bf16[1024,768]{1,0:T(8,128)(2,1)S(1)}, bf16[1024,768]{1,0:T(8,128)(2,1)}, u32[]{:S(2)}) copy-start(bf16[1024,768]{1,0:T(8,128)(2,1)} %refs_7_.3) | copy-start | bytes 4718596
  44.9 3.8 copy-start.5
  44.9 3.8 copy-start.6
  44.9 3.8 copy-start.7
  44.9 3.8 copy-start.8
  48.7 2.8 copy-start.12
  51.5 38.9 %copy-start.1 = (bf16[1024,768]{1,0:T(8,128)(2,1)}, bf16[1024,768]{1,0:T(8,128)(2,1)S(1)}, u32[]{:S(2)}) copy-start(bf16[1024,768]{1,0:T(8,128)(2,1)S(1)} %get-tuple-element.146.left_q_ref.refs_7_) | copy-start | bytes 4718596
  90.3 1.1 copy-start.9
  91.5 1.1 copy-start.10
  92.6 0.7 copy-start.11
  316.1 76.9 %copy-start.23 = (s32[1,22]{1,0:T(1,128)S(1)}, s32[1,22]{1,0:T(1,128)}, u32[]{:S(2)}) copy-start(s32[1,22]{1,0:T(1,128)} %constant.103.clone.1) | copy-start | bytes 268
  390.6 49.8 %collective-permute-start = (bf16[5,384,384]{2,1,0:T(8,128)(2,1)}, bf16[5,384,384]{2,1,0:T(8,128)(2,1)S(1)}, u32[]{:S(2)}, u32[]{:S(2)}) collective-permute-start(bf16[5,384,384]{2,1,0:T(8,128)(2,1)} %get-tuple-element.113.refs_2_), channel_id=1, source_target_pairs={{0,2},{2,0},{4,6},{6,4},{8,10},{10,8},{12,14},{14,12},{16,18},{18,... | collective-permute-start | bytes 4423688 | tf_op jit(solution)/shard_map/ppermute | solution.py:1284
  392.2 48.2 %collective-permute-start.1 = (bf16[5,384,384]{2,1,0:T(8,128)(2,1)}, bf16[5,384,384]{2,1,0:T(8,128)(2,1)S(1)}, u32[]{:S(2)}, u32[]{:S(2)}) collective-permute-start(bf16[5,384,384]{2,1,0:T(8,128)(2,1)} %get-tuple-element.114.refs_3_), channel_id=1, source_target_pairs={{0,4},{2,6},{4,0},{6,2},{8,12},{10,14},{12,8},{14,10},{16,20},{18,... | collective-permute-start | bytes 4423688 | tf_op jit(solution)/shard_map/ppermute | solution.py:1284
  393.6 45.5 %copy-start.22 = (s32[1,10]{1,0:T(1,128)S(1)}, s32[1,10]{1,0:T(1,128)}, u32[]{:S(2)}) copy-start(s32[1,10]{1,0:T(1,128)} %constant.87.clone.1) | copy-start | bytes 124
  393.6 46.1 %copy-start.18 = (f32[384,17]{0,1:T(8,128)S(1)}, f32[384,17]{0,1:T(8,128)}, u32[]{:S(2)}) copy-start(f32[384,17]{0,1:T(8,128)} %param.19) | copy-start | bytes 78340
  393.6 46.1 %copy-start.19 = (f32[384,17]{0,1:T(8,128)S(1)}, f32[384,17]{0,1:T(8,128)}, u32[]{:S(2)}) copy-start(f32[384,17]{0,1:T(8,128)} %param.22) | copy-start | bytes 78340
  393.6 46.1 %copy-start.20 = (f32[384,17]{0,1:T(8,128)S(1)}, f32[384,17]{0,1:T(8,128)}, u32[]{:S(2)}) copy-start(f32[384,17]{0,1:T(8,128)} %param.25) | copy-start | bytes 78340
  393.6 46.1 %copy-start.21 = (f32[24,384]{1,0:T(8,128)S(1)}, f32[24,384]{1,0:T(8,128)}, u32[]{:S(2)}) copy-start(f32[24,384]{1,0:T(8,128)} %get-tuple-element.129) | copy-start | bytes 110596
  440.4 1.1 copy-start.16
  440.4 1.6 copy-start.17
  442.0 22.5 %copy-start.15 = (bf16[1024,768]{1,0:T(8,128)(2,1)S(1)}, bf16[1024,768]{1,0:T(8,128)(2,1)}, u32[]{:S(2)}) copy-start(bf16[1024,768]{1,0:T(8,128)(2,1)} %get-tuple-element.176) | copy-start | bytes 4718596
  464.5 2.5 copy-start.14

commit v5 on v4

--- a/solution.py
+++ b/solution.py
@@ -27,10 +27,8 @@
 masked_score = -1e30
 FACTOR = HD ** (-0.5)
 SCALE2 = FACTOR / math.log(2.0)
-WIDE_UNITS = 12
-ALL_UNITS = 16
-N_BOTH = 4
-N_SCATTER = 4
+N_BOTH = 2
+N_SCATTER = 6
 N_GATHER = 2
 N_MIDDLE = 2
 
@@ -38,41 +36,37 @@
 CROSS_TABLE = {
     (0, 0): ((0, 0), (1, 0), (2, 0), (3, 0)),
     (0, 9): ((0, 1), (1, 1), (2, 1), (3, 1)),
-    (1, 9): ((0, 2), (1, 2), (2, 2), (3, 2)),
-    (2, 0): ((4, 0), (5, 0), (6, 0), (7, 0)),
-    (2, 5): ((0, 3), (1, 3), (2, 3), (3, 3)),
-    (2, 9): ((4, 1), (5, 1), (6, 1), (7, 1)),
-    (3, 5): ((0, 4), (1, 4), (2, 4), (3, 4)),
-    (3, 9): ((4, 2), (5, 2), (6, 2), (7, 2)),
-    (4, 5): ((0, 5), (1, 5), (2, 5), (3, 5), (4, 3), (5, 3), (6, 3), (7, 3)),
-    (5, 0): ((0, 6), (1, 6), (2, 6), (3, 6)),
-    (5, 5): ((4, 4), (5, 4), (6, 4), (7, 4)),
-    (5, 9): ((0, 7), (1, 7), (2, 7), (3, 7), (0, 8), (1, 8), (2, 8), (3, 8)),
+    (2, 0): ((0, 2), (1, 2), (2, 2), (3, 2)),
+    (2, 3): ((4, 0), (5, 0), (6, 0), (7, 0)),
+    (2, 9): ((0, 3), (1, 3), (2, 3), (3, 3), (4, 1), (5, 1), (6, 1), (7, 1)),
+    (4, 0): ((0, 4), (1, 4), (2, 4), (3, 4), (4, 2), (5, 2), (6, 2), (7, 2)),
+    (4, 9): ((0, 5), (1, 5), (4, 3), (5, 3), (6, 3), (7, 3)),
+    (5, 3): ((0, 6), (1, 6)),
+    (5, 9): ((4, 4), (5, 4), (6, 4), (7, 4), (0, 7), (1, 7), (0, 8), (1, 8)),
 }
 
 
 SELF_TABLE = {
     (0, 0): ((0, 0), (1, 0), (2, 0), (3, 0)),
-    (0, 8): ((2, 1), (3, 1)),
-    (1, 3): ((0, 1), (1, 1)),
-    (2, 8): ((0, 2), (1, 2), (2, 2), (3, 2)),
-    (4, 3): ((2, 3), (3, 3)),
-    (4, 8): ((0, 3), (1, 3)),
-    (5, 3): ((0, 4), (1, 4)),
-    (5, 8): ((2, 4), (3, 4)),
+    (0, 5): ((2, 1), (3, 1)),
+    (1, 5): ((0, 1), (1, 1)),
+    (2, 5): ((0, 2), (1, 2), (2, 2), (3, 2)),
+    (4, 5): ((0, 3), (1, 3), (2, 3), (3, 3)),
+    (5, 5): ((0, 4), (1, 4), (2, 4), (3, 4)),
 }
 
 
 TAIL_ORDER = (
-    (10, 0), (0, 0), (1, 0), (2, 0), (3, 0), (4, 0), (5, 0), (4, 1),
-    (5, 1), (4, 2), (10, 1), (5, 2), (6, 0), (7, 0), (0, 1), (1, 1),
-    (2, 1), (3, 1), (6, 1), (7, 1), (10, 2), (4, 3), (5, 3), (0, 2),
-    (1, 2), (2, 2), (3, 2), (8, 0), (9, 0), (4, 4), (10, 3), (5, 4),
-    (0, 3), (1, 3), (2, 3), (3, 3), (6, 2), (7, 2), (8, 1), (9, 1),
-    (10, 4), (4, 5), (5, 5), (6, 3), (7, 3), (8, 2), (9, 2), (4, 6),
-    (5, 6), (6, 4), (7, 4), (4, 7), (5, 7), (8, 3), (9, 3), (6, 5),
-    (7, 5), (8, 4), (9, 4), (6, 6), (7, 6), (6, 7), (7, 7), (8, 5),
-    (9, 5), (8, 6), (9, 6), (8, 7), (9, 7),
+    (12, 0), (0, 0), (1, 0), (2, 0), (3, 0), (4, 0), (5, 0), (6, 0),
+    (7, 0), (6, 1), (12, 1), (7, 1), (6, 2), (7, 2), (8, 0), (9, 0),
+    (8, 1), (9, 1), (6, 3), (7, 3), (12, 2), (0, 1), (1, 1), (2, 1),
+    (3, 1), (4, 1), (5, 1), (6, 4), (7, 4), (8, 2), (12, 3), (9, 2),
+    (10, 0), (11, 0), (0, 2), (1, 2), (2, 2), (3, 2), (4, 2), (5, 2),
+    (12, 4), (6, 5), (7, 5), (10, 1), (11, 1), (0, 3), (1, 3), (2, 3),
+    (3, 3), (4, 3), (5, 3), (8, 3), (9, 3), (6, 6), (7, 6), (6, 7),
+    (7, 7), (8, 4), (9, 4), (10, 2), (11, 2), (10, 3), (11, 3), (8, 5),
+    (9, 5), (8, 6), (9, 6), (10, 4), (11, 4), (8, 7), (9, 7), (10, 5),
+    (11, 5), (10, 6), (11, 6), (10, 7), (11, 7),
 )
 
 
@@ -95,10 +89,12 @@
     )
 
 
-def forward_kernel(
-    causal, mask_ref, left_q_ref, left_k_ref, wq_ref, wk_ref, wv_ref, vec_ref,
-    o_ref, lse_ref, q_ref, k_ref, v_ref, qm_ref, vt_ref, acc_ref, sum_ref, top_ref,
-):
+def forward_kernel(causal, carry, *refs):
+    mask_ref, left_q_ref, left_k_ref, wq_ref, wk_ref, wv_ref, vec_ref = refs[:7]
+    masters, refs = refs[7 : 7 + 2 * carry], refs[7 + 2 * carry :]
+    o_ref, lse_ref, q_ref, k_ref, v_ref = refs[:5]
+    copies, refs = refs[5 : 5 + 2 * carry], refs[5 + 2 * carry :]
+    qm_ref, vt_ref, acc_ref, sum_ref, top_ref = refs[:5]
     rows, keys = q_ref.shape[0], k_ref.shape[0]
     tile = BLK
     bias_q, bias_v = (vec_ref[0:1, :], vec_ref[1:2, :]) if causal else (vec_ref[3:4, :], vec_ref[4:5, :])
@@ -161,21 +157,7 @@
             both.append(acc_ref[head] * (1.0 / total))
         o_ref[...] = jnp.concatenate(both, axis=0).T.astype(jnp.bfloat16)
 
-    lse_ref[...] = jnp.zeros_like(lse_ref)
-    waiting = []
-    for j in range(keys // tile):
-        for head in range(2):
-            waiting.append((j, head, scores_of(j, head)))
-            if len(waiting) > 1:
-                add_tile(*waiting.pop(0), None)
-    while waiting:
-        add_tile(*waiting.pop(0), None)
-    finish(None)
-    sums = sum_ref[...]
-    usable = jnp.min(jnp.where((sums > 1e-25) & (sums < 1e30), 1, 0))
-
-    @pl.when(usable == 0)
-    def _():
+    def peaks():
         for head in range(2):
             for j in range(keys // tile):
                 peak = jnp.max(scores_of(j, head), axis=0, keepdims=True)
@@ -186,16 +168,43 @@
                     top_ref[head : head + 1, begin:] = jnp.maximum(
                         top_ref[head : head + 1, begin:], peak
                     )
-        shifts = [top_ref[0:1, :], top_ref[1:2, :]]
+        return [top_ref[0:1, :], top_ref[1:2, :]]
+
+    lse_ref[...] = jnp.zeros_like(lse_ref)
+    shifts = peaks() if carry else None
+    waiting = []
+
+    def next_tile():
+        j, head, scores = waiting.pop(0)
+        add_tile(j, head, scores, shifts[head] if carry else None)
+
+    for j in range(keys // tile):
+        for head in range(2):
+            waiting.append((j, head, scores_of(j, head)))
+            if len(waiting) > 1:
+                next_tile()
+    while waiting:
+        next_tile()
+    finish(shifts)
+    if carry:
+        gather_rest(pl.program_id(0), *masters, *copies, refs[5:])
+        return
+    sums = sum_ref[...]
+    usable = jnp.min(jnp.where((sums > 1e-25) & (sums < 1e30), 1, 0))
+
+    @pl.when(usable == 0)
+    def _():
+        tops = peaks()
         for head in range(2):
             for j in range(keys // tile):
-                add_tile(j, head, scores_of(j, head), shifts[head])
-        finish(shifts)
-
-
-def attend_forward(left_q, left_k, block_table, wide_full, vec_rows, causal):
+                add_tile(j, head, scores_of(j, head), tops[head])
+        finish(tops)
+
+
+def attend_forward(left_q, left_k, block_table, weights, vec_rows, causal, masters):
     rows, keys = left_q.shape[0], left_k.shape[0]
-    first = 0 if causal else 4
+    first = 0 if causal else 1
+    carry = masters is not None
     bf16, f32 = jnp.bfloat16, jnp.float32
 
     def columns(count):
@@ -207,32 +216,38 @@
     def weight(unit):
         return pl.BlockSpec((D, 128), lambda i: (0, unit * (D // 128) + i))
 
+    anywhere = [pl.BlockSpec(memory_space=pl.ANY)] * 2
+    params = dict(vmem_limit_bytes=56 << 20)
+    if carry:
+        params.update(collective_id=4, has_side_effects=True)
     return pl.pallas_call(
-        partial(forward_kernel, causal),
+        partial(forward_kernel, causal, carry),
         grid=(D // 128,),
         in_specs=[pl.BlockSpec(memory_space=pltpu.SMEM), whole(rows), whole(keys)]
-        + [weight(first), weight(first + 1), weight(first + 2), columns(vec_rows.shape[0])],
+        + [weight(first), weight(first + 1), weight(first + 2), columns(vec_rows.shape[0])] + anywhere * carry,
         out_specs=[columns(rows), pl.BlockSpec((1, 8, rows), lambda i: (i, 0, 0)), columns(rows)]
-        + [columns(keys)] * 2,
+        + [columns(keys)] * 2 + anywhere * carry,
         out_shape=[
             jax.ShapeDtypeStruct((rows, D), bf16),
             jax.ShapeDtypeStruct((D // 128, 8, rows), f32),
             jax.ShapeDtypeStruct((rows, D), bf16),
             jax.ShapeDtypeStruct((keys, D), bf16),
             jax.ShapeDtypeStruct((keys, D), bf16),
-        ],
+        ]
+        + [jax.ShapeDtypeStruct((D, 9 * D), bf16), jax.ShapeDtypeStruct((FF, D), bf16)] * carry,
         scratch_shapes=[
             pltpu.VMEM((2, rows, 128), bf16),
             pltpu.VMEM((128, keys), bf16),
             pltpu.VMEM((2, HD, rows), f32),
             pltpu.VMEM((2, rows), f32),
             pltpu.VMEM((2, rows), f32),
-        ],
-        compiler_params=pltpu.CompilerParams(vmem_limit_bytes=48 << 20),
+        ]
+        + (rest_scratch() if carry else []),
+        compiler_params=pltpu.CompilerParams(**params),
         cost_estimate=pl.CostEstimate(
             flops=(8 if causal else 16) * rows * keys * D, bytes_accessed=4 * left_q.size, transcendentals=0
         ),
-    )(block_table, left_q, left_k, wide_full, wide_full, wide_full, vec_rows)
+    )(block_table, left_q, left_k, weights, weights, weights, vec_rows, *(masters or ()))
 
 
 ROWS = 256
@@ -383,8 +398,8 @@
             whole,
             whole,
             whole,
-            pl.BlockSpec((D, D), lambda i: (0, 7)),
-            pl.BlockSpec((D, D), lambda i: (0, 8 + i % 4)),
+            pl.BlockSpec((D, D), lambda i: (0, 4)),
+            pl.BlockSpec((D, D), lambda i: (0, 5 + i % 4)),
             pl.BlockSpec((D, D), lambda i: (i % 4, 0)),
             pl.BlockSpec(vec_rows.shape, lambda i: (0, 0)),
         ],
@@ -468,7 +483,7 @@
     if mode != "gather":
         shapes += [
             pltpu.VMEM((UNIT, D), bf16),
-            pltpu.VMEM((UNIT, HALF), bf16),
+            pltpu.VMEM((UNIT // 2, D), bf16),
             pltpu.VMEM((UNIT // 2, HALF), bf16),
             pltpu.VMEM((lanes, block, HALF), bf16),
         ]
@@ -491,18 +506,16 @@
     sems, local_sem = scratch[-3:-1], scratch[-1]
     shard, z, here_a, here_b, sibling, peer_a, peer_b, others = unit_places(x_first, lanes)
     half_rows, block = UNIT // 2, UNIT // (2 * lanes)
-    mine_cols = pl.ds(aligned(here_a * HALF, 128), HALF)
-    their_cols = pl.ds(aligned((1 - here_a) * HALF, 128), HALF)
-    mine_b = aligned(here_b * half_rows)
+    mine_a = aligned(here_a * half_rows)
+    mine_cols = pl.ds(aligned(here_b * HALF, 128), HALF)
+    their_cols = pl.ds(aligned((1 - here_b) * HALF, 128), HALF)
     core = remote_copy(sems, 0, term.at[1 - shard, pl.ds(row, UNIT)], got, sibling)
     load = pltpu.make_async_copy(term.at[shard, pl.ds(row, UNIT)], acc, local_sem.at[0])
-    to_a = remote_copy(sems, 1, acc.at[:, their_cols], got_a, peer_a)
-    to_b = remote_copy(
-        sems, 2, acc.at[pl.ds(aligned((1 - here_b) * half_rows), half_rows), mine_cols], got_b, peer_b
-    )
+    to_a = remote_copy(sems, 1, acc.at[pl.ds(aligned((1 - here_a) * half_rows), half_rows)], got_a, peer_a)
+    to_b = remote_copy(sems, 2, acc.at[pl.ds(mine_a, half_rows), their_cols], got_b, peer_b)
     to_z = [
         remote_copy(
-            sems, 5 + k, acc.at[pl.ds(aligned(mine_b + ((z + k + 1) % lanes) * block), block), mine_cols],
+            sems, 5 + k, acc.at[pl.ds(aligned(mine_a + ((z + k + 1) % lanes) * block), block), mine_cols],
             got_z.at[z], peer,
         )
         for k, peer in enumerate(others)
@@ -529,18 +542,18 @@
         to_a.wait()
 
         def body(i, carry):
-            at = pl.ds(aligned(i * block), block)
-            acc[at, mine_cols] = acc[at, mine_cols] + got_a[at, :]
+            at = pl.ds(aligned(mine_a + i * block), block)
+            acc[at, :] = acc[at, :] + got_a[pl.ds(aligned(i * block), block), :]
             return carry
 
-        lax.fori_loop(0, UNIT // block, body, 0, unroll=True)
+        lax.fori_loop(0, half_rows // block, body, 0, unroll=True)
         to_b.start()
 
     def step_z():
         to_b.wait()
 
         def body(i, carry):
-            at = pl.ds(aligned(mine_b + i * block), block)
+            at = pl.ds(aligned(mine_a + i * block), block)
             acc[at, mine_cols] = acc[at, mine_cols] + got_b[pl.ds(aligned(i * block), block), :]
             return carry
 
@@ -551,7 +564,7 @@
     def step_own():
         for copy in to_z:
             copy.wait()
-        total = acc[pl.ds(aligned(mine_b + z * block), block), mine_cols].astype(f32)
+        total = acc[pl.ds(aligned(mine_a + z * block), block), mine_cols].astype(f32)
         for k in range(1, lanes):
             total = total + got_z[(z + k) % lanes].astype(f32)
         block_ref[...] = total.astype(bf16)
@@ -566,19 +579,19 @@
     sems, local_sem = scratch[-3:-1], scratch[-1]
     shard, z, here_a, here_b, sibling, peer_a, peer_b, others = unit_places(x_first, lanes)
     half_rows, block = UNIT // 2, UNIT // (2 * lanes)
-    mine_cols = pl.ds(aligned(here_a * HALF, 128), HALF)
-    mine_b = aligned(here_b * half_rows)
-    mine_z = full.at[pl.ds(aligned(mine_b + z * block), block), mine_cols]
-    mine_half = full.at[pl.ds(mine_b, half_rows), mine_cols]
+    mine_a = aligned(here_a * half_rows)
+    mine_cols = pl.ds(aligned(here_b * HALF, 128), HALF)
+    mine_z = full.at[pl.ds(aligned(mine_a + z * block), block), mine_cols]
+    mine_half = full.at[pl.ds(mine_a, half_rows), mine_cols]
     all_z = [remote_copy(sems, 5 + lanes + k, mine_z, mine_z, peer) for k, peer in enumerate(others)]
     all_b = remote_copy(sems, 3, mine_half, mine_half, peer_b)
-    mine_all = full.at[:, mine_cols]
+    mine_all = full.at[pl.ds(mine_a, half_rows)]
     all_a = remote_copy(sems, 4, mine_all, mine_all, peer_a)
     store = pltpu.make_async_copy(full if entire else mine_all, sum_out, local_sem.at[1])
 
     def start():
         source = block_ref if block_in is None else block_in
-        full[pl.ds(aligned(mine_b + z * block), block), mine_cols] = source[...]
+        full[pl.ds(aligned(mine_a + z * block), block), mine_cols] = source[...]
         for copy in all_z:
             copy.start()
 
@@ -681,7 +694,7 @@
             found.append((vmem, shape((self.n_scatter, UNIT // (2 * self.lanes), HALF), bf16)))
         for count in (self.n_x, self.n_y):
             if count:
-                found.append((anywhere, shape((count, UNIT, D if self.entire else HALF), bf16)))
+                found.append((anywhere, shape((count, UNIT if self.entire else UNIT // 2, D), bf16)))
         if self.small is not None:
             found.append((vmem, shape(self.small.shape[1:], jnp.float32)))
         return found
@@ -759,74 +772,118 @@
     )(*traffic.operands())
 
 
-def gather_kernel(wide_ref, narrow_ref, wide_out, narrow_out, held, send_sem, recv_sem, local_sem):
+REST = tuple(("wide", i) for i in range(3, 12)) + tuple(("narrow", i) for i in range(4))
+
+
+def meet_sibling():
+    rep, shard = lax.axis_index("rep"), lax.axis_index("shard")
+    barrier = pltpu.get_barrier_semaphore()
+    pl.semaphore_signal(barrier, inc=1, device_id=(rep, 1 - shard), device_id_type=MESH_ID)
+    pl.semaphore_wait(barrier, 1)
+
+
+def share(index, source, target, sems):
+    rep, shard = lax.axis_index("rep"), lax.axis_index("shard")
+    local = pltpu.make_async_copy(source, target, sems[2].at[index])
+    return local, remote_copy(sems[:2], index, source, target, (rep, 1 - shard))
+
+
+def first_kernel(wide_ref, vec_ref, wide_out, vec_out, held, held_vec, *sems):
     step = pl.program_id(0)
-    rep, shard = lax.axis_index("rep"), lax.axis_index("shard")
-    sibling = (rep, 1 - shard)
+    shard = lax.axis_index("shard")
+    rows = pl.ds(aligned(shard * UNIT), UNIT)
+
+    def wide_copies(unit):
+        return share(unit, held.at[unit], wide_out.at[rows, pl.ds(aligned(unit * D, 128), D)], sems)
+
+    def vec_copies():
+        return share(3, held_vec, vec_out.at[rows], sems)
 
     @pl.when(step == 0)
     def _():
-        barrier = pltpu.get_barrier_semaphore()
-        pl.semaphore_signal(barrier, inc=1, device_id=sibling, device_id_type=MESH_ID)
-        pl.semaphore_wait(barrier, 1)
-
-    def copies(unit, target):
-        local = pltpu.make_async_copy(held.at[unit], target, local_sem.at[unit])
-        return local, remote_copy((send_sem, recv_sem), unit, held.at[unit], target, sibling)
-
-    def wide_copies(unit):
-        target = wide_out.at[
-            pl.ds(aligned(shard * UNIT), UNIT), pl.ds(aligned(unit * D, 128), D)
-        ]
-        return copies(unit, target)
-
-    def narrow_copies(unit):
-        row = aligned(shard * (FF // 2) + (unit - WIDE_UNITS) * UNIT)
-        return copies(unit, narrow_out.at[pl.ds(row, UNIT)])
-
-    @pl.when(step < WIDE_UNITS)
+        meet_sibling()
+        held_vec[...] = vec_ref[...].astype(jnp.bfloat16)
+        for copy in vec_copies():
+            copy.start()
+
+    held[step] = wide_ref[...].astype(jnp.bfloat16)
+    for copy in wide_copies(step):
+        copy.start()
+
+    @pl.when(step == 2)
     def _():
-        held[step] = wide_ref[...].astype(jnp.bfloat16)
-        for copy in wide_copies(step):
-            copy.start()
-
-    @pl.when(step >= WIDE_UNITS)
-    def _():
-        held[step] = narrow_ref[...].astype(jnp.bfloat16)
-        for copy in narrow_copies(step):
-            copy.start()
-
-    @pl.when(step == ALL_UNITS - 1)
-    def _():
-        for unit in range(ALL_UNITS):
-            for copy in wide_copies(unit) if unit < WIDE_UNITS else narrow_copies(unit):
+        for copies in [wide_copies(unit) for unit in range(3)] + [vec_copies()]:
+            for copy in copies:
                 copy.wait()
 
 
-def gather_weights(wide_master, narrow_master):
+def gather_first(wide_master, vec_master):
     bf16 = jnp.bfloat16
     return pl.pallas_call(
-        gather_kernel,
-        grid=(ALL_UNITS,),
+        first_kernel,
+        grid=(3,),
         in_specs=[
-            pl.BlockSpec((UNIT, D), lambda i: (0, jnp.minimum(i, WIDE_UNITS - 1))),
-            pl.BlockSpec((UNIT, D), lambda i: (jnp.maximum(i - WIDE_UNITS, 0), 0)),
+            pl.BlockSpec((UNIT, D), lambda i: (0, i)),
+            pl.BlockSpec(vec_master.shape, lambda i: (0, 0)),
         ],
         out_specs=[pl.BlockSpec(memory_space=pl.ANY)] * 2,
         out_shape=[
-            jax.ShapeDtypeStruct((D, wide_master.shape[1]), bf16),
-            jax.ShapeDtypeStruct((FF, D), bf16),
+            jax.ShapeDtypeStruct((D, 3 * D), bf16),
+            jax.ShapeDtypeStruct((D, vec_master.shape[1]), bf16),
         ],
-        scratch_shapes=[
-            pltpu.VMEM((ALL_UNITS, UNIT, D), bf16),
-            pltpu.SemaphoreType.DMA((ALL_UNITS,)),
-            pltpu.SemaphoreType.DMA((ALL_UNITS,)),
-            pltpu.SemaphoreType.DMA((ALL_UNITS,)),
-        ],
+        scratch_shapes=[pltpu.VMEM((3, UNIT, D), bf16), pltpu.VMEM(vec_master.shape, bf16)]
+        + [pltpu.SemaphoreType.DMA((4,))] * 3,
         compiler_params=pltpu.CompilerParams(
             collective_id=3, has_side_effects=True, vmem_limit_bytes=40 << 20
         ),
-    )(wide_master, narrow_master)
+    )(wide_master, vec_master)
+
+
+def rest_scratch():
+    count = len(REST)
+    return [
+        pltpu.VMEM((count, UNIT, D), jnp.float32),
+        pltpu.VMEM((count, UNIT, D), jnp.bfloat16),
+        pltpu.SemaphoreType.DMA((count,)),
+    ] + [pltpu.SemaphoreType.DMA((count,))] * 3
+
+
+def gather_rest(pair, wide_ref, narrow_ref, wide_out, narrow_out, scratch):
+    raw, held, load_sem = scratch[:3]
+    sems = scratch[3:]
+    shard = lax.axis_index("shard")
+    loads, copies = [], []
+    for k, (kind, index) in enumerate(REST):
+        if kind == "wide":
+            source = wide_ref.at[:, pl.ds(index * D, D)]
+            target = wide_out.at[pl.ds(aligned(shard * UNIT), UNIT), pl.ds((index - 3) * D, D)]
+        else:
+            source = narrow_ref.at[pl.ds(index * UNIT, UNIT)]
+            target = narrow_out.at[pl.ds(aligned(shard * (FF // 2) + index * UNIT), UNIT)]
+        loads.append(pltpu.make_async_copy(source, raw.at[k], load_sem.at[k]))
+        copies.append(share(k, held.at[k], target, sems))
+
+    @pl.when(pair == 0)
+    def _():
+        meet_sibling()
+        for load in loads:
+            load.start()
+
+    for turn in range(1, 5):
+
+        @pl.when(pair == turn)
+        def _():
+            for k in range(4 * turn - 4, min(4 * turn, len(REST))):
+                loads[k].wait()
+                held[k] = raw[k].astype(jnp.bfloat16)
+                for copy in copies[k]:
+                    copy.start()
+
+    @pl.when(pair == D // 128 - 1)
+    def _():
+        for pairs in copies:
+            for copy in pairs:
+                copy.wait()
 
 
 def backward_kernel(causal, traffic, table, factor, *refs):
@@ -1014,7 +1071,7 @@
 ):
     rows, keys = queries.shape[0], keys_in.shape[0]
     bf16, f32 = jnp.bfloat16, jnp.float32
-    first = 0 if causal else 4
+    first = 0 if causal else 1
 
     def columns(count):
         return pl.BlockSpec((count, 128), lambda i: (0, i))
@@ -1048,7 +1105,7 @@
     ]
     if not causal:
         states, resid, mixed_self, vec_rows = extra
-        in_specs += [whole((keys, D)), pl.BlockSpec((D, D), lambda i: (0, 3), pipeline_mode=pl.Buffered(1)), whole((rows, D)), whole((rows, D))]
+        in_specs += [whole((keys, D)), pl.BlockSpec((D, D), lambda i: (0, 0), pipeline_mode=pl.Buffered(1)), whole((rows, D)), whole((rows, D))]
         in_specs += [whole(vec_rows.shape)]
         operands += [states, wide_full, resid, mixed_self, vec_rows]
         out_specs += [whole((keys, D)), whole((rows, D)), whole((D, D)), whole((8, D))]
@@ -1106,7 +1163,7 @@
             copy[at, :] = value.astype(jnp.bfloat16)
             return carry
 
-        lax.fori_loop(0, UNIT // 32, body, 0, unroll=3)
+        lax.fori_loop(0, UNIT // 64, body, 0, unroll=3)
 
     for which, begin, end, wide in spans:
 
@@ -1119,12 +1176,12 @@
 
 
 def adam_halves(parts, x, y, wide, narrow, before):
-    spans, starts, wides, narrow_rows, narrow_cols = [], [], [], [], []
+    spans, starts, wides, wide_halves, narrow_rows = [], [], [], [], []
     step = 0
     for which, (array, names, by_x, own) in enumerate(parts):
         starts.append(step)
         here = x if by_x else y
-        entire = array.shape[2] == D
+        entire = array.shape[1] == UNIT
         for k, (kind, index) in enumerate([n for n in names for _ in range(1 + entire)]):
             half = k % 2 if entire else here if own else 1 - here
             is_wide = kind == "wide"
@@ -1132,9 +1189,9 @@
                 spans[-1] = (which, spans[-1][1], step + 1, is_wide)
             else:
                 spans.append((which, step, step + 1, is_wide))
-            wides.append(2 * index + half if is_wide else None)
-            narrow_rows.append(None if is_wide else index)
-            narrow_cols.append(None if is_wide else half)
+            wides.append(index if is_wide else None)
+            wide_halves.append(half if is_wide else None)
+            narrow_rows.append(None if is_wide else 2 * index + half)
             step += 1
 
     def filled(values):
@@ -1145,19 +1202,19 @@
             found.append(jnp.asarray(last, jnp.int32))
         return jnp.stack(found)
 
-    table = jnp.stack([filled(wides), filled(narrow_rows), filled(narrow_cols)])
+    table = jnp.stack([filled(wides), filled(wide_halves), filled(narrow_rows)])
     f32, bf16 = jnp.float32, jnp.bfloat16
-    spec_w = pl.BlockSpec((UNIT, HALF), lambda i, t: (0, t[0, i]))
-    spec_n = pl.BlockSpec((UNIT, HALF), lambda i, t: (t[1, i], t[2, i]))
+    spec_w = pl.BlockSpec((UNIT // 2, D), lambda i, t: (t[1, i], t[0, i]))
+    spec_n = pl.BlockSpec((UNIT // 2, D), lambda i, t: (t[2, i], 0))
 
     def spec_sum(start, array):
-        halves = array.shape[2] // HALF
+        halves = 2 * array.shape[1] // UNIT
 
         def place(i, t):
             at = jnp.clip(i - start, 0, array.shape[0] * halves - 1)
-            return (at // halves, 0, at % halves)
-
-        return pl.BlockSpec((1, UNIT, HALF), place)
+            return (at // halves, at % halves, 0)
+
+        return pl.BlockSpec((1, UNIT // 2, D), place)
 
     def shapes(like):
         return [jax.ShapeDtypeStruct(like.shape, f32)] * 4 + [jax.ShapeDtypeStruct(like.shape, bf16)]
@@ -1235,23 +1292,27 @@
     def gathered(part):
         return lax.all_gather(part.astype(bf16), "shard", axis=0, tiled=True)
 
+    masters = None
     if shards == 2:
-        wide_full, narrow_full = gather_weights(wide_master, narrow_master)
+        masters = (wide_master, narrow_master)
+        wide_early, vec_full = gather_first(wide_master, vec_master)
     else:
-        wide_full, narrow_full = gathered(wide_master), gathered(narrow_master)
-    vector = gathered(vec_master).astype(f32)
+        wide_early, vec_full = gathered(wide_master[:, : 3 * D]), gathered(vec_master)
+        wide_late, narrow_full = gathered(wide_master[:, 3 * D :]), gathered(narrow_master)
+    vector = vec_full.astype(f32)
     vec_rows = jnp.pad(vector.T, ((0, 24 - vector.shape[1]), (0, 0)))
-    mixed_self, totals_self, queries, keys_self, values_self = attend_forward(
-        tokens, tokens, block_mask, wide_full, vec_rows, True
-    )
-    resid_one = tokens.astype(f32) + matmul(mixed_self, wide_full[:, 3 * D : 4 * D]) + vector[:, 2]
+    found = attend_forward(tokens, tokens, block_mask, wide_early, vec_rows, True, masters)
+    mixed_self, totals_self, queries, keys_self, values_self = found[:5]
+    if masters is not None:
+        wide_late, narrow_full = found[5:]
+    resid_one = tokens.astype(f32) + matmul(mixed_self, wide_late[:, :D]) + vector[:, 2]
     normed_one = norm_forward(resid_one, vector[:, 11], vector[:, 14])
     normed_low = normed_one.astype(bf16)
     mixed_cross, totals_cross, cross_queries, cross_keys, cross_values = attend_forward(
-        normed_low, encoder_states, block_mask, wide_full, vec_rows, False
+        normed_low, encoder_states, block_mask, wide_late, vec_rows, False, None
     )
     output, grad_two, grad_cross_mix, term_in, term_narrow, term_co, sums = center(
-        mixed_cross, normed_one, cotangent, wide_full, narrow_full, vec_rows, factor, shards
+        mixed_cross, normed_one, cotangent, wide_late, narrow_full, vec_rows, factor, shards
     )
 
     def split(term):
@@ -1291,7 +1352,7 @@
         traffic = Traffic(items, lanes, True, terms)
     found = attend_backward(
         cross_queries, cross_keys, cross_values, block_mask, False, mixed_cross, totals_cross,
-        grad_cross_mix, normed_low, grad_two, wide_full, factor,
+        grad_cross_mix, normed_low, grad_two, wide_late, factor,
         (encoder_states, resid_one, mixed_self, vec_rows), traffic, CROSS_TABLE, 1,
     )
     term_cq, term_ck, term_cv, cross_sums, grad_one, enc_grad, grad_self_mix, term_wo, norm_sums = found[:9]
@@ -1304,7 +1365,7 @@
         traffic = Traffic(items, lanes, True, middle[:N_MIDDLE], blocks[:N_GATHER])
     found = attend_backward(
         queries, keys_self, values_self, block_mask, True, mixed_self, totals_self,
-        grad_self_mix, tokens, grad_one, wide_full, factor, None, traffic, SELF_TABLE, 2,
+        grad_self_mix, tokens, grad_one, wide_early, factor, None, traffic, SELF_TABLE, 2,
     )
     late = [split(term) for term in found[:3]]
     self_sums, in_grad = found[3:5]

time: 477 us -> 463 us (0.971)
  Pallas kernels: 432 us -> 425 us
    unnamed x50 -> x29, local copies, waits for them, and re-layouts: 13.2 us -> 8.63 us
  transfers between devices with their start and end apart: 2 -> 2, of which waited for: 0 -> 0; matrix products, arithmetic and copies ran while one was open for 0% -> 1% of each run, Pallas kernels for 10% -> 9%
where the time goes in v5:
time: 463 us; the launch traced here: 457 us
  Pallas kernels  425 us (92%)
  local copies, waits for them, and re-layouts  16.1 us (3%)
  other arithmetic  8.04 us (2%)
    pallas_call x2, Pallas kernels, attend_backward(): pl.pallas_call(partial(backward_kernel, causal, traffic, table, factor),...  154 us
    pallas_call x1, Pallas kernels, run_traffic(): pl.pallas_call(partial(traffic_kernel, traffic, order), in_specs=traffic....  76.2 us
    pallas_call x2, Pallas kernels, attend_forward(): pl.pallas_call(partial(forward_kernel, causal, carry), grid=(D // 128,),...  67.9 us
    pallas_call x2, Pallas kernels, adam_halves(): pl.pallas_call(partial(adam_kernel, tuple(spans), 0 if before is None els...  66.4 us
    pallas_call x1, Pallas kernels, center(): pl.pallas_call(partial(center_kernel, factor), grid=(8,), in_specs=[whole...  55.9 us
  transfers between devices with their start and end apart: 2, of which 0 were waited for; matrix products, arithmetic and copies ran while one was open for 1% of the time, Pallas kernels for 9%

profile of v5, /device:TPU:0, one launch (start us, length us, event | category | flops | bytes accessed | tf_op | source)
XLA Modules:
  0.0 457.0 jit_solution(10474950940694706971)
XLA Ops:
  0.7 0.9 copy.44.vec_ref
  1.6 5.4 %shard_map.268 = (bf16[768,2304]{1,0:T(8,128)(2,1)S(1)}, bf16[768,17]{1,0:T(8,128)(2,1)S(1)}) custom-call(f32[384,9216]{1,0:T(8,128)} %refs_2_.5, f32[384,17]{1,0:T(8,128)S(1)} %copy.44.vec_ref), custom_call_target="tpu_custom_call" | custom-call | tf_op jit(solution)/shard_map/pallas_call | solution.py:822
  7.0 0.0 copy-start
  7.0 1.8 copy-done
  8.8 0.1 copy.45
  9.0 0.6 pad.4.refs_6_.vec_ref.refs_16_
  9.6 29.1 %shard_map.269 = (bf16[1024,768]{1,0:T(8,128)(2,1)}, f32[6,8,1024]{2,1,0:T(8,128)}, bf16[1024,768]{1,0:T(8,128)(2,1)}, bf16[1024,768]{1,0:T(8,128)(2,1)}, bf16[1...) custom-call(s32[1,4,4]{2,1,0:T(4,128)} %refs_0_.7, bf16[1024,768]{1,0:T(8,128)(2,1)} %refs_7_.5, ...), custom_call_target="tpu_custom_call" | custom-call | flops 6442450944 | bytes 3145728 | tf_op jit(solution)/shard_map/pallas_call | solution.py:223
  38.7 0.0 copy-done.2
  38.7 3.3 fusion.6
  42.0 0.0 copy-start.1
  42.0 0.5 multiply_reduce_fusion
  42.5 2.8 fusion.4
  45.3 0.0 copy-done.1
  45.3 38.8 %shard_map.270 = (bf16[1024,768]{1,0:T(8,128)(2,1)}, f32[6,8,1024]{2,1,0:T(8,128)}, bf16[1024,768]{1,0:T(8,128)(2,1)}, bf16[2048,768]{1,0:T(8,128)(2,1)}, bf16[2048,768]{1,0:T(8,128)(2,1)}) custom-call(s32[1,4,4]{2,1,0:T(4,128)} %refs_0_.7, bf16[1024,768]{1,0:T(8,128)(2,1)} %get-tuple-element.150.refs_1_.refs_7_, bf16[2048,768]{1,0:T(8,128)(2,1)} %refs_12_.1, ...), custom_call_target="tpu_custom_call" | custom-call | flops 25769803776 | bytes 3145728 | tf_op jit(solution)/shard_map/pallas_call | solution.py:223
  84.2 55.9 %shard_map.271 = (bf16[1024,768]{1,0:T(8,128)(2,1)}, f32[1024,768]{1,0:T(8,128)}, bf16[1024,768]{1,0:T(8,128)(2,1)}, bf16[2,1536,768]{2,1,0:T(8,128)(2,1)}, bf16...) custom-call(bf16[1024,768]{1,0:T(8,128)(2,1)} %get-tuple-element.84.mix_ref.refs_5_, ...), custom_call_target="tpu_custom_call" | custom-call | flops 32614907904 | bytes 31457280 | tf_op jit(solution)/shard_map/pallas_call | solution.py:394
  140.1 107.5 %shard_map.272 = (bf16[768,768]{1,0:T(8,128)(2,1)}, bf16[768,768]{1,0:T(8,128)(2,1)}, bf16[768,768]{1,0:T(8,128)(2,1)}, f32[8,768]{1,0:T(8,128)}, f32[1024,768]{...) custom-call(s32[1,4,4]{2,1,0:T(4,128)} %refs_0_.7, ...), custom_call_target="tpu_custom_call" | custom-call | flops 64424509440 | bytes 3145728 | tf_op jit(solution)/shard_map/pallas_call | solution.py:1122
  247.6 1.5 slice.49.refs_14_
  249.1 0.9 slice.50
  250.0 0.0 copy-done.8
  250.1 46.1 %shard_map.273 = (bf16[768,768]{1,0:T(8,128)(2,1)}, bf16[768,768]{1,0:T(8,128)(2,1)}, bf16[768,768]{1,0:T(8,128)(2,1)}, f32[8,768]{1,0:T(8,128)}, bf16[1024,768]...) custom-call(s32[1,4,4]{2,1,0:T(4,128)} %refs_0_.7, ...), custom_call_target="tpu_custom_call" | custom-call | flops 16106127360 | bytes 3145728 | tf_op jit(solution)/shard_map/pallas_call | solution.py:1122
  296.2 0.7 slice.51
  296.9 0.9 fusion.5
  297.8 0.7 slice.53
  298.6 0.3 concatenate.32
  298.9 0.6 multiply_bitcast_fusion.refs_9_
  299.5 1.6 pad_maximum_fusion.refs_8_
  301.1 76.2 %shard_map.274 = (bf16[6,192,768]{2,1,0:T(8,128)(2,1)}, bf16[6,192,768]{2,1,0:T(8,128)(2,1)}, f32[24,384]{1,0:T(8,128)}) custom-call(bf16[2,1536,768]{2,1,0:T(8,128)(2,1)} %get-tuple-element.96.refs_17_.refs_0_, bf16[2,1536,768]{2,1,0:T(8,128)(2,1)} %bitcast.39, bf16[2,384,768]{2,1,0:T(8,128)(2,1)} %bitcast.41, bf16[2,384,768]{2,1,0:T(8,128)(2,1)} %bitcast.42, ...), custom_call_target="tpu_custom_call" | custom-call | tf_op jit(solution)/shard_map/pallas_call | solution.py:763
  377.3 1.4 collective-permute-start
  378.8 1.3 collective-permute-start.1
  380.1 0.1 stack.42
  380.2 0.1 stack.47
  380.3 0.1 stack.57
  380.4 0.5 broadcast.38
  380.9 0.7 stack.52
  381.6 1.2 pad_add_fusion.1.table_ref
  382.9 0.0 copy-start.11
  382.9 42.0 %shard_map.275 = (f32[384,9216]{1,0:T(8,128)}, f32[384,9216]{1,0:T(8,128)}, f32[384,9216]{1,0:T(8,128)}, f32[384,9216]{1,0:T(8,128)}, bf16[384,9216]{1,0:T(8,128...) custom-call(s32[3,20]{1,0:T(4,128)} %pad_add_fusion.1.table_ref, ...), custom_call_target="tpu_custom_call" | custom-call | flops 88473600 | bytes 94371840 | tf_op jit(solution)/shard_map/pallas_call | solution.py:1230
  424.9 0.6 pad_add_fusion.table_ref
  425.5 0.0 copy-done.7
  425.5 0.7 fusion.2
  426.2 0.0 collective-permute-done.refs_0_
  426.2 0.0 collective-permute-done.1.refs_1_
  426.2 1.2 copy-done.4
  427.4 0.6 copy-done.5
  428.0 24.4 %shard_map.276 = (f32[384,9216]{1,0:T(8,128)}, f32[384,9216]{1,0:T(8,128)}, f32[384,9216]{1,0:T(8,128)}, f32[384,9216]{1,0:T(8,128)}, bf16[384,9216]{1,0:T(8,128...) custom-call(s32[3,12]{1,0:T(4,128)} %pad_add_fusion.table_ref, ...), custom_call_target="tpu_custom_call", output_to_operand_aliasing={{0}: (9, {}), {1}: (10, {}), {2}: (11, {}), {3}: (12, {}), ... | custom-call | flops 53084160 | bytes 56623104 | tf_op jit(solution)/shard_map/pallas_call | solution.py:1230
  452.4 1.1 copy.61
  453.6 1.3 copy-done.3
  454.9 1.7 copy.62
  (24 shorter events, 0.1 us)
Async XLA Ops:
  7.0 1.8 copy-start
  9.6 29.1 %copy-start.2 = (bf16[1024,768]{1,0:T(8,128)(2,1)S(1)}, bf16[1024,768]{1,0:T(8,128)(2,1)}, u32[]{:S(2)}) copy-start(bf16[1024,768]{1,0:T(8,128)(2,1)} %refs_7_.5) | copy-start | bytes 4718596
  42.0 3.3 copy-start.1
  140.1 110.0 %copy-start.8 = (f32[24,768]{1,0:T(8,128)S(1)}, f32[24,768]{1,0:T(8,128)}, u32[]{:S(2)}) copy-start(f32[24,768]{1,0:T(8,128)} %get-tuple-element.116) | copy-start | bytes 221188
  377.3 48.8 %collective-permute-start = (bf16[6,192,768]{2,1,0:T(8,128)(2,1)}, bf16[6,192,768]{2,1,0:T(8,128)(2,1)S(1)}, u32[]{:S(2)}, u32[]{:S(2)}) collective-permute-start(bf16[6,192,768]{2,1,0:T(8,128)(2,1)} %get-tuple-element.117.refs_2_), channel_id=1, source_target_pairs={{0,2},{2,0},{4,6},{6,4},{8,10},{10,8},{12,14},{14,12},{16,18},{18,... | collective-permute-start | bytes 5308424 | tf_op jit(solution)/shard_map/ppermute | solution.py:1345
  378.8 47.4 %collective-permute-start.1 = (bf16[6,192,768]{2,1,0:T(8,128)(2,1)}, bf16[6,192,768]{2,1,0:T(8,128)(2,1)S(1)}, u32[]{:S(2)}, u32[]{:S(2)}) collective-permute-start(bf16[6,192,768]{2,1,0:T(8,128)(2,1)} %get-tuple-element.118.refs_3_), channel_id=1, source_target_pairs={{0,4},{2,6},{4,0},{6,2},{8,12},{10,14},{12,8},{14,10},{16,20},{18,... | collective-permute-start | bytes 5308424 | tf_op jit(solution)/shard_map/ppermute | solution.py:1345
  382.9 42.0 %copy-start.12 = (s32[1,12]{1,0:T(1,128)S(1)}, s32[1,12]{1,0:T(1,128)}, u32[]{:S(2)}) copy-start(s32[1,12]{1,0:T(1,128)} %constant.57.clone.1) | copy-start | bytes 148
  382.9 42.6 %copy-start.7 = (f32[384,17]{0,1:T(8,128)S(1)}, f32[384,17]{0,1:T(8,128)}, u32[]{:S(2)}) copy-start(f32[384,17]{0,1:T(8,128)} %param.19) | copy-start | bytes 78340
  382.9 42.6 %copy-start.9 = (f32[384,17]{0,1:T(8,128)S(1)}, f32[384,17]{0,1:T(8,128)}, u32[]{:S(2)}) copy-start(f32[384,17]{0,1:T(8,128)} %param.22) | copy-start | bytes 78340
  382.9 42.6 %copy-start.10 = (f32[384,17]{0,1:T(8,128)S(1)}, f32[384,17]{0,1:T(8,128)}, u32[]{:S(2)}) copy-start(f32[384,17]{0,1:T(8,128)} %param.25) | copy-start | bytes 78340
  382.9 42.6 %copy-start.11 = (f32[24,384]{1,0:T(8,128)S(1)}, f32[24,384]{1,0:T(8,128)}, u32[]{:S(2)}) copy-start(f32[24,384]{1,0:T(8,128)} %get-tuple-element.133) | copy-start | bytes 110596
  426.2 1.2 copy-start.4
  426.2 1.8 copy-start.5
  428.0 24.4 %copy-start.6 = (bf16[1024,768]{1,0:T(8,128)(2,1)S(1)}, bf16[1024,768]{1,0:T(8,128)(2,1)}, u32[]{:S(2)}) copy-start(bf16[1024,768]{1,0:T(8,128)(2,1)} %get-tuple-element.178) | copy-start | bytes 4718596
  452.4 2.5 copy-start.3

commit v6 on v5

--- a/solution.py
+++ b/solution.py
@@ -27,7 +27,7 @@
 masked_score = -1e30
 FACTOR = HD ** (-0.5)
 SCALE2 = FACTOR / math.log(2.0)
-N_BOTH = 2
+N_BOTH = 3
 N_SCATTER = 6
 N_GATHER = 2
 N_MIDDLE = 2
@@ -35,14 +35,19 @@
 
 CROSS_TABLE = {
     (0, 0): ((0, 0), (1, 0), (2, 0), (3, 0)),
-    (0, 9): ((0, 1), (1, 1), (2, 1), (3, 1)),
-    (2, 0): ((0, 2), (1, 2), (2, 2), (3, 2)),
-    (2, 3): ((4, 0), (5, 0), (6, 0), (7, 0)),
-    (2, 9): ((0, 3), (1, 3), (2, 3), (3, 3), (4, 1), (5, 1), (6, 1), (7, 1)),
-    (4, 0): ((0, 4), (1, 4), (2, 4), (3, 4), (4, 2), (5, 2), (6, 2), (7, 2)),
-    (4, 9): ((0, 5), (1, 5), (4, 3), (5, 3), (6, 3), (7, 3)),
-    (5, 3): ((0, 6), (1, 6)),
-    (5, 9): ((4, 4), (5, 4), (6, 4), (7, 4), (0, 7), (1, 7), (0, 8), (1, 8)),
+    (0, 6): ((0, 1), (1, 1), (2, 1), (3, 1)),
+    (1, 6): ((0, 2), (1, 2), (2, 2), (3, 2)),
+    (1, 9): ((4, 0), (5, 0), (6, 0), (7, 0)),
+    (2, 3): ((0, 3), (1, 3), (2, 3), (3, 3), (4, 1), (5, 1), (6, 1), (7, 1)),
+    (3, 3): ((0, 4), (1, 4), (2, 4), (3, 4), (4, 2), (5, 2), (6, 2), (7, 2)),
+    (3, 6): ((8, 0),),
+    (3, 9): ((8, 1),),
+    (4, 0): ((0, 5), (1, 5), (2, 5), (4, 3), (5, 3), (6, 3), (7, 3)),
+    (4, 6): ((8, 2),),
+    (4, 9): ((0, 6), (1, 6), (2, 6)),
+    (5, 0): ((4, 4), (5, 4), (6, 4), (7, 4), (8, 3)),
+    (5, 6): ((1, 7), (8, 4)),
+    (5, 9): ((0, 7), (1, 8), (2, 7), (0, 8), (2, 8)),
 }
 
 
@@ -57,16 +62,15 @@
 
 
 TAIL_ORDER = (
-    (12, 0), (0, 0), (1, 0), (2, 0), (3, 0), (4, 0), (5, 0), (6, 0),
-    (7, 0), (6, 1), (12, 1), (7, 1), (6, 2), (7, 2), (8, 0), (9, 0),
-    (8, 1), (9, 1), (6, 3), (7, 3), (12, 2), (0, 1), (1, 1), (2, 1),
-    (3, 1), (4, 1), (5, 1), (6, 4), (7, 4), (8, 2), (12, 3), (9, 2),
-    (10, 0), (11, 0), (0, 2), (1, 2), (2, 2), (3, 2), (4, 2), (5, 2),
-    (12, 4), (6, 5), (7, 5), (10, 1), (11, 1), (0, 3), (1, 3), (2, 3),
-    (3, 3), (4, 3), (5, 3), (8, 3), (9, 3), (6, 6), (7, 6), (6, 7),
-    (7, 7), (8, 4), (9, 4), (10, 2), (11, 2), (10, 3), (11, 3), (8, 5),
-    (9, 5), (8, 6), (9, 6), (10, 4), (11, 4), (8, 7), (9, 7), (10, 5),
-    (11, 5), (10, 6), (11, 6), (10, 7), (11, 7),
+    (11, 0), (0, 0), (1, 0), (2, 0), (3, 0), (4, 0), (5, 0), (6, 0),
+    (7, 0), (6, 1), (11, 1), (7, 1), (6, 2), (7, 2), (8, 0), (9, 0),
+    (8, 1), (9, 1), (6, 3), (7, 3), (11, 2), (0, 1), (1, 1), (2, 1),
+    (3, 1), (4, 1), (5, 1), (6, 4), (7, 4), (8, 2), (11, 3), (9, 2),
+    (10, 0), (0, 2), (1, 2), (2, 2), (3, 2), (4, 2), (5, 2), (6, 5),
+    (11, 4), (7, 5), (10, 1), (0, 3), (1, 3), (2, 3), (3, 3), (4, 3),
+    (5, 3), (8, 3), (9, 3), (6, 6), (6, 7), (7, 6), (7, 7), (8, 4),
+    (9, 4), (10, 2), (10, 3), (8, 5), (9, 5), (10, 4), (8, 6), (9, 6),
+    (8, 7), (9, 7), (10, 5), (10, 6), (10, 7),
 )
 
 

time: 463 us -> 461 us (level)
  transfers between devices with their start and end apart: 2 -> 2, of which waited for: 0 -> 0; matrix products, arithmetic and copies ran while one was open for 1% -> 0% of each run, Pallas kernels for 9% -> 10%
where the time goes in v6:
time: 461 us; the launch traced here: 455 us
  Pallas kernels  426 us (92%)
  local copies, waits for them, and re-layouts  14.8 us (3%)
  other arithmetic  7.38 us (2%)
    pallas_call x2, Pallas kernels, attend_backward(): pl.pallas_call(partial(backward_kernel, causal, traffic, table, factor),...  156 us
    pallas_call x1, Pallas kernels, run_traffic(): pl.pallas_call(partial(traffic_kernel, traffic, order), in_specs=traffic....  71.9 us
    pallas_call x2, Pallas kernels, adam_halves(): pl.pallas_call(partial(adam_kernel, tuple(spans), 0 if before is None els...  68.4 us
    pallas_call x2, Pallas kernels, attend_forward(): pl.pallas_call(partial(forward_kernel, causal, carry), grid=(D // 128,),...  67.9 us
    pallas_call x1, Pallas kernels, center(): pl.pallas_call(partial(center_kernel, factor), grid=(8,), in_specs=[whole...  55.9 us
  transfers between devices with their start and end apart: 2, of which 0 were waited for; matrix products, arithmetic and copies ran while one was open for 0% of the time, Pallas kernels for 10%

profile of v6, /device:TPU:0, one launch (start us, length us, event | category | flops | bytes accessed | tf_op | source)
XLA Modules:
  0.0 454.8 jit_solution(11526814789433672308)
XLA Ops:
  0.7 0.9 copy.44.vec_ref
  1.6 5.4 %shard_map.268 = (bf16[768,2304]{1,0:T(8,128)(2,1)S(1)}, bf16[768,17]{1,0:T(8,128)(2,1)S(1)}) custom-call(f32[384,9216]{1,0:T(8,128)} %refs_2_.5, f32[384,17]{1,0:T(8,128)S(1)} %copy.44.vec_ref), custom_call_target="tpu_custom_call" | custom-call | tf_op jit(solution)/shard_map/pallas_call | solution.py:826
  7.0 0.0 copy-start
  7.0 1.8 copy-done
  8.8 0.1 copy.45
  9.0 0.6 pad.4.refs_6_.vec_ref.refs_16_
  9.6 29.1 %shard_map.269 = (bf16[1024,768]{1,0:T(8,128)(2,1)}, f32[6,8,1024]{2,1,0:T(8,128)}, bf16[1024,768]{1,0:T(8,128)(2,1)}, bf16[1024,768]{1,0:T(8,128)(2,1)}, bf16[1...) custom-call(s32[1,4,4]{2,1,0:T(4,128)} %refs_0_.7, bf16[1024,768]{1,0:T(8,128)(2,1)} %refs_7_.5, ...), custom_call_target="tpu_custom_call" | custom-call | flops 6442450944 | bytes 3145728 | tf_op jit(solution)/shard_map/pallas_call | solution.py:227
  38.7 0.0 copy-done.2
  38.7 3.3 fusion.6
  42.0 0.0 copy-start.1
  42.1 0.5 multiply_reduce_fusion
  42.6 2.8 fusion.4
  45.3 0.0 copy-done.1
  45.3 38.8 %shard_map.270 = (bf16[1024,768]{1,0:T(8,128)(2,1)}, f32[6,8,1024]{2,1,0:T(8,128)}, bf16[1024,768]{1,0:T(8,128)(2,1)}, bf16[2048,768]{1,0:T(8,128)(2,1)}, bf16[2048,768]{1,0:T(8,128)(2,1)}) custom-call(s32[1,4,4]{2,1,0:T(4,128)} %refs_0_.7, bf16[1024,768]{1,0:T(8,128)(2,1)} %get-tuple-element.150.refs_1_.refs_7_, bf16[2048,768]{1,0:T(8,128)(2,1)} %refs_12_.1, ...), custom_call_target="tpu_custom_call" | custom-call | flops 25769803776 | bytes 3145728 | tf_op jit(solution)/shard_map/pallas_call | solution.py:227
  84.1 55.9 %shard_map.271 = (bf16[1024,768]{1,0:T(8,128)(2,1)}, f32[1024,768]{1,0:T(8,128)}, bf16[1024,768]{1,0:T(8,128)(2,1)}, bf16[2,1536,768]{2,1,0:T(8,128)(2,1)}, bf16...) custom-call(bf16[1024,768]{1,0:T(8,128)(2,1)} %get-tuple-element.84.mix_ref.refs_5_, ...), custom_call_target="tpu_custom_call" | custom-call | flops 32614907904 | bytes 31457280 | tf_op jit(solution)/shard_map/pallas_call | solution.py:398
  140.1 110.3 %shard_map.272 = (bf16[768,768]{1,0:T(8,128)(2,1)}, bf16[768,768]{1,0:T(8,128)(2,1)}, bf16[768,768]{1,0:T(8,128)(2,1)}, f32[8,768]{1,0:T(8,128)}, f32[1024,768]{...) custom-call(s32[1,4,4]{2,1,0:T(4,128)} %refs_0_.7, ...), custom_call_target="tpu_custom_call" | custom-call | flops 64424509440 | bytes 3145728 | tf_op jit(solution)/shard_map/pallas_call | solution.py:1126
  250.4 1.5 slice.49.refs_14_
  251.9 0.9 slice.50
  252.9 0.0 copy-done.8
  252.9 45.8 %shard_map.273 = (bf16[768,768]{1,0:T(8,128)(2,1)}, bf16[768,768]{1,0:T(8,128)(2,1)}, bf16[768,768]{1,0:T(8,128)(2,1)}, f32[8,768]{1,0:T(8,128)}, bf16[1024,768]...) custom-call(s32[1,4,4]{2,1,0:T(4,128)} %refs_0_.7, ...), custom_call_target="tpu_custom_call" | custom-call | flops 16106127360 | bytes 3145728 | tf_op jit(solution)/shard_map/pallas_call | solution.py:1126
  298.7 0.7 slice.51
  299.5 0.9 fusion.5
  300.3 0.7 slice.53
  301.1 0.3 concatenate.32
  301.4 0.6 multiply_bitcast_fusion.refs_9_
  302.0 1.6 pad_maximum_fusion.refs_8_
  303.6 71.9 %shard_map.274 = (bf16[5,192,768]{2,1,0:T(8,128)(2,1)}, bf16[6,192,768]{2,1,0:T(8,128)(2,1)}, f32[24,384]{1,0:T(8,128)}) custom-call(bf16[2,1536,768]{2,1,0:T(8,128)(2,1)} %get-tuple-element.96.refs_17_.refs_0_, bf16[2,1536,768]{2,1,0:T(8,128)(2,1)} %bitcast.39, bf16[2,384,768]{2,1,0:T(8,128)(2,1)} %bitcast.41, bf16[2,384,768]{2,1,0:T(8,128)(2,1)} %bitcast.42, ...), custom_call_target="tpu_custom_call" | custom-call | tf_op jit(solution)/shard_map/pallas_call | solution.py:767
  375.5 1.1 collective-permute-start.1
  376.6 1.3 collective-permute-start
  377.9 0.1 stack.42
  378.0 0.1 stack.47
  378.1 0.1 stack.52
  378.2 0.1 stack.110
  378.3 0.6 pad_add_fusion.1.table_ref
  378.9 0.0 copy-start.11
  378.9 44.6 %shard_map.275 = (f32[384,9216]{1,0:T(8,128)}, f32[384,9216]{1,0:T(8,128)}, f32[384,9216]{1,0:T(8,128)}, f32[384,9216]{1,0:T(8,128)}, bf16[384,9216]{1,0:T(8,128...) custom-call(s32[3,21]{1,0:T(4,128)} %pad_add_fusion.1.table_ref, ...), custom_call_target="tpu_custom_call" | custom-call | flops 92897280 | bytes 99090432 | tf_op jit(solution)/shard_map/pallas_call | solution.py:1234
  423.5 0.6 pad_add_fusion.table_ref
  424.1 0.0 copy-done.9
  424.1 0.7 fusion.2
  424.8 0.0 collective-permute-done.refs_0_
  424.8 0.0 collective-permute-done.1.refs_1_
  424.8 0.0 copy-start.4
  424.8 1.1 copy-done.6
  425.9 0.6 copy-done.4
  426.5 23.8 %shard_map.276 = (f32[384,9216]{1,0:T(8,128)}, f32[384,9216]{1,0:T(8,128)}, f32[384,9216]{1,0:T(8,128)}, f32[384,9216]{1,0:T(8,128)}, bf16[384,9216]{1,0:T(8,128...) custom-call(s32[3,11]{1,0:T(4,128)} %pad_add_fusion.table_ref, ...), custom_call_target="tpu_custom_call", output_to_operand_aliasing={{0}: (9, {}), {1}: (10, {}), {2}: (11, {}), {3}: (12, {}), ... | custom-call | flops 48660480 | bytes 51904512 | tf_op jit(solution)/shard_map/pallas_call | solution.py:1234
  450.3 1.1 copy.61
  451.4 1.3 copy-done.3
  452.7 1.7 copy.62
  (27 shorter events, 0.1 us)
Async XLA Ops:
  7.0 1.8 copy-start
  9.6 29.1 %copy-start.2 = (bf16[1024,768]{1,0:T(8,128)(2,1)S(1)}, bf16[1024,768]{1,0:T(8,128)(2,1)}, u32[]{:S(2)}) copy-start(bf16[1024,768]{1,0:T(8,128)(2,1)} %refs_7_.5) | copy-start | bytes 4718596
  42.0 3.3 copy-start.1
  140.1 112.8 %copy-start.8 = (f32[24,768]{1,0:T(8,128)S(1)}, f32[24,768]{1,0:T(8,128)}, u32[]{:S(2)}) copy-start(f32[24,768]{1,0:T(8,128)} %get-tuple-element.116) | copy-start | bytes 221188
  303.6 74.7 %copy-start.13 = (s32[1,21]{1,0:T(1,128)S(1)}, s32[1,21]{1,0:T(1,128)}, u32[]{:S(2)}) copy-start(s32[1,21]{1,0:T(1,128)} %constant.69.clone.1) | copy-start | bytes 256
  375.5 49.3 %collective-permute-start.1 = (bf16[6,192,768]{2,1,0:T(8,128)(2,1)}, bf16[6,192,768]{2,1,0:T(8,128)(2,1)S(1)}, u32[]{:S(2)}, u32[]{:S(2)}) collective-permute-start(bf16[6,192,768]{2,1,0:T(8,128)(2,1)} %get-tuple-element.118.refs_3_), channel_id=1, source_target_pairs={{0,4},{2,6},{4,0},{6,2},{8,12},{10,14},{12,8},{14,10},{16,20},{18,... | collective-permute-start | bytes 5308424 | tf_op jit(solution)/shard_map/ppermute | solution.py:1349
  376.6 48.1 %collective-permute-start = (bf16[5,192,768]{2,1,0:T(8,128)(2,1)}, bf16[5,192,768]{2,1,0:T(8,128)(2,1)S(1)}, u32[]{:S(2)}, u32[]{:S(2)}) collective-permute-start(bf16[5,192,768]{2,1,0:T(8,128)(2,1)} %get-tuple-element.117.refs_2_), channel_id=1, source_target_pairs={{0,2},{2,0},{4,6},{6,4},{8,10},{10,8},{12,14},{14,12},{16,18},{18,... | collective-permute-start | bytes 4423688 | tf_op jit(solution)/shard_map/ppermute | solution.py:1349
  378.9 44.6 %copy-start.12 = (s32[1,11]{1,0:T(1,128)S(1)}, s32[1,11]{1,0:T(1,128)}, u32[]{:S(2)}) copy-start(s32[1,11]{1,0:T(1,128)} %constant.58.clone.1) | copy-start | bytes 136
  378.9 45.2 %copy-start.7 = (f32[384,17]{0,1:T(8,128)S(1)}, f32[384,17]{0,1:T(8,128)}, u32[]{:S(2)}) copy-start(f32[384,17]{0,1:T(8,128)} %param.19) | copy-start | bytes 78340
  378.9 45.2 %copy-start.9 = (f32[384,17]{0,1:T(8,128)S(1)}, f32[384,17]{0,1:T(8,128)}, u32[]{:S(2)}) copy-start(f32[384,17]{0,1:T(8,128)} %param.22) | copy-start | bytes 78340
  378.9 45.2 %copy-start.10 = (f32[384,17]{0,1:T(8,128)S(1)}, f32[384,17]{0,1:T(8,128)}, u32[]{:S(2)}) copy-start(f32[384,17]{0,1:T(8,128)} %param.25) | copy-start | bytes 78340
  378.9 45.2 %copy-start.11 = (f32[24,384]{1,0:T(8,128)S(1)}, f32[24,384]{1,0:T(8,128)}, u32[]{:S(2)}) copy-start(f32[24,384]{1,0:T(8,128)} %get-tuple-element.133) | copy-start | bytes 110596
  424.8 1.1 copy-start.6
  424.8 1.7 copy-start.4
  426.5 23.8 %copy-start.5 = (bf16[1024,768]{1,0:T(8,128)(2,1)S(1)}, bf16[1024,768]{1,0:T(8,128)(2,1)}, u32[]{:S(2)}) copy-start(bf16[1024,768]{1,0:T(8,128)(2,1)} %get-tuple-element.178) | copy-start | bytes 4718596
  450.3 2.5 copy-start.3
